TPU v7x, 32 devices: a whole 2x2x4 slice. The times are simulated.
32 devices in a mesh: sub: 8 (over z, x), vec: 4 (over y, core).
Axes of the slice: x: 2, y: 2, z: 4, core: 2. Of those that a mesh axis runs over, the one named last changes fastest.
Arguments:
- coefficients: bfloat16 [1024, 5120], P('sub', 'vec'), may hold values from -6 to 6
- row_counts: int32 [8], replicated, may hold values from 1 to 1024, 4096 in all
- ancestors: int32 [8, 3], replicated, may hold values from 0 to 6, as said below
- interior_modes: bfloat16 [32768, 1024], P('sub'), may hold values from -0.25 to 0.25
- separator_modes: bfloat16 [2048, 128], replicated, may hold values from -0.5 to 0.5
- coupling: bfloat16 [32768, 768], P('sub'), may hold values from -0.3125 to 0.3125
- pattern: int32 [8, 16, 3], P('sub'), may hold values 0 or 1
Outputs:
- interior_field: bfloat16 [32768, 1024], P('sub', 'vec')
- separator_field: bfloat16 [2048, 1024], P('sub', 'vec')
Inputs may be any that keep to these rules, and one draw needn't show every extreme that they name: `ancestors`: the separators form binary trees: substructures pair under level-1 separators, pairs of those under level-2 separators, and so on, so that a level-l separator lies over 2**l substructures; no separator appears at two levels. `row_counts`: the counts sum to 512 * 8.
All inputs are finite; a program needn't handle non-finite values. No bound on the sum of `pattern` on one device may be relied on, other than what follows from the above.
Results may differ from a plain program's by a relative error of at most 0.0038.
Values may be sent and summed in bfloat16 or wider, within the bound.
No kernel may reach another device: no remote copies, remote signals or barrier semaphores. Data moves between devices by JAX's collectives and lax.ppermute only.
A program may use at most 128 MiB of HBM per device.

v0:
```python
import jax
import jax.numpy as jnp
from jax import lax
from jax.sharding import PartitionSpec as P

BW = 256
SEPM = 128
LEVELS = 3


def window_rows(full_rows, row_counts, interior_total, cap_rows):
    slice_cols = full_rows.shape[0]
    block_total = interior_total // cap_rows + 1
    padded = jnp.concatenate(
        [full_rows[:, :interior_total], jnp.zeros((slice_cols, cap_rows), full_rows.dtype)], axis=1
    )
    blocks = padded.reshape(slice_cols, block_total, cap_rows)
    offsets = jnp.cumsum(row_counts) - row_counts
    first_block = offsets // cap_rows
    remainder = offsets - first_block * cap_rows
    labels = jnp.arange(block_total, dtype=jnp.int32)
    pick_first = (first_block[:, None] == labels[None, :]).astype(blocks.dtype)
    pick_second = (first_block[:, None] + 1 == labels[None, :]).astype(blocks.dtype)
    lower = jnp.einsum("ob,cbj->ocj", pick_first, blocks, preferred_element_type=jnp.float32)
    upper = jnp.einsum("ob,cbj->ocj", pick_second, blocks, preferred_element_type=jnp.float32)
    window = jnp.concatenate([lower, upper], axis=2).astype(blocks.dtype)
    for bit in range(cap_rows.bit_length() - 1):
        amount = 1 << bit
        moved = jnp.concatenate(
            [window[:, :, amount:], jnp.zeros(window.shape[:2] + (amount,), window.dtype)], axis=2
        )
        flag = remainder >> bit & 1 == 1
        window = jnp.where(flag[:, None, None], moved, window)
    window = window[:, :, :cap_rows]
    positions = jnp.arange(cap_rows, dtype=jnp.int32)
    live = positions[None, :] < row_counts[:, None]
    window = jnp.where(live[:, None, :], window, jnp.zeros((), window.dtype))
    return jnp.transpose(window, (1, 0, 2))


def body(coefficients, row_counts, ancestors, interior_modes, separator_modes, coupling, pattern):
    sub_count = lax.axis_size("sub")
    vec_count = lax.axis_size("vec")
    my_index = lax.axis_index("sub")
    slice_cols = coefficients.shape[0] // vec_count
    rows_vec = coefficients.shape[1]
    regrouped = coefficients.reshape(vec_count, slice_cols, rows_vec)
    full_rows = lax.all_to_all(regrouped, "vec", split_axis=0, concat_axis=2, tiled=True)
    full_rows = full_rows.reshape(slice_cols, vec_count * rows_vec)
    total_rows = full_rows.shape[1]
    interior_total = total_rows - sub_count * SEPM
    cap_rows = interior_modes.shape[1]
    interior_part = window_rows(full_rows, row_counts, interior_total, cap_rows)
    sep_part = full_rows[:, interior_total:].reshape(slice_cols, sub_count, SEPM)
    parts = [interior_part, sep_part]
    owners = jnp.arange(sub_count, dtype=jnp.int32)
    select_all = (ancestors[:, :, None] == owners[None, None, :]).astype(sep_part.dtype)
    above = jnp.einsum(
        "ols,csm->colm", select_all, sep_part, preferred_element_type=jnp.float32
    ).astype(sep_part.dtype)
    parts.append(above.reshape(slice_cols, sub_count, LEVELS * SEPM))
    picked = jnp.concatenate(parts, axis=2)
    slot_width = picked.shape[2]
    received = lax.all_to_all(picked, "sub", split_axis=1, concat_axis=0, tiled=True)
    group_cols = sub_count * slice_cols
    received = received.reshape(group_cols, slot_width)
    interior_coef = received[:, :cap_rows]
    own_coef = received[:, cap_rows : cap_rows + SEPM]
    modes_by_sep = separator_modes.reshape(sub_count, BW, SEPM)
    own_modes = lax.dynamic_index_in_dim(modes_by_sep, my_index, 0, keepdims=False)
    contract = (((1,), (1,)), ((), ()))
    own_field = lax.dot_general(
        own_modes, own_coef, contract, preferred_element_type=jnp.float32
    ).astype(jnp.bfloat16)
    interior_sum = lax.dot_general(
        interior_modes, interior_coef, contract, preferred_element_type=jnp.float32
    )
    my_ancestors = lax.dynamic_index_in_dim(ancestors, my_index, 0, keepdims=False)
    sep_labels = jnp.arange(sub_count, dtype=jnp.int32)
    select_mine = (my_ancestors[:, None] == sep_labels[None, :]).astype(modes_by_sep.dtype)
    ancestor_modes = jnp.einsum(
        "ls,sbm->lbm", select_mine, modes_by_sep, preferred_element_type=jnp.float32
    ).astype(modes_by_sep.dtype)
    ancestor_coef = received[:, cap_rows + SEPM :].reshape(group_cols, LEVELS, SEPM)
    ancestor_blocks = jnp.einsum(
        "lbm,klm->lbk", ancestor_modes, ancestor_coef, preferred_element_type=jnp.float32
    ).astype(jnp.bfloat16)
    block_count = coupling.shape[0] // BW
    gates = pattern[0].astype(coupling.dtype)
    masked = (coupling.reshape(block_count, BW, LEVELS, BW) * gates[:, None, :, None]).reshape(
        coupling.shape
    )
    interior_sum = interior_sum + jnp.dot(
        masked, ancestor_blocks.reshape(LEVELS * BW, group_cols), preferred_element_type=jnp.float32
    )
    return (interior_sum.astype(jnp.bfloat16), own_field)


def solution(mesh):
    placed = (P("sub", "vec"), P(), P(), P("sub", None), P(), P("sub", None), P("sub", None, None))
    return jax.shard_map(
        body,
        mesh=mesh,
        in_specs=placed,
        out_specs=(P("sub", "vec"), P("sub", "vec")),
        check_vma=False,
    )
```

profile of v0, /device:TPU:0, one launch (start us, length us, event | category | flops | bytes accessed | tf_op | source)
XLA Modules:
  0.0 68.0 jit_solution(640351005595886947)
XLA Ops:
  0.7 4.4 %all-to-all-start = ((bf16[4,32,1280]{2,1,0:T(8,128)(2,1)}), bf16[4,32,1280]{2,1,0:T(8,128)(2,1)S(1)}, u32[]{:S(2)}, u32[]{:S(2)}) async-start(bf16[4,32,1280]{2,1,0:T(8,128)(2,1)} %bitcast.86), calls=%async_computation | async-start | bytes 655360 | tf_op jit(solution)/shard_map/all_to_all | solution.py:48
  5.0 0.8 %reduce-window.9 = s32[8,1]{0,1:T(1,128)S(1)} reduce-window(s32[8,1]{0,1:T(1,128)} %bitcast.88, s32[]{:T(128)} %constant.18.clone.1), window={size=8x1 pad=7_0x0_0}, to_apply=%region_0.0 | reduce-window | flops 56 | bytes 68 | tf_op jit(solution)/shard_map/reduce-window.4
  5.9 0.7 and_compare_fusion.9
  6.6 0.7 %iota_compare_fusion = pred[8,1024]{1,0:T(8,128)(4,1)S(1)} fusion(s32[8]{0:T(128)} %param.8), kind=kLoop, calls=%fused_computation.40 | loop fusion | flops 8192 | bytes 8224 | tf_op jit(solution)/shard_map/lt | solution.py:36
  7.3 4.5 %all-to-all-done = bf16[4,32,1280]{2,1,0:T(8,128)(2,1)S(1)} async-done(((bf16[4,32,1280]{2,1,0:T(8,128)(2,1)}), bf16[4,32,1280]{2,1,0:T(8,128)(2,1)S(1)}, u32[]{:S(2)}, u32[]{:S(2)}) %all-to-all-start) | async-done | bytes 327712 | tf_op jit(solution)/shard_map/all_to_all | solution.py:48
  12.3 0.9 %fusion.8 = bf16[32,8,3,128]{3,1,0,2:T(8,128)(2,1)S(1)} fusion(bf16[32,8,128,1]{2,1,0,3:T(8,128)(2,1)S(1)} %bitcast.83, s32[8,3]{0,1:T(4,128)} %param.9), kind=kOutput, calls=%fused_computation.13 | convolution fusion | flops 1671360 | bytes 262240 | tf_op jit(solution)/shard_map/ols,csm->colm/dot_general | solution.py:58
  13.3 1.1 %convolution_convert_fusion.1 = bf16[8,32,1024]{2,0,1:T(8,128)(2,1)S(1)} fusion(bf16[32,5,1024]{2,1,0:T(8,128)(2,1)S(1)} %reshape.109, pred[5,1024]{1,0:T(8,128)(4,1)} %constant.37.clone.1, s32[8]{0:T(128)S(1)} %get-tuple-element.12), kind=kOutput, calls=%fused_computation.6 | convolution fusion | flops 3047464 | bytes 857120 | tf_op jit(solution)/shard_map/ob,cbj->ocj/dot_general | solution.py:24
  14.7 0.5 fusion.9
  15.2 0.5 fusion.10
  15.7 0.4 slice.64
  16.1 0.5 pad_select_fusion.7
  17.1 0.5 pad_select_fusion.6
  17.6 0.4 slice.66
  18.0 0.5 pad_select_fusion.5
  19.0 0.5 pad_select_fusion.4
  19.9 0.5 pad_select_fusion.3
  20.8 0.5 pad_select_fusion.2
  21.4 0.5 pad_select_fusion.1
  22.0 0.4 pad_select_fusion
  22.8 1.1 %copy.36 = bf16[32,8,1536]{2,0,1:T(8,128)(2,1)} copy(bf16[32,8,1536]{2,1,0:T(8,128)(2,1)S(1)} %pad_maximum_fusion.1) | data formatting | bytes 1572864 | tf_op jit(solution)/shard_map/concatenate | solution.py:62
  23.9 6.4 %all-to-all-start.1 = ((bf16[32,8,1536]{2,0,1:T(8,128)(2,1)}), bf16[32,8,1536]{2,0,1:T(8,128)(2,1)S(1)}, u32[]{:S(2)}, u32[]{:S(2)}) async-start(bf16[32,8,1536]{2,0,1:T(8,128)(2,1)} %copy.36), calls=%async_computation.1 | async-start | bytes 1572864 | tf_op jit(solution)/shard_map/all_to_all | solution.py:64
  30.6 0.5 mul.15
  31.1 6.9 %copy.51 = bf16[96,8,16,256]{3,1,2,0:T(8,128)(2,1)} copy(bf16[96,8,16,256]{3,2,1,0:T(8,128)(2,1)S(1)} %bitcast.74) | data formatting | bytes 12582912
  37.9 8.7 %copy.37 = bf16[4096,768]{0,1:T(8,128)(2,1)} copy(bf16[4096,768]{1,0:T(8,128)(2,1)} %param.12) | data formatting | bytes 12582912 | tf_op args[5]
  46.7 1.1 %convolution_convert_fusion.3 = bf16[3,256,128]{2,0,1:T(4,128)(2,1)} fusion(bf16[8,256,128]{2,1,0:T(8,128)(2,1)S(1)} %bitcast.69, s32[3]{0:T(128)S(1)} %dynamic-slice_reduce_fusion), kind=kOutput, calls=%fused_computation.8 | convolution fusion | flops 1671192 | bytes 720908 | tf_op jit(solution)/shard_map/ls,sbm->lbm/dot_general | solution.py:81
  47.8 2.6 %all-to-all-done.1 = bf16[32,8,1536]{2,0,1:T(8,128)(2,1)S(1)} async-done(((bf16[32,8,1536]{2,0,1:T(8,128)(2,1)}), bf16[32,8,1536]{2,0,1:T(8,128)(2,1)S(1)}, u32[]{:S(2)}, u32[]{:S(2)}) %all-to-all-start.1) | async-done | bytes 786464 | tf_op jit(solution)/shard_map/all_to_all | solution.py:64
  50.4 0.8 %convolution_convert_fusion.5 = bf16[256,256]{1,0:T(8,128)(2,1)} fusion(bf16[256,1536]{1,0:T(8,128)(2,1)S(1)} %bitcast.77, bf16[8,256,128]{2,1,0:T(8,128)(2,1)S(1)} %bitcast.70, s32[]{:T(128)S(6)} %select_n.58), kind=kOutput, calls=%fused_computation.14 | convolution fusion | flops 16842752 | bytes 262148 | tf_op jit(solution)/shard_map/dot_general | solution.py:72
  51.3 0.7 %slice.76 = bf16[256,384]{1,0:T(8,128)(2,1)} slice(bf16[256,1536]{1,0:T(8,128)(2,1)S(1)} %bitcast.78), slice={[0:256], [1152:1536]} | slice | bytes 393216 | tf_op jit(solution)/shard_map/slice | solution.py:84
  52.0 1.9 %copy.39 = bf16[256,384]{0,1:T(8,128)(2,1)} copy(bf16[256,384]{1,0:T(8,128)(2,1)} %slice.76) | data formatting | bytes 393216 | tf_op jit(solution)/shard_map/slice | solution.py:84
  53.9 5.9 %convolution_bitcast_fusion = f32[4096,256]{0,1:T(8,128)S(1)} fusion(bf16[4096,1024]{1,0:T(8,128)(2,1)} %param.10, bf16[256,1536]{1,0:T(8,128)(2,1)S(1)} %bitcast.79), kind=kOutput, calls=%fused_computation.2 | convolution fusion | flops 2147483648 | bytes 13107200 | tf_op jit(solution)/shard_map/dot_general | solution.py:75
  60.5 3.4 %fusion.5 = bf16[4096,256]{0,1:T(8,128)(2,1)} fusion(f32[4096,256]{0,1:T(8,128)S(1)} %convolution_bitcast_fusion, bf16[768,256]{1,0:T(8,128)(2,1)S(1)} %bitcast.76, bf16[4096,768]{0,1:T(8,128)(2,1)S(1)} %copy-done.1, bf16[4096,768]{0,1:T(8,128)(2,1)S(1)} %bitcast.73), kind=kOutput, calls=%fused_computation.4 | convolution fusion | flops 1615855616 | bytes 19267584 | tf_op jit(solution)/shard_map/dot_general | solution.py:93
  63.9 4.1 %copy.43 = bf16[4096,256]{1,0:T(8,128)(2,1)} copy(bf16[4096,256]{0,1:T(8,128)(2,1)} %fusion.5) | data formatting | bytes 4194304
  (41 shorter events, 3.9 us)
Async XLA Ops:
  0.6 46.0 %copy-start = (bf16[2048,128]{1,0:T(8,128)(2,1)S(1)}, bf16[2048,128]{1,0:T(8,128)(2,1)}, u32[]{:S(2)}) copy-start(bf16[2048,128]{1,0:T(8,128)(2,1)} %param.11) | copy-start | bytes 1572868
  0.6 13.7 %copy-start.4 = (pred[5,1024]{1,0:T(8,128)(4,1)S(1)}, pred[5,1024]{1,0:T(8,128)(4,1)}, u32[]{:S(2)}) copy-start(pred[5,1024]{1,0:T(8,128)(4,1)} %constant.37.clone.1) | copy-start | bytes 15364
  0.7 11.1 %all-to-all-start = ((bf16[4,32,1280]{2,1,0:T(8,128)(2,1)}), bf16[4,32,1280]{2,1,0:T(8,128)(2,1)S(1)}, u32[]{:S(2)}, u32[]{:S(2)}) async-start(bf16[4,32,1280]{2,1,0:T(8,128)(2,1)} %bitcast.86), calls=%async_computation | async-start | bytes 655360 | tf_op jit(solution)/shard_map/all_to_all | solution.py:48
  22.4 8.0 %copy-start.5 = (s32[8,3]{0,1:T(4,128)S(1)}, s32[8,3]{0,1:T(4,128)}, u32[]{:S(2)}) copy-start(s32[8,3]{0,1:T(4,128)} %param.9) | copy-start | bytes 292
  22.4 8.1 %copy-start.6 = (s32[1,16,3]{1,0,2:T(1,128)S(1)}, s32[1,16,3]{1,0,2:T(1,128)}, u32[]{:S(2)}) copy-start(s32[1,16,3]{1,0,2:T(1,128)} %param.13) | copy-start | bytes 580
  23.9 26.5 %all-to-all-start.1 = ((bf16[32,8,1536]{2,0,1:T(8,128)(2,1)}), bf16[32,8,1536]{2,0,1:T(8,128)(2,1)S(1)}, u32[]{:S(2)}, u32[]{:S(2)}) async-start(bf16[32,8,1536]{2,0,1:T(8,128)(2,1)} %copy.36), calls=%async_computation.1 | async-start | bytes 1572864 | tf_op jit(solution)/shard_map/all_to_all | solution.py:64
  52.0 8.1 %slice-start = ((s8[6291456]{0:T(1024)(128)(4,1)}), s8[2097152]{0:T(1024)(128)(4,1)S(1)}, s32[]{:S(2)}) async-start(s8[6291456]{0:T(1024)(128)(4,1)} %bitcast.71), calls=%async_computation.2 | async-start | bytes 4194304
  53.9 5.9 %copy-start.2 = (bf16[3,256,128]{2,0,1:T(4,128)(2,1)S(1)}, bf16[3,256,128]{2,0,1:T(4,128)(2,1)}, u32[]{:S(2)}) copy-start(bf16[3,256,128]{2,0,1:T(4,128)(2,1)} %convolution_convert_fusion.3) | copy-start | bytes 589828
  53.9 5.9 %copy-start.3 = (bf16[256,384]{0,1:T(8,128)(2,1)S(1)}, bf16[256,384]{0,1:T(8,128)(2,1)}, u32[]{:S(2)}) copy-start(bf16[256,384]{0,1:T(8,128)(2,1)} %copy.39) | copy-start | bytes 589828
  53.9 6.2 %slice-start.1 = ((s8[6291456]{0:T(1024)(128)(4,1)}), s8[4194304]{0:T(1024)(128)(4,1)S(1)}, s32[]{:S(2)}) async-start(s8[6291456]{0:T(1024)(128)(4,1)} %bitcast.71), calls=%async_computation.3 | async-start | bytes 8388608
  53.9 6.6 %copy-start.1 = (bf16[4096,768]{0,1:T(8,128)(2,1)S(1)}, bf16[4096,768]{0,1:T(8,128)(2,1)}, u32[]{:S(2)}) copy-start(bf16[4096,768]{0,1:T(8,128)(2,1)} %copy.37) | copy-start | bytes 18874372
where the time goes:
time: 68.6 us; the launch traced here: 68 us
  local copies, waits for them, and re-layouts  27.7 us (40%)
  matrix products  13.9 us (20%)
  starting transfers between devices  10.8 us (16%)
  other arithmetic  7.48 us (11%)
  waiting for transfers between devices  7.09 us (10%)
  between operations  0.99 us (1%)
    unnamed x25, local copies, waits for them, and re-layouts  20.1 us
    all_to_all x1, starting transfers between devices, body(): lax.all_to_all(picked, 'sub', split_axis=1, concat_axis=0, tiled=True)  6.44 us
    dot_general x1, matrix products, body(): lax.dot_general(interior_modes, interior_coef, contract, preferred_elemen...  5.91 us
    all_to_all x1, waiting for transfers between devices, body(): lax.all_to_all(regrouped, 'vec', split_axis=0, concat_axis=2, tiled=True)  4.48 us
    select_n x9, other arithmetic, window_rows(): window = jnp.where(flag[:, None, None], moved, window)  4.44 us
    all_to_all x1, starting transfers between devices, body(): lax.all_to_all(regrouped, 'vec', split_axis=0, concat_axis=2, tiled=True)  4.38 us
    dot_general x1, matrix products, body(): jnp.dot(masked, ancestor_blocks.reshape(LEVELS * BW, group_cols), preferr...  3.44 us
    slice x9, local copies, waits for them, and re-layouts, window_rows(): window[:, :, amount:]  2.69 us
  transfers between devices with their start and end apart: 2, of which 2 were waited for; matrix products, arithmetic and copies ran while one was open for 29% of the time, Pallas kernels for 0%

commit v1 on v0

v1 whole, which is shorter than its diff:
```python
import functools

import jax
import jax.numpy as jnp
from jax import lax
from jax.experimental import pallas as pl
from jax.experimental.pallas import tpu as pltpu
from jax.sharding import PartitionSpec as P

BW = 256
SEPM = 128
LEVELS = 3
LANES = 128
ROWS = 16
CONTRACT = (((1,), (1,)), ((), ()))


def partner_pairs(count, turn):
    return [(i, i ^ turn) for i in range(count)]


def exchange(blocks, axis):
    count = len(blocks)
    sent = [lax.ppermute(blocks[k], axis, partner_pairs(count, k)) for k in range(1, count)]
    return [blocks[0]] + sent


def split_kernel(coef_ref, *refs):
    count = len(refs) - 1
    sems = refs[count]
    slice_cols = refs[0].shape[0]
    me = lax.axis_index("vec")
    copies = []
    for k in list(range(1, count)) + [0]:
        at = pl.multiple_of(jnp.bitwise_xor(me, k) * slice_cols, slice_cols)
        copy = pltpu.make_async_copy(coef_ref.at[pl.ds(at, slice_cols)], refs[k], sems.at[k])
        copy.start()
        copies.append(copy)
    for copy in copies:
        copy.wait()


def split(coefficients, count):
    shape = (coefficients.shape[0] // count, coefficients.shape[1])
    return pl.pallas_call(
        split_kernel,
        out_shape=[jax.ShapeDtypeStruct(shape, coefficients.dtype)] * count,
        in_specs=[pl.BlockSpec(memory_space=pl.ANY)],
        out_specs=[pl.BlockSpec(memory_space=pltpu.VMEM)] * count,
        scratch_shapes=[pltpu.SemaphoreType.DMA((count,))],
        compiler_params=pltpu.CompilerParams(vmem_limit_bytes=4 << 20),
        name="split_slices",
    )(coefficients)


def pack_kernel(interior_total, cap, sub_count, vec_count, direct, counts_ref, anc_ref, *refs):
    chunks, outs, rows_ref = refs[:vec_count], refs[vec_count : vec_count + sub_count], refs[-1]
    slice_cols, width = chunks[0].shape
    total = vec_count * width
    mine = lax.axis_index("vec") if direct else jnp.int32(0)
    sub = lax.axis_index("sub") if direct else jnp.int32(0)
    for k in range(vec_count):
        at = pl.multiple_of(jnp.bitwise_xor(mine, k) * width, LANES)
        rows_ref[:, pl.ds(at, width)] = chunks[k][...]
    if rows_ref.shape[1] > total:
        rows_ref[:, total:] = jnp.zeros((slice_cols, rows_ref.shape[1] - total), rows_ref.dtype)
    lane = lax.broadcasted_iota(jnp.int32, (slice_cols, LANES), 1)
    for k in range(sub_count):
        owner = jnp.bitwise_xor(sub, k)
        count = counts_ref[owner]
        offset = jnp.int32(0)
        for p in range(sub_count):
            offset = offset + jnp.where(p < owner, counts_ref[p], 0)
        start = offset // LANES
        shift = offset - start * LANES
        back = lax.rem(LANES - shift, LANES)
        base = pl.multiple_of(start * LANES, LANES)
        keep = lane < LANES - shift
        pieces = []
        for j in range(cap // LANES + 1):
            piece = rows_ref[:, pl.ds(base + j * LANES, LANES)].astype(jnp.float32)
            pieces.append(pltpu.roll(piece, back, 1))
        for j in range(cap // LANES):
            merged = jnp.where(keep, pieces[j], pieces[j + 1])
            merged = jnp.where(lane + j * LANES < count, merged, 0.0)
            outs[k][:, j * LANES : (j + 1) * LANES] = merged.astype(rows_ref.dtype)
        labels = [owner] + [anc_ref[l, owner] for l in range(LEVELS)]
        for n, label in enumerate(labels):
            at = pl.multiple_of(interior_total + label * SEPM, SEPM)
            outs[k][:, cap + n * SEPM : cap + (n + 1) * SEPM] = rows_ref[:, pl.ds(at, SEPM)]


def pack(chunks, row_counts, ancestors, cap, direct):
    vec_count = len(chunks)
    slice_cols, width = chunks[0].shape
    dtype = chunks[0].dtype
    sub_count = row_counts.shape[0]
    total = vec_count * width
    interior_total = total - sub_count * SEPM
    slot = cap + (LEVELS + 1) * SEPM
    smem, vmem = pl.BlockSpec(memory_space=pltpu.SMEM), pl.BlockSpec(memory_space=pltpu.VMEM)
    return pl.pallas_call(
        functools.partial(pack_kernel, interior_total, cap, sub_count, vec_count, direct),
        out_shape=[jax.ShapeDtypeStruct((slice_cols, slot), dtype)] * sub_count,
        in_specs=[smem, smem] + [vmem] * vec_count,
        out_specs=[vmem] * sub_count,
        scratch_shapes=[pltpu.VMEM((slice_cols, max(total, interior_total + cap)), dtype)],
        compiler_params=pltpu.CompilerParams(vmem_limit_bytes=8 << 20),
        name="pack_windows",
    )(row_counts, ancestors, *chunks)


def stage_kernel(
    anc_ref, pattern_ref, sep_ref, modes_ref, coupling_ref,
    sep_out, modes_out, coupling_out, sep_sem, modes_sem, coupling_sem,
):
    phys = coupling_out.shape[0]
    me = lax.axis_index("sub")
    whole = pltpu.make_async_copy(coupling_ref, coupling_out, coupling_sem)
    whole.start()
    parts = [pltpu.make_async_copy(modes_ref, modes_out, modes_sem)]
    for k in range(LEVELS + 1):
        label = me if k == 0 else anc_ref[k - 1, me]
        part = pltpu.make_async_copy(
            sep_ref.at[pl.ds(pl.multiple_of(label * BW, BW), BW)],
            sep_out.at[pl.ds(k * BW, BW)],
            sep_sem.at[k],
        )
        parts.append(part)
    for part in parts:
        part.start()
    whole.wait()
    for b in range(phys // BW):
        for l in range(LEVELS):

            @pl.when(pattern_ref[l, 0, b] == 0)
            def _(b=b, l=l):
                coupling_out[b * BW : (b + 1) * BW, l * BW : (l + 1) * BW] = jnp.zeros(
                    (BW, BW), coupling_out.dtype
                )

    for part in parts:
        part.wait()


def stage(ancestors, pattern, separator_modes, modes, coupling):
    hbm = pl.BlockSpec(memory_space=pl.ANY)
    smem, vmem = pl.BlockSpec(memory_space=pltpu.SMEM), pl.BlockSpec(memory_space=pltpu.VMEM)
    moved = 2 * separator_modes.size + 2 * coupling.size + 2 * modes.size
    return pl.pallas_call(
        stage_kernel,
        out_shape=(
            pltpu.VMEM(((LEVELS + 1) * BW, SEPM), coupling.dtype),
            pltpu.VMEM(modes.shape, modes.dtype),
            pltpu.VMEM(coupling.shape, coupling.dtype),
        ),
        in_specs=[smem, smem, hbm, hbm, hbm],
        out_specs=(vmem, vmem, vmem),
        scratch_shapes=[
            pltpu.SemaphoreType.DMA((LEVELS + 1,)),
            pltpu.SemaphoreType.DMA,
            pltpu.SemaphoreType.DMA,
        ],
        compiler_params=pltpu.CompilerParams(vmem_limit_bytes=4 << 20),
        cost_estimate=pl.CostEstimate(flops=0, transcendentals=0, bytes_accessed=moved),
        name="stage_operands",
    )(ancestors, pattern, separator_modes, modes, coupling)


def field_kernel(rows, slot_count, *refs):
    slots = refs[:slot_count]
    sep_ref, modes_ref, coupling_ref = refs[slot_count : slot_count + 3]
    field_ref, own_ref = refs[slot_count + 3 : slot_count + 5]
    got_ref, coef_ref, above_ref, block_ref, sems = refs[slot_count + 5 :]
    phys, cap = modes_ref.shape
    slice_cols = slots[0].shape[0]
    sub = lax.axis_index("sub")
    for k in range(slot_count):
        turned = jnp.bitwise_xor(sub, k) if slot_count > 1 else 0
        at = pl.multiple_of(turned * slice_cols, slice_cols)
        got_ref[pl.ds(at, slice_cols), :] = slots[k][...]
    coef_ref[...] = got_ref[:, :cap].T
    for k in range(LEVELS + 1):
        part = got_ref[:, cap + k * SEPM : cap + (k + 1) * SEPM]
        block = lax.dot_general(
            sep_ref[k * BW : (k + 1) * BW, :], part, CONTRACT, preferred_element_type=jnp.float32
        ).astype(jnp.bfloat16)
        if k == 0:
            own_ref[...] = block
        else:
            above_ref[(k - 1) * BW : k * BW, :] = block
    copies = []
    for s in range(phys // rows):
        at = slice(s * rows, (s + 1) * rows)
        acc = jnp.dot(modes_ref[at, :], coef_ref[...], preferred_element_type=jnp.float32)
        acc = acc + jnp.dot(coupling_ref[at, :], above_ref[...], preferred_element_type=jnp.float32)
        block_ref[at, :] = acc.astype(block_ref.dtype)
        copy = pltpu.make_async_copy(
            block_ref.at[pl.ds(s * rows, rows)], field_ref.at[pl.ds(s * rows, rows)], sems.at[s]
        )
        copy.start()
        copies.append(copy)
    for copy in copies:
        copy.wait()


def fields(slots, sep, modes, coupling):
    slot_count = len(slots)
    phys, cap = modes.shape
    group = slot_count * slots[0].shape[0]
    rows = 2 * BW
    vmem = pl.BlockSpec(memory_space=pltpu.VMEM)
    return pl.pallas_call(
        functools.partial(field_kernel, rows, slot_count),
        out_shape=(
            jax.ShapeDtypeStruct((phys, group), jnp.bfloat16),
            jax.ShapeDtypeStruct((BW, group), jnp.bfloat16),
        ),
        in_specs=[vmem] * (slot_count + 3),
        out_specs=(pl.BlockSpec(memory_space=pl.ANY), vmem),
        scratch_shapes=[
            pltpu.VMEM((group, slots[0].shape[1]), jnp.bfloat16),
            pltpu.VMEM((cap, group), jnp.bfloat16),
            pltpu.VMEM((LEVELS * BW, group), jnp.bfloat16),
            pltpu.VMEM((phys, group), jnp.bfloat16),
            pltpu.SemaphoreType.DMA((phys // rows,)),
        ],
        compiler_params=pltpu.CompilerParams(vmem_limit_bytes=16 << 20),
        name="interior_and_separator_fields",
    )(*slots, sep, modes, coupling)


def in_hbm(array):
    return pltpu.with_memory_space_constraint(array, pltpu.HBM)


def body(coefficients, row_counts, ancestors, interior_modes, separator_modes, coupling, pattern):
    vec_count, sub_count = lax.axis_size("vec"), lax.axis_size("sub")
    slice_cols = coefficients.shape[0] // vec_count
    cap = interior_modes.shape[1]
    counts = in_hbm(row_counts)
    above = in_hbm(ancestors.T)
    gates = in_hbm(jnp.transpose(pattern, (2, 0, 1)))
    powers = vec_count & (vec_count - 1) == 0 and sub_count & (sub_count - 1) == 0
    if powers and slice_cols % ROWS == 0:
        chunks = exchange(split(in_hbm(coefficients), vec_count), "vec")
        slots = exchange(pack(chunks, counts, above, cap, True), "sub")
    else:
        regrouped = coefficients.reshape(vec_count, slice_cols, coefficients.shape[1])
        regrouped = lax.all_to_all(regrouped, "vec", split_axis=0, concat_axis=0, tiled=True)
        slots = jnp.stack(pack(list(regrouped), counts, above, cap, False))
        slots = lax.all_to_all(slots, "sub", split_axis=0, concat_axis=0, tiled=True)
        slots = [slots.reshape(-1, slots.shape[2])]
    sep, modes, masked = stage(
        above, gates, in_hbm(separator_modes), in_hbm(interior_modes), in_hbm(coupling)
    )
    return fields(slots, sep, modes, masked)


def solution(mesh):
    placed = (P("sub", "vec"), P(), P(), P("sub", None), P(), P("sub", None), P("sub", None, None))
    return jax.shard_map(
        body,
        mesh=mesh,
        in_specs=placed,
        out_specs=(P("sub", "vec"), P("sub", "vec")),
        check_vma=False,
    )
```

time: 68.6 us -> 39.5 us (0.58)
  the two profiles are of different devices: /device:TPU:0 before, /device:TPU:20 now
where the time goes in v1:
time: 39.5 us; the launch traced here: 39.2 us
  Pallas kernels  14 us (35%)
  waiting for transfers between devices  13.2 us (33%)
  starting transfers between devices  11.3 us (29%)
  between operations  0.68 us (2%)
    ppermute x10, waiting for transfers between devices, exchange(): lax.ppermute(blocks[k], axis, partner_pairs(count, k))  13.2 us
    ppermute x10, starting transfers between devices, exchange(): lax.ppermute(blocks[k], axis, partner_pairs(count, k))  11.3 us
    pallas_call x1, Pallas kernels, stage(): pl.pallas_call(stage_kernel, out_shape=(pltpu.VMEM(((LEVELS + 1) * BW, SE...  5.99 us
    pallas_call x1, Pallas kernels, fields(): pl.pallas_call(functools.partial(field_kernel, rows, slot_count), out_sha...  5.81 us
    pallas_call x1, Pallas kernels, pack(): pl.pallas_call(functools.partial(pack_kernel, interior_total, cap, sub_co...  1.13 us
    pallas_call x1, Pallas kernels, split(): pl.pallas_call(split_kernel, out_shape=[jax.ShapeDtypeStruct(shape, coeff...  1.05 us
  transfers between devices with their start and end apart: 10, of which 5 were waited for; matrix products, arithmetic and copies ran while one was open for 0% of the time, Pallas kernels for 15%

profile of v1, /device:TPU:20, one launch (start us, length us, event | category | flops | bytes accessed | tf_op | source)
XLA Modules:
  0.0 39.2 jit_solution(3399576536811011279)
XLA Ops:
  0.6 1.1 %split_slices.1 = (bf16[32,1280]{1,0:T(8,128)(2,1)S(1)}, bf16[32,1280]{1,0:T(8,128)(2,1)S(1)}, bf16[32,1280]{1,0:T(8,128)(2,1)S(1)}, bf16[32,1280]{1,0:T(8,128)(2,1)S(1)}) custom-call(bf16[128,1280]{1,0:T(8,128)(2,1)} %coef_ref.1), custom_call_target="tpu_custom_call" | custom-call | tf_op jit(solution)/shard_map/split_slices/pallas_call | solution.py:45
  1.7 0.1 collective-permute-start
  1.8 0.6 %collective-permute-start.1 = (bf16[32,1280]{1,0:T(8,128)(2,1)S(1)}, bf16[32,1280]{1,0:T(8,128)(2,1)S(1)}, u32[]{:S(2)}, u32[]{:S(2)}) collective-permute-start(bf16[32,1280]{1,0:T(8,128)(2,1)S(1)} %get-tuple-element.19), channel_id=1, source_target_pairs={{0,2},{1,3},{2,0},{3,1},{4,6},{5,7},{6,4},{7,5},{8,10},{9,11},{10,... | collective-permute-start | bytes 245768 | tf_op jit(solution)/shard_map/ppermute | solution.py:24
  2.3 1.3 %collective-permute-start.2 = (bf16[32,1280]{1,0:T(8,128)(2,1)S(1)}, bf16[32,1280]{1,0:T(8,128)(2,1)S(1)}, u32[]{:S(2)}, u32[]{:S(2)}) collective-permute-start(bf16[32,1280]{1,0:T(8,128)(2,1)S(1)} %get-tuple-element.20), channel_id=1, source_target_pairs={{0,3},{1,2},{2,1},{3,0},{4,7},{5,6},{6,5},{7,4},{8,11},{9,10},{10,... | collective-permute-start | bytes 245768 | tf_op jit(solution)/shard_map/ppermute | solution.py:24
  3.6 0.0 collective-permute-done.refs_1_
  3.6 3.4 %collective-permute-done.1.refs_2_ = bf16[32,1280]{1,0:T(8,128)(2,1)S(1)} collective-permute-done((bf16[32,1280]{1,0:T(8,128)(2,1)S(1)}, bf16[32,1280]{1,0:T(8,128)(2,1)S(1)}, u32[]{:S(2)}, u32[]{:S(2)}) %collective-permute-start.1) | collective-permute-done | bytes 81952 | tf_op jit(solution)/shard_map/ppermute | solution.py:24
  7.1 0.8 %collective-permute-done.2.refs_3_ = bf16[32,1280]{1,0:T(8,128)(2,1)S(1)} collective-permute-done((bf16[32,1280]{1,0:T(8,128)(2,1)S(1)}, bf16[32,1280]{1,0:T(8,128)(2,1)S(1)}, u32[]{:S(2)}, u32[]{:S(2)}) %collective-permute-start.2) | collective-permute-done | bytes 81952 | tf_op jit(solution)/shard_map/ppermute | solution.py:24
  7.9 1.1 %pack_windows.1 = (bf16[32,1536]{1,0:T(8,128)(2,1)S(1)}, bf16[32,1536]{1,0:T(8,128)(2,1)S(1)}, bf16[32,1536]{1,0:T(8,128)(2,1)S(1)}, bf16[32,1536]{1,0:T(8,128)(...) custom-call(s32[8]{0:T(128)} %counts_ref.1, ...), custom_call_target="tpu_custom_call" | custom-call | tf_op jit(solution)/shard_map/pack_windows/pallas_call | solution.py:102
  9.1 1.6 %collective-permute-start.3 = (bf16[32,1536]{1,0:T(8,128)(2,1)S(1)}, bf16[32,1536]{1,0:T(8,128)(2,1)S(1)}, u32[]{:S(2)}, u32[]{:S(2)}) collective-permute-start(bf16[32,1536]{1,0:T(8,128)(2,1)S(1)} %get-tuple-element.22), channel_id=1, source_target_pairs={{0,4},{4,0},{8,12},{12,8},{16,20},{20,16},{24,28},{28,24},{1,5},{5... | collective-permute-start | bytes 294920 | tf_op jit(solution)/shard_map/ppermute | solution.py:24
  10.6 1.6 %collective-permute-start.4 = (bf16[32,1536]{1,0:T(8,128)(2,1)S(1)}, bf16[32,1536]{1,0:T(8,128)(2,1)S(1)}, u32[]{:S(2)}, u32[]{:S(2)}) collective-permute-start(bf16[32,1536]{1,0:T(8,128)(2,1)S(1)} %get-tuple-element.23), channel_id=1, source_target_pairs={{0,8},{4,12},{8,0},{12,4},{16,24},{20,28},{24,16},{28,20},{1,9},{5... | collective-permute-start | bytes 294920 | tf_op jit(solution)/shard_map/ppermute | solution.py:24
  12.2 0.4 %collective-permute-start.5 = (bf16[32,1536]{1,0:T(8,128)(2,1)S(1)}, bf16[32,1536]{1,0:T(8,128)(2,1)S(1)}, u32[]{:S(2)}, u32[]{:S(2)}) collective-permute-start(bf16[32,1536]{1,0:T(8,128)(2,1)S(1)} %get-tuple-element.24), channel_id=1, source_target_pairs={{0,12},{4,8},{8,4},{12,0},{16,28},{20,24},{24,20},{28,16},{1,13},{... | collective-permute-start | bytes 294920 | tf_op jit(solution)/shard_map/ppermute | solution.py:24
  12.6 0.3 collective-permute-start.6
  13.0 3.5 %collective-permute-start.7 = (bf16[32,1536]{1,0:T(8,128)(2,1)S(1)}, bf16[32,1536]{1,0:T(8,128)(2,1)S(1)}, u32[]{:S(2)}, u32[]{:S(2)}) collective-permute-start(bf16[32,1536]{1,0:T(8,128)(2,1)S(1)} %get-tuple-element.26), channel_id=1, source_target_pairs={{0,20},{4,16},{8,28},{12,24},{16,4},{20,0},{24,12},{28,8},{1,21},{... | collective-permute-start | bytes 294920 | tf_op jit(solution)/shard_map/ppermute | solution.py:24
  16.5 0.0 collective-permute-done.3.refs_1_
  16.5 0.5 %collective-permute-start.8 = (bf16[32,1536]{1,0:T(8,128)(2,1)S(1)}, bf16[32,1536]{1,0:T(8,128)(2,1)S(1)}, u32[]{:S(2)}, u32[]{:S(2)}) collective-permute-start(bf16[32,1536]{1,0:T(8,128)(2,1)S(1)} %get-tuple-element.27), channel_id=1, source_target_pairs={{0,24},{4,28},{8,16},{12,20},{16,8},{20,12},{24,0},{28,4},{1,25},{... | collective-permute-start | bytes 294920 | tf_op jit(solution)/shard_map/ppermute | solution.py:24
  16.9 0.0 collective-permute-done.4.refs_2_
  16.9 1.5 %collective-permute-start.9 = (bf16[32,1536]{1,0:T(8,128)(2,1)S(1)}, bf16[32,1536]{1,0:T(8,128)(2,1)S(1)}, u32[]{:S(2)}, u32[]{:S(2)}) collective-permute-start(bf16[32,1536]{1,0:T(8,128)(2,1)S(1)} %get-tuple-element.28), channel_id=1, source_target_pairs={{0,28},{4,24},{8,20},{12,16},{16,12},{20,8},{24,4},{28,0},{1,29},{... | collective-permute-start | bytes 294920 | tf_op jit(solution)/shard_map/ppermute | solution.py:24
  18.5 6.0 %stage_operands.1 = (bf16[1024,128]{1,0:T(8,128)(2,1)S(1)}, bf16[4096,1024]{1,0:T(8,128)(2,1)S(1)}, bf16[4096,768]{1,0:T(8,128)(2,1)S(1)}) custom-call(s32[3,8]{1,0:T(4,128)} %bitcast.3, s32[3,1,16]{2,1,0:T(1,128)} %bitcast.4, bf16[2048,128]{1,0:T(8,128)(2,1)} %sep_ref.1, bf16[4096,1024]{1,0:T(8,128)(2,1)} %modes_ref.1, bf16[4096,768]{1,0:T(8,128)(2,1)} %coupling_ref.1), custom_call_target="tpu_custom_call" | custom-call | bytes 15204352 | tf_op jit(solution)/shard_map/stage_operands/pallas_call | solution.py:150
  24.5 0.0 collective-permute-done.5.refs_3_
  24.5 0.0 collective-permute-done.6.refs_4_
  24.5 2.6 %collective-permute-done.7.refs_5_ = bf16[32,1536]{1,0:T(8,128)(2,1)S(1)} collective-permute-done((bf16[32,1536]{1,0:T(8,128)(2,1)S(1)}, bf16[32,1536]{1,0:T(8,128)(2,1)S(1)}, u32[]{:S(2)}, u32[]{:S(2)}) %collective-permute-start.7) | collective-permute-done | bytes 98336 | tf_op jit(solution)/shard_map/ppermute | solution.py:24
  27.1 4.4 %collective-permute-done.8.refs_6_ = bf16[32,1536]{1,0:T(8,128)(2,1)S(1)} collective-permute-done((bf16[32,1536]{1,0:T(8,128)(2,1)S(1)}, bf16[32,1536]{1,0:T(8,128)(2,1)S(1)}, u32[]{:S(2)}, u32[]{:S(2)}) %collective-permute-start.8) | collective-permute-done | bytes 98336 | tf_op jit(solution)/shard_map/ppermute | solution.py:24
  31.5 2.0 %collective-permute-done.9.refs_7_ = bf16[32,1536]{1,0:T(8,128)(2,1)S(1)} collective-permute-done((bf16[32,1536]{1,0:T(8,128)(2,1)S(1)}, bf16[32,1536]{1,0:T(8,128)(2,1)S(1)}, u32[]{:S(2)}, u32[]{:S(2)}) %collective-permute-start.9) | collective-permute-done | bytes 98336 | tf_op jit(solution)/shard_map/ppermute | solution.py:24
  33.4 5.8 %interior_and_separator_fields.1 = (bf16[4096,256]{1,0:T(8,128)(2,1)}, bf16[256,256]{1,0:T(8,128)(2,1)}) custom-call(bf16[32,1536]{1,0:T(8,128)(2,1)S(1)} %get-tuple-element.21.refs_0_, bf16[32,1536]{1,0:T(8,128)(2,1)S(1)} %collective-permute-done.3.refs_1_, bf16[32,1536]{1,0:T(8,128)(2,1)S(1)} %collective-permute-done.4.refs_2_, ...), custom_call_target="tpu_custom_call" | custom-call | tf_op jit(solution)/shard_map/interior_and_separator_fields/pallas_call | solution.py:213
Async XLA Ops:
  1.7 1.9 %collective-permute-start = (bf16[32,1280]{1,0:T(8,128)(2,1)S(1)}, bf16[32,1280]{1,0:T(8,128)(2,1)S(1)}, u32[]{:S(2)}, u32[]{:S(2)}) collective-permute-start(bf16[32,1280]{1,0:T(8,128)(2,1)S(1)} %get-tuple-element.18), channel_id=1, source_target_pairs={{0,1},{1,0},{2,3},{3,2},{4,5},{5,4},{6,7},{7,6},{8,9},{9,8},{10,11... | collective-permute-start | bytes 245768 | tf_op jit(solution)/shard_map/ppermute | solution.py:24
  1.8 5.3 %collective-permute-start.1 = (bf16[32,1280]{1,0:T(8,128)(2,1)S(1)}, bf16[32,1280]{1,0:T(8,128)(2,1)S(1)}, u32[]{:S(2)}, u32[]{:S(2)}) collective-permute-start(bf16[32,1280]{1,0:T(8,128)(2,1)S(1)} %get-tuple-element.19), channel_id=1, source_target_pairs={{0,2},{1,3},{2,0},{3,1},{4,6},{5,7},{6,4},{7,5},{8,10},{9,11},{10,... | collective-permute-start | bytes 245768 | tf_op jit(solution)/shard_map/ppermute | solution.py:24
  2.3 5.6 %collective-permute-start.2 = (bf16[32,1280]{1,0:T(8,128)(2,1)S(1)}, bf16[32,1280]{1,0:T(8,128)(2,1)S(1)}, u32[]{:S(2)}, u32[]{:S(2)}) collective-permute-start(bf16[32,1280]{1,0:T(8,128)(2,1)S(1)} %get-tuple-element.20), channel_id=1, source_target_pairs={{0,3},{1,2},{2,1},{3,0},{4,7},{5,6},{6,5},{7,4},{8,11},{9,10},{10,... | collective-permute-start | bytes 245768 | tf_op jit(solution)/shard_map/ppermute | solution.py:24
  9.1 7.4 %collective-permute-start.3 = (bf16[32,1536]{1,0:T(8,128)(2,1)S(1)}, bf16[32,1536]{1,0:T(8,128)(2,1)S(1)}, u32[]{:S(2)}, u32[]{:S(2)}) collective-permute-start(bf16[32,1536]{1,0:T(8,128)(2,1)S(1)} %get-tuple-element.22), channel_id=1, source_target_pairs={{0,4},{4,0},{8,12},{12,8},{16,20},{20,16},{24,28},{28,24},{1,5},{5... | collective-permute-start | bytes 294920 | tf_op jit(solution)/shard_map/ppermute | solution.py:24
  10.6 6.3 %collective-permute-start.4 = (bf16[32,1536]{1,0:T(8,128)(2,1)S(1)}, bf16[32,1536]{1,0:T(8,128)(2,1)S(1)}, u32[]{:S(2)}, u32[]{:S(2)}) collective-permute-start(bf16[32,1536]{1,0:T(8,128)(2,1)S(1)} %get-tuple-element.23), channel_id=1, source_target_pairs={{0,8},{4,12},{8,0},{12,4},{16,24},{20,28},{24,16},{28,20},{1,9},{5... | collective-permute-start | bytes 294920 | tf_op jit(solution)/shard_map/ppermute | solution.py:24
  12.2 12.3 %collective-permute-start.5 = (bf16[32,1536]{1,0:T(8,128)(2,1)S(1)}, bf16[32,1536]{1,0:T(8,128)(2,1)S(1)}, u32[]{:S(2)}, u32[]{:S(2)}) collective-permute-start(bf16[32,1536]{1,0:T(8,128)(2,1)S(1)} %get-tuple-element.24), channel_id=1, source_target_pairs={{0,12},{4,8},{8,4},{12,0},{16,28},{20,24},{24,20},{28,16},{1,13},{... | collective-permute-start | bytes 294920 | tf_op jit(solution)/shard_map/ppermute | solution.py:24
  12.6 11.9 %collective-permute-start.6 = (bf16[32,1536]{1,0:T(8,128)(2,1)S(1)}, bf16[32,1536]{1,0:T(8,128)(2,1)S(1)}, u32[]{:S(2)}, u32[]{:S(2)}) collective-permute-start(bf16[32,1536]{1,0:T(8,128)(2,1)S(1)} %get-tuple-element.25), channel_id=1, source_target_pairs={{0,16},{4,20},{8,24},{12,28},{16,0},{20,4},{24,8},{28,12},{1,17},{... | collective-permute-start | bytes 294920 | tf_op jit(solution)/shard_map/ppermute | solution.py:24
  13.0 14.1 %collective-permute-start.7 = (bf16[32,1536]{1,0:T(8,128)(2,1)S(1)}, bf16[32,1536]{1,0:T(8,128)(2,1)S(1)}, u32[]{:S(2)}, u32[]{:S(2)}) collective-permute-start(bf16[32,1536]{1,0:T(8,128)(2,1)S(1)} %get-tuple-element.26), channel_id=1, source_target_pairs={{0,20},{4,16},{8,28},{12,24},{16,4},{20,0},{24,12},{28,8},{1,21},{... | collective-permute-start | bytes 294920 | tf_op jit(solution)/shard_map/ppermute | solution.py:24
  16.5 15.0 %collective-permute-start.8 = (bf16[32,1536]{1,0:T(8,128)(2,1)S(1)}, bf16[32,1536]{1,0:T(8,128)(2,1)S(1)}, u32[]{:S(2)}, u32[]{:S(2)}) collective-permute-start(bf16[32,1536]{1,0:T(8,128)(2,1)S(1)} %get-tuple-element.27), channel_id=1, source_target_pairs={{0,24},{4,28},{8,16},{12,20},{16,8},{20,12},{24,0},{28,4},{1,25},{... | collective-permute-start | bytes 294920 | tf_op jit(solution)/shard_map/ppermute | solution.py:24
  16.9 16.5 %collective-permute-start.9 = (bf16[32,1536]{1,0:T(8,128)(2,1)S(1)}, bf16[32,1536]{1,0:T(8,128)(2,1)S(1)}, u32[]{:S(2)}, u32[]{:S(2)}) collective-permute-start(bf16[32,1536]{1,0:T(8,128)(2,1)S(1)} %get-tuple-element.28), channel_id=1, source_target_pairs={{0,28},{4,24},{8,20},{12,16},{16,12},{20,8},{24,4},{28,0},{1,29},{... | collective-permute-start | bytes 294920 | tf_op jit(solution)/shard_map/ppermute | solution.py:24

commit v2 on v1

v2 whole, which is shorter than its diff:
```python
import functools

import jax
import jax.numpy as jnp
from jax import lax
from jax.experimental import pallas as pl
from jax.experimental.pallas import tpu as pltpu
from jax.sharding import PartitionSpec as P

BW = 256
SEPM = 128
LEVELS = 3
LANES = 128
ROWS = 16
ORD = [0, 1, 4, 2, 6, 5, 3, 7]
CUT = ()
CONTRACT = (((1,), (1,)), ((), ()))


def turn_over(block, axis, count, turn):
    return lax.ppermute(block, axis, [(i, i ^ turn) for i in range(count)])


def split_kernel(coef_ref, *refs):
    count = len(refs) - 1
    sems = refs[count]
    slice_cols = refs[0].shape[0]
    me = lax.axis_index("vec")
    copies = []
    for k in list(range(1, count)) + [0]:
        at = pl.multiple_of(jnp.bitwise_xor(me, k) * slice_cols, slice_cols)
        copy = pltpu.make_async_copy(coef_ref.at[pl.ds(at, slice_cols)], refs[k], sems.at[k])
        copy.start()
        copies.append(copy)
    for copy in copies:
        copy.wait()


def split(coefficients, count):
    shape = (coefficients.shape[0] // count, coefficients.shape[1])
    return pl.pallas_call(
        split_kernel,
        out_shape=[jax.ShapeDtypeStruct(shape, coefficients.dtype)] * count,
        in_specs=[pl.BlockSpec(memory_space=pl.ANY)],
        out_specs=[pl.BlockSpec(memory_space=pltpu.VMEM)] * count,
        scratch_shapes=[pltpu.SemaphoreType.DMA((count,))],
        compiler_params=pltpu.CompilerParams(vmem_limit_bytes=4 << 20),
        name="split_slices",
    )(coefficients)


def put_windows(rows_ref, out_ref, count, offset, cap, lane):
    start = offset // LANES
    shift = offset - start * LANES
    back = lax.rem(LANES - shift, LANES)
    base = pl.multiple_of(start * LANES, LANES)
    keep = lane < LANES - shift
    pieces = []
    for j in range(cap // LANES + 1):
        piece = rows_ref[:, pl.ds(base + j * LANES, LANES)].astype(jnp.float32)
        pieces.append(pltpu.roll(piece, back, 1))
    for j in range(cap // LANES):
        merged = jnp.where(keep, pieces[j], pieces[j + 1])
        merged = jnp.where(lane + j * LANES < count, merged, 0.0)
        out_ref[:, j * LANES : (j + 1) * LANES] = merged.astype(rows_ref.dtype)


def put_separators(from_ref, first, out_ref, to, owner, anc_ref):
    labels = [owner] + [anc_ref[l, owner] for l in range(LEVELS)]
    for n, label in enumerate(labels):
        at = pl.multiple_of(first + label * SEPM, SEPM)
        out_ref[:, to + n * SEPM : to + (n + 1) * SEPM] = from_ref[:, pl.ds(at, SEPM)]


def window_start(counts_ref, sub_count, owner):
    offset = jnp.int32(0)
    for p in range(sub_count):
        offset = offset + jnp.where(p < owner, counts_ref[p], 0)
    return offset


def pack_kernel(interior_total, cap, turns, direct, counts_ref, anc_ref, *refs):
    sub_count = counts_ref.shape[0]
    chunks, outs, rows_ref = refs[1 : -len(turns) - 1], refs[-len(turns) - 1 : -1], refs[-1]
    slice_cols, width = chunks[0].shape
    total = len(chunks) * width
    mine = lax.axis_index("vec") if direct else jnp.int32(0)
    sub = lax.axis_index("sub") if direct else jnp.int32(0)
    for k in range(len(chunks)):
        at = pl.multiple_of(jnp.bitwise_xor(mine, k) * width, LANES)
        rows_ref[:, pl.ds(at, width)] = chunks[k][...]
    if rows_ref.shape[1] > total:
        rows_ref[:, total:] = jnp.zeros((slice_cols, rows_ref.shape[1] - total), rows_ref.dtype)
    lane = lax.broadcasted_iota(jnp.int32, (slice_cols, LANES), 1)
    for out_ref, (turn, has_interior, has_separators) in zip(outs, turns):
        owner = jnp.bitwise_xor(sub, turn)
        if has_interior:
            offset = window_start(counts_ref, sub_count, owner)
            put_windows(rows_ref, out_ref, counts_ref[owner], offset, cap, lane)
        if has_separators:
            put_separators(rows_ref, interior_total, out_ref, cap * has_interior, owner, anc_ref)


def pack(token, chunks, row_counts, ancestors, cap, turns, direct):
    slice_cols, width = chunks[0].shape
    dtype = chunks[0].dtype
    sub_count = row_counts.shape[0]
    total = len(chunks) * width
    interior_total = total - sub_count * SEPM
    kept = (LEVELS + 1) * SEPM
    smem, vmem = pl.BlockSpec(memory_space=pltpu.SMEM), pl.BlockSpec(memory_space=pltpu.VMEM)
    return pl.pallas_call(
        functools.partial(pack_kernel, interior_total, cap, turns, direct),
        out_shape=[jax.ShapeDtypeStruct((slice_cols, cap * a + kept * b), dtype) for _, a, b in turns],
        in_specs=[smem, smem, pl.BlockSpec(memory_space=pl.ANY)] + [vmem] * len(chunks),
        out_specs=[vmem] * len(turns),
        scratch_shapes=[pltpu.VMEM((slice_cols, max(total, interior_total + cap)), dtype)],
        compiler_params=pltpu.CompilerParams(vmem_limit_bytes=8 << 20),
        name="pack_windows",
    )(row_counts, ancestors, token, *chunks)


def stage_modes_kernel(modes_ref, modes_out, token_ref, sem):
    whole = pltpu.make_async_copy(modes_ref, modes_out, sem)
    whole.start()
    token_ref[...] = jnp.zeros_like(token_ref)
    whole.wait()


def stage_modes(modes):
    vmem = pl.BlockSpec(memory_space=pltpu.VMEM)
    return pl.pallas_call(
        stage_modes_kernel,
        out_shape=(pltpu.VMEM(modes.shape, modes.dtype), pltpu.VMEM((8, LANES), jnp.float32)),
        in_specs=[pl.BlockSpec(memory_space=pl.ANY)],
        out_specs=(vmem, vmem),
        scratch_shapes=[pltpu.SemaphoreType.DMA],
        compiler_params=pltpu.CompilerParams(vmem_limit_bytes=4 << 20),
        cost_estimate=pl.CostEstimate(flops=0, transcendentals=0, bytes_accessed=2 * modes.size),
        name="stage_modes",
    )(modes)


def stage_kernel(
    anc_ref, pattern_ref, sep_ref, coupling_ref, sep_out, coupling_out, sep_sem, coupling_sem
):
    phys = coupling_out.shape[0]
    me = lax.axis_index("sub")
    whole = pltpu.make_async_copy(coupling_ref, coupling_out, coupling_sem)
    whole.start()
    parts = []
    for k in range(LEVELS + 1):
        label = me if k == 0 else anc_ref[k - 1, me]
        part = pltpu.make_async_copy(
            sep_ref.at[pl.ds(pl.multiple_of(label * BW, BW), BW)],
            sep_out.at[pl.ds(k * BW, BW)],
            sep_sem.at[k],
        )
        part.start()
        parts.append(part)
    whole.wait()
    for b in range(phys // BW):
        for l in range(LEVELS):

            @pl.when(pattern_ref[l, 0, b] == 0)
            def _(b=b, l=l):
                coupling_out[b * BW : (b + 1) * BW, l * BW : (l + 1) * BW] = jnp.zeros(
                    (BW, BW), coupling_out.dtype
                )

    for part in parts:
        part.wait()


def stage_coupling(ancestors, pattern, separator_modes, coupling):
    hbm = pl.BlockSpec(memory_space=pl.ANY)
    smem, vmem = pl.BlockSpec(memory_space=pltpu.SMEM), pl.BlockSpec(memory_space=pltpu.VMEM)
    return pl.pallas_call(
        stage_kernel,
        out_shape=(
            pltpu.VMEM(((LEVELS + 1) * BW, SEPM), coupling.dtype),
            pltpu.VMEM(coupling.shape, coupling.dtype),
        ),
        in_specs=[smem, smem, hbm, hbm],
        out_specs=(vmem, vmem),
        scratch_shapes=[pltpu.SemaphoreType.DMA((LEVELS + 1,)), pltpu.SemaphoreType.DMA],
        compiler_params=pltpu.CompilerParams(vmem_limit_bytes=4 << 20),
        cost_estimate=pl.CostEstimate(flops=0, transcendentals=0, bytes_accessed=2 * coupling.size),
        name="stage_coupling",
    )(ancestors, pattern, separator_modes, coupling)


def gather_rows(places, slots, got_ref):
    width = got_ref.shape[1]
    for n, lanes, turn in places:
        slice_cols = slots[n].shape[0]
        block = 0 if turn is None else jnp.bitwise_xor(lax.axis_index("sub"), turn)
        at = pl.multiple_of(block * slice_cols, slice_cols)
        got_ref[pl.ds(at, slice_cols), :] = slots[n][:, lanes : lanes + width]


def above_kernel(rows, places, slot_count, *refs):
    slots, (sep_ref, coupling_ref, total_ref, own_ref, got_ref, above_ref) = refs[:slot_count], refs[slot_count:]
    gather_rows(places, slots, got_ref)
    for k in range(LEVELS + 1):
        part = got_ref[:, k * SEPM : (k + 1) * SEPM]
        block = lax.dot_general(
            sep_ref[k * BW : (k + 1) * BW, :], part, CONTRACT, preferred_element_type=jnp.float32
        ).astype(jnp.bfloat16)
        if k == 0:
            own_ref[...] = block
        else:
            above_ref[(k - 1) * BW : k * BW, :] = block
    for s in range(coupling_ref.shape[0] // rows):
        at = slice(s * rows, (s + 1) * rows)
        total_ref[at, :] = jnp.dot(
            coupling_ref[at, :], above_ref[...], preferred_element_type=jnp.float32
        )


def above_fields(slots, places, group, sep, coupling):
    phys = coupling.shape[0]
    vmem = pl.BlockSpec(memory_space=pltpu.VMEM)
    return pl.pallas_call(
        functools.partial(above_kernel, 2 * BW, places, len(slots)),
        out_shape=(
            pltpu.VMEM((phys, group), jnp.float32),
            jax.ShapeDtypeStruct((BW, group), jnp.bfloat16),
        ),
        in_specs=[vmem] * (len(slots) + 2),
        out_specs=(vmem, vmem),
        scratch_shapes=[
            pltpu.VMEM((group, (LEVELS + 1) * SEPM), jnp.bfloat16),
            pltpu.VMEM((LEVELS * BW, group), jnp.bfloat16),
        ],
        compiler_params=pltpu.CompilerParams(vmem_limit_bytes=4 << 20),
        cost_estimate=pl.CostEstimate(
            flops=2 * coupling.size * group, transcendentals=0, bytes_accessed=2 * coupling.size
        ),
        name="separator_fields_and_coupling",
    )(*slots, sep, coupling)


def interior_kernel(rows, places, slot_count, *refs):
    slots, refs = refs[:slot_count], refs[slot_count:]
    modes_ref, total_ref, field_ref, got_ref, coef_ref, block_ref, sems = refs
    gather_rows(places, slots, got_ref)
    coef_ref[...] = got_ref[...].T
    copies = []
    for s in range(modes_ref.shape[0] // rows):
        at = slice(s * rows, (s + 1) * rows)
        acc = jnp.dot(modes_ref[at, :], coef_ref[...], preferred_element_type=jnp.float32)
        block_ref[at, :] = (acc + total_ref[at, :]).astype(block_ref.dtype)
        copy = pltpu.make_async_copy(
            block_ref.at[pl.ds(s * rows, rows)], field_ref.at[pl.ds(s * rows, rows)], sems.at[s]
        )
        copy.start()
        copies.append(copy)
    for copy in copies:
        copy.wait()


def interior(slots, places, group, modes, total):
    phys, cap = modes.shape
    rows = 2 * BW
    vmem = pl.BlockSpec(memory_space=pltpu.VMEM)
    return pl.pallas_call(
        functools.partial(interior_kernel, rows, places, len(slots)),
        out_shape=jax.ShapeDtypeStruct((phys, group), jnp.bfloat16),
        in_specs=[vmem] * (len(slots) + 2),
        out_specs=pl.BlockSpec(memory_space=pl.ANY),
        scratch_shapes=[
            pltpu.VMEM((group, cap), jnp.bfloat16),
            pltpu.VMEM((cap, group), jnp.bfloat16),
            pltpu.VMEM((phys, group), jnp.bfloat16),
            pltpu.SemaphoreType.DMA((phys // rows,)),
        ],
        compiler_params=pltpu.CompilerParams(vmem_limit_bytes=8 << 20),
        name="interior_field",
    )(*slots, modes, total)


def in_hbm(array):
    return pltpu.with_memory_space_constraint(array, pltpu.HBM)


def turn_order(count):
    half = count // 2
    first = [k for k in range(half)]
    return ORD if count == 8 else first + list(range(half, count))


def body(coefficients, row_counts, ancestors, interior_modes, separator_modes, coupling, pattern):
    vec_count, sub_count = lax.axis_size("vec"), lax.axis_size("sub")
    slice_cols = coefficients.shape[0] // vec_count
    group = slice_cols * sub_count
    cap = interior_modes.shape[1]
    kept = (LEVELS + 1) * SEPM
    counts = in_hbm(row_counts)
    above = in_hbm(ancestors.T)
    gates = in_hbm(jnp.transpose(pattern, (2, 0, 1)))
    modes, token = stage_modes(in_hbm(interior_modes))
    sep, masked = stage_coupling(above, gates, in_hbm(separator_modes), in_hbm(coupling))
    powers = vec_count & (vec_count - 1) == 0 and sub_count & (sub_count - 1) == 0
    if powers and sub_count > 1 and slice_cols % ROWS == 0:
        blocks = split(in_hbm(coefficients), vec_count)
        chunks = [turn_over(blocks[k], "vec", vec_count, k) if k else blocks[0] for k in range(vec_count)]
        turns = []
        for k in turn_order(sub_count):
            turns += [(k, 0, 1), (k, 1, 0)] if k in CUT else [(k, 1, 1)]
        packed = pack(token, chunks, counts, above, cap, turns, True)
        slots = [turn_over(p, "sub", sub_count, t[0]) if t[0] else p for p, t in zip(packed, turns)]
        early = [n for n in range(len(turns)) if turns[n][2]]
        late = [n for n in range(len(turns)) if turns[n][1]]
        above_places = [(i, cap * turns[n][1], turns[n][0]) for i, n in enumerate(early)]
        places = [(i, 0, turns[n][0]) for i, n in enumerate(late)]
        early, late = [slots[n] for n in early], [slots[n] for n in late]
    else:
        regrouped = coefficients.reshape(vec_count, slice_cols, coefficients.shape[1])
        regrouped = lax.all_to_all(regrouped, "vec", split_axis=0, concat_axis=0, tiled=True)
        turns = [(k, 1, 1) for k in range(sub_count)]
        slots = pack(token, list(regrouped), counts, above, cap, turns, False)
        slots = lax.all_to_all(jnp.stack(slots), "sub", split_axis=0, concat_axis=0, tiled=True)
        early = late = [slots.reshape(group, cap + kept)]
        above_places, places = [(0, cap, None)], [(0, 0, None)]
    total, own = above_fields(early, above_places, group, sep, masked)
    return interior(late, places, group, modes, total), own


def solution(mesh):
    placed = (P("sub", "vec"), P(), P(), P("sub", None), P(), P("sub", None), P("sub", None, None))
    return jax.shard_map(
        body,
        mesh=mesh,
        in_specs=placed,
        out_specs=(P("sub", "vec"), P("sub", "vec")),
        check_vma=False,
    )
```

time: 39.5 us -> 36.8 us (0.932)
  the two profiles are of different devices: /device:TPU:20 before, /device:TPU:0 now
where the time goes in v2:
time: 36.8 us; the launch traced here: 36.4 us
  starting transfers between devices  19.4 us (53%)
  Pallas kernels  15 us (41%)
  waiting for transfers between devices  1.27 us (3%)
  between operations  0.7 us (2%)
    ppermute x10, starting transfers between devices, turn_over(): return lax.ppermute(block, axis, [(i, i ^ turn) for i in range(count)])  19.4 us
    pallas_call x1, Pallas kernels, stage_coupling(): pl.pallas_call(stage_kernel, out_shape=(pltpu.VMEM(((LEVELS + 1) * BW, SE...  4.01 us
    pallas_call x1, Pallas kernels, stage_modes(): pl.pallas_call(stage_modes_kernel, out_shape=(pltpu.VMEM(modes.shape, mod...  3.39 us
    pallas_call x1, Pallas kernels, interior(): pl.pallas_call(functools.partial(interior_kernel, rows, places, len(slots...  3.38 us
    pallas_call x1, Pallas kernels, above_fields(): pl.pallas_call(functools.partial(above_kernel, 2 * BW, places, len(slots)...  2.03 us
    ppermute x10, waiting for transfers between devices, turn_over(): return lax.ppermute(block, axis, [(i, i ^ turn) for i in range(count)])  1.27 us
    pallas_call x1, Pallas kernels, pack(): pl.pallas_call(functools.partial(pack_kernel, interior_total, cap, turns,...  1.13 us
    pallas_call x1, Pallas kernels, split(): pl.pallas_call(split_kernel, out_shape=[jax.ShapeDtypeStruct(shape, coeff...  1.05 us
  transfers between devices with their start and end apart: 10, of which 2 were waited for; matrix products, arithmetic and copies ran while one was open for 0% of the time, Pallas kernels for 20%

profile of v2, /device:TPU:0, one launch (start us, length us, event | category | flops | bytes accessed | tf_op | source)
XLA Modules:
  0.0 36.4 jit_solution(9409838973779480169)
XLA Ops:
  0.6 1.1 %split_slices.1 = (bf16[32,1280]{1,0:T(8,128)(2,1)S(1)}, bf16[32,1280]{1,0:T(8,128)(2,1)S(1)}, bf16[32,1280]{1,0:T(8,128)(2,1)S(1)}, bf16[32,1280]{1,0:T(8,128)(2,1)S(1)}) custom-call(bf16[128,1280]{1,0:T(8,128)(2,1)} %coef_ref.1), custom_call_target="tpu_custom_call" | custom-call | tf_op jit(solution)/shard_map/split_slices/pallas_call | solution.py:41
  1.7 0.5 %collective-permute-start = (bf16[32,1280]{1,0:T(8,128)(2,1)S(1)}, bf16[32,1280]{1,0:T(8,128)(2,1)S(1)}, u32[]{:S(2)}, u32[]{:S(2)}) collective-permute-start(bf16[32,1280]{1,0:T(8,128)(2,1)S(1)} %get-tuple-element.22), channel_id=1, source_target_pairs={{0,1},{1,0},{2,3},{3,2},{4,5},{5,4},{6,7},{7,6},{8,9},{9,8},{10,11... | collective-permute-start | bytes 245768 | tf_op jit(solution)/shard_map/ppermute | solution.py:21
  2.2 2.6 %collective-permute-start.1 = (bf16[32,1280]{1,0:T(8,128)(2,1)S(1)}, bf16[32,1280]{1,0:T(8,128)(2,1)S(1)}, u32[]{:S(2)}, u32[]{:S(2)}) collective-permute-start(bf16[32,1280]{1,0:T(8,128)(2,1)S(1)} %get-tuple-element.23), channel_id=1, source_target_pairs={{0,2},{1,3},{2,0},{3,1},{4,6},{5,7},{6,4},{7,5},{8,10},{9,11},{10,... | collective-permute-start | bytes 245768 | tf_op jit(solution)/shard_map/ppermute | solution.py:21
  4.8 0.1 collective-permute-start.2
  4.9 3.4 %stage_modes.1 = (bf16[4096,1024]{1,0:T(8,128)(2,1)S(1)}, f32[8,128]{1,0:T(8,128)S(1)}) custom-call(bf16[4096,1024]{1,0:T(8,128)(2,1)} %modes_ref.1), custom_call_target="tpu_custom_call" | custom-call | bytes 8388608 | tf_op jit(solution)/shard_map/stage_modes/pallas_call | solution.py:132
  8.3 0.0 collective-permute-done.refs_2_
  8.3 0.0 collective-permute-done.1.refs_3_
  8.3 1.0 %collective-permute-done.2.refs_4_ = bf16[32,1280]{1,0:T(8,128)(2,1)S(1)} collective-permute-done((bf16[32,1280]{1,0:T(8,128)(2,1)S(1)}, bf16[32,1280]{1,0:T(8,128)(2,1)S(1)}, u32[]{:S(2)}, u32[]{:S(2)}) %collective-permute-start.2) | collective-permute-done | bytes 81952 | tf_op jit(solution)/shard_map/ppermute | solution.py:21
  9.3 1.1 %pack_windows.1 = (bf16[32,1536]{1,0:T(8,128)(2,1)S(1)}, bf16[32,1536]{1,0:T(8,128)(2,1)S(1)}, bf16[32,1536]{1,0:T(8,128)(2,1)S(1)}, bf16[32,1536]{1,0:T(8,128)(...) custom-call(s32[8]{0:T(128)} %counts_ref.1, ...), custom_call_target="tpu_custom_call" | custom-call | tf_op jit(solution)/shard_map/pack_windows/pallas_call | solution.py:112
  10.4 1.8 %collective-permute-start.3 = (bf16[32,1536]{1,0:T(8,128)(2,1)S(1)}, bf16[32,1536]{1,0:T(8,128)(2,1)S(1)}, u32[]{:S(2)}, u32[]{:S(2)}) collective-permute-start(bf16[32,1536]{1,0:T(8,128)(2,1)S(1)} %get-tuple-element.26), channel_id=1, source_target_pairs={{0,4},{4,0},{8,12},{12,8},{16,20},{20,16},{24,28},{28,24},{1,5},{5... | collective-permute-start | bytes 294920 | tf_op jit(solution)/shard_map/ppermute | solution.py:21
  12.2 2.6 %collective-permute-start.4 = (bf16[32,1536]{1,0:T(8,128)(2,1)S(1)}, bf16[32,1536]{1,0:T(8,128)(2,1)S(1)}, u32[]{:S(2)}, u32[]{:S(2)}) collective-permute-start(bf16[32,1536]{1,0:T(8,128)(2,1)S(1)} %get-tuple-element.27), channel_id=1, source_target_pairs={{0,16},{4,20},{8,24},{12,28},{16,0},{20,4},{24,8},{28,12},{1,17},{... | collective-permute-start | bytes 294920 | tf_op jit(solution)/shard_map/ppermute | solution.py:21
  14.8 1.6 %collective-permute-start.5 = (bf16[32,1536]{1,0:T(8,128)(2,1)S(1)}, bf16[32,1536]{1,0:T(8,128)(2,1)S(1)}, u32[]{:S(2)}, u32[]{:S(2)}) collective-permute-start(bf16[32,1536]{1,0:T(8,128)(2,1)S(1)} %get-tuple-element.28), channel_id=1, source_target_pairs={{0,8},{4,12},{8,0},{12,4},{16,24},{20,28},{24,16},{28,20},{1,9},{5... | collective-permute-start | bytes 294920 | tf_op jit(solution)/shard_map/ppermute | solution.py:21
  16.4 0.2 collective-permute-start.6
  16.6 1.7 %collective-permute-start.7 = (bf16[32,1536]{1,0:T(8,128)(2,1)S(1)}, bf16[32,1536]{1,0:T(8,128)(2,1)S(1)}, u32[]{:S(2)}, u32[]{:S(2)}) collective-permute-start(bf16[32,1536]{1,0:T(8,128)(2,1)S(1)} %get-tuple-element.30), channel_id=1, source_target_pairs={{0,20},{4,16},{8,28},{12,24},{16,4},{20,0},{24,12},{28,8},{1,21},{... | collective-permute-start | bytes 294920 | tf_op jit(solution)/shard_map/ppermute | solution.py:21
  18.3 0.0 collective-permute-done.3.refs_1_
  18.3 3.4 %collective-permute-start.8 = (bf16[32,1536]{1,0:T(8,128)(2,1)S(1)}, bf16[32,1536]{1,0:T(8,128)(2,1)S(1)}, u32[]{:S(2)}, u32[]{:S(2)}) collective-permute-start(bf16[32,1536]{1,0:T(8,128)(2,1)S(1)} %get-tuple-element.31), channel_id=1, source_target_pairs={{0,12},{4,8},{8,4},{12,0},{16,28},{20,24},{24,20},{28,16},{1,13},{... | collective-permute-start | bytes 294920 | tf_op jit(solution)/shard_map/ppermute | solution.py:21
  21.7 0.0 collective-permute-done.4.refs_2_
  21.7 5.0 %collective-permute-start.9 = (bf16[32,1536]{1,0:T(8,128)(2,1)S(1)}, bf16[32,1536]{1,0:T(8,128)(2,1)S(1)}, u32[]{:S(2)}, u32[]{:S(2)}) collective-permute-start(bf16[32,1536]{1,0:T(8,128)(2,1)S(1)} %get-tuple-element.32), channel_id=1, source_target_pairs={{0,28},{4,24},{8,20},{12,16},{16,12},{20,8},{24,4},{28,0},{1,29},{... | collective-permute-start | bytes 294920 | tf_op jit(solution)/shard_map/ppermute | solution.py:21
  26.7 4.0 %stage_coupling.1 = (bf16[1024,128]{1,0:T(8,128)(2,1)S(1)}, bf16[4096,768]{1,0:T(8,128)(2,1)S(1)}) custom-call(s32[3,8]{1,0:T(4,128)} %bitcast.3, s32[3,1,16]{2,1,0:T(1,128)} %bitcast.4, bf16[2048,128]{1,0:T(8,128)(2,1)} %sep_ref.1, bf16[4096,768]{1,0:T(8,128)(2,1)} %coupling_ref.1), custom_call_target="tpu_custom_call" | custom-call | bytes 6291456 | tf_op jit(solution)/shard_map/stage_coupling/pallas_call | solution.py:178
  30.7 0.0 collective-permute-done.5.refs_3_
  30.7 0.0 collective-permute-done.6.refs_4_
  30.7 0.3 collective-permute-done.7.refs_5_
  30.9 0.0 collective-permute-done.8.refs_6_
  31.0 0.0 collective-permute-done.9.refs_7_
  31.0 2.0 %separator_fields_and_coupling.1 = (f32[4096,256]{1,0:T(8,128)S(1)}, bf16[256,256]{1,0:T(8,128)(2,1)}) custom-call(bf16[32,1536]{1,0:T(8,128)(2,1)S(1)} %get-tuple-element.25.refs_0_, bf16[32,1536]{1,0:T(8,128)(2,1)S(1)} %collective-permute-done.3.refs_1_, bf16[32,1536]{1,0:T(8,128)(2,1)S(1)} %collective-permute-done.4.refs_2_, ...), custom_call_target="tpu_custom_call" | custom-call | flops 1610612736 | bytes 6291456 | tf_op jit(solution)/shard_map/separator_fields_and_coupling/pallas_call | solution.py:224
  33.0 3.4 %interior_field.1 = bf16[4096,256]{1,0:T(8,128)(2,1)} custom-call(bf16[32,1536]{1,0:T(8,128)(2,1)S(1)} %get-tuple-element.25.refs_0_, bf16[32,1536]{1,0:T(8,128)(2,1)S(1)} %collective-permute-done.3.refs_1_, bf16[32,1536]{1,0:T(8,128)(2,1)S(1)} %collective-permute-done.4.refs_2_, bf16[32,1536]{1,0:T(8,128)(2,1)S(1)} %collective-permute-done.5.refs_3_, ...), custom_call_target="tpu_custom_call" | custom-call | tf_op jit(solution)/shard_map/interior_field/pallas_call | solution.py:267
Async XLA Ops:
  1.7 6.6 %collective-permute-start = (bf16[32,1280]{1,0:T(8,128)(2,1)S(1)}, bf16[32,1280]{1,0:T(8,128)(2,1)S(1)}, u32[]{:S(2)}, u32[]{:S(2)}) collective-permute-start(bf16[32,1280]{1,0:T(8,128)(2,1)S(1)} %get-tuple-element.22), channel_id=1, source_target_pairs={{0,1},{1,0},{2,3},{3,2},{4,5},{5,4},{6,7},{7,6},{8,9},{9,8},{10,11... | collective-permute-start | bytes 245768 | tf_op jit(solution)/shard_map/ppermute | solution.py:21
  2.2 6.1 %collective-permute-start.1 = (bf16[32,1280]{1,0:T(8,128)(2,1)S(1)}, bf16[32,1280]{1,0:T(8,128)(2,1)S(1)}, u32[]{:S(2)}, u32[]{:S(2)}) collective-permute-start(bf16[32,1280]{1,0:T(8,128)(2,1)S(1)} %get-tuple-element.23), channel_id=1, source_target_pairs={{0,2},{1,3},{2,0},{3,1},{4,6},{5,7},{6,4},{7,5},{8,10},{9,11},{10,... | collective-permute-start | bytes 245768 | tf_op jit(solution)/shard_map/ppermute | solution.py:21
  4.8 4.5 %collective-permute-start.2 = (bf16[32,1280]{1,0:T(8,128)(2,1)S(1)}, bf16[32,1280]{1,0:T(8,128)(2,1)S(1)}, u32[]{:S(2)}, u32[]{:S(2)}) collective-permute-start(bf16[32,1280]{1,0:T(8,128)(2,1)S(1)} %get-tuple-element.24), channel_id=1, source_target_pairs={{0,3},{1,2},{2,1},{3,0},{4,7},{5,6},{6,5},{7,4},{8,11},{9,10},{10,... | collective-permute-start | bytes 245768 | tf_op jit(solution)/shard_map/ppermute | solution.py:21
  10.4 7.8 %collective-permute-start.3 = (bf16[32,1536]{1,0:T(8,128)(2,1)S(1)}, bf16[32,1536]{1,0:T(8,128)(2,1)S(1)}, u32[]{:S(2)}, u32[]{:S(2)}) collective-permute-start(bf16[32,1536]{1,0:T(8,128)(2,1)S(1)} %get-tuple-element.26), channel_id=1, source_target_pairs={{0,4},{4,0},{8,12},{12,8},{16,20},{20,16},{24,28},{28,24},{1,5},{5... | collective-permute-start | bytes 294920 | tf_op jit(solution)/shard_map/ppermute | solution.py:21
  12.2 9.5 %collective-permute-start.4 = (bf16[32,1536]{1,0:T(8,128)(2,1)S(1)}, bf16[32,1536]{1,0:T(8,128)(2,1)S(1)}, u32[]{:S(2)}, u32[]{:S(2)}) collective-permute-start(bf16[32,1536]{1,0:T(8,128)(2,1)S(1)} %get-tuple-element.27), channel_id=1, source_target_pairs={{0,16},{4,20},{8,24},{12,28},{16,0},{20,4},{24,8},{28,12},{1,17},{... | collective-permute-start | bytes 294920 | tf_op jit(solution)/shard_map/ppermute | solution.py:21
  14.8 15.9 %collective-permute-start.5 = (bf16[32,1536]{1,0:T(8,128)(2,1)S(1)}, bf16[32,1536]{1,0:T(8,128)(2,1)S(1)}, u32[]{:S(2)}, u32[]{:S(2)}) collective-permute-start(bf16[32,1536]{1,0:T(8,128)(2,1)S(1)} %get-tuple-element.28), channel_id=1, source_target_pairs={{0,8},{4,12},{8,0},{12,4},{16,24},{20,28},{24,16},{28,20},{1,9},{5... | collective-permute-start | bytes 294920 | tf_op jit(solution)/shard_map/ppermute | solution.py:21
  16.4 14.3 %collective-permute-start.6 = (bf16[32,1536]{1,0:T(8,128)(2,1)S(1)}, bf16[32,1536]{1,0:T(8,128)(2,1)S(1)}, u32[]{:S(2)}, u32[]{:S(2)}) collective-permute-start(bf16[32,1536]{1,0:T(8,128)(2,1)S(1)} %get-tuple-element.29), channel_id=1, source_target_pairs={{0,24},{4,28},{8,16},{12,20},{16,8},{20,12},{24,0},{28,4},{1,25},{... | collective-permute-start | bytes 294920 | tf_op jit(solution)/shard_map/ppermute | solution.py:21
  16.6 14.3 %collective-permute-start.7 = (bf16[32,1536]{1,0:T(8,128)(2,1)S(1)}, bf16[32,1536]{1,0:T(8,128)(2,1)S(1)}, u32[]{:S(2)}, u32[]{:S(2)}) collective-permute-start(bf16[32,1536]{1,0:T(8,128)(2,1)S(1)} %get-tuple-element.30), channel_id=1, source_target_pairs={{0,20},{4,16},{8,28},{12,24},{16,4},{20,0},{24,12},{28,8},{1,21},{... | collective-permute-start | bytes 294920 | tf_op jit(solution)/shard_map/ppermute | solution.py:21
  18.3 12.7 %collective-permute-start.8 = (bf16[32,1536]{1,0:T(8,128)(2,1)S(1)}, bf16[32,1536]{1,0:T(8,128)(2,1)S(1)}, u32[]{:S(2)}, u32[]{:S(2)}) collective-permute-start(bf16[32,1536]{1,0:T(8,128)(2,1)S(1)} %get-tuple-element.31), channel_id=1, source_target_pairs={{0,12},{4,8},{8,4},{12,0},{16,28},{20,24},{24,20},{28,16},{1,13},{... | collective-permute-start | bytes 294920 | tf_op jit(solution)/shard_map/ppermute | solution.py:21
  21.7 9.3 %collective-permute-start.9 = (bf16[32,1536]{1,0:T(8,128)(2,1)S(1)}, bf16[32,1536]{1,0:T(8,128)(2,1)S(1)}, u32[]{:S(2)}, u32[]{:S(2)}) collective-permute-start(bf16[32,1536]{1,0:T(8,128)(2,1)S(1)} %get-tuple-element.32), channel_id=1, source_target_pairs={{0,28},{4,24},{8,20},{12,16},{16,12},{20,8},{24,4},{28,0},{1,29},{... | collective-permute-start | bytes 294920 | tf_op jit(solution)/shard_map/ppermute | solution.py:21

commit v3 on v2

--- a/solution.py
+++ b/solution.py
@@ -12,8 +12,11 @@
 LEVELS = 3
 LANES = 128
 ROWS = 16
-ORD = [0, 1, 4, 2, 6, 5, 3, 7]
-CUT = ()
+EARLY_ORDER = [0, 4, 6, 1, 5, 3, 2, 7]
+CUT = (4, 6)
+LATE_ORDER = [0, 4, 6, 5, 1, 3, 2, 7]
+VEC_ORDER = [2, 3, 1, 0]
+AHEAD = 6 << 30
 CONTRACT = (((1,), (1,)), ((), ()))
 
 
@@ -45,6 +48,7 @@
         out_specs=[pl.BlockSpec(memory_space=pltpu.VMEM)] * count,
         scratch_shapes=[pltpu.SemaphoreType.DMA((count,))],
         compiler_params=pltpu.CompilerParams(vmem_limit_bytes=4 << 20),
+        cost_estimate=pl.CostEstimate(flops=AHEAD, transcendentals=0, bytes_accessed=1 << 20),
         name="split_slices",
     )(coefficients)
 
@@ -79,16 +83,16 @@
     return offset
 
 
-def pack_kernel(interior_total, cap, turns, direct, counts_ref, anc_ref, *refs):
+def pack_kernel(interior_total, cap, turns, direct, chunk_turns, counts_ref, anc_ref, *refs):
     sub_count = counts_ref.shape[0]
     chunks, outs, rows_ref = refs[1 : -len(turns) - 1], refs[-len(turns) - 1 : -1], refs[-1]
     slice_cols, width = chunks[0].shape
     total = len(chunks) * width
     mine = lax.axis_index("vec") if direct else jnp.int32(0)
     sub = lax.axis_index("sub") if direct else jnp.int32(0)
-    for k in range(len(chunks)):
-        at = pl.multiple_of(jnp.bitwise_xor(mine, k) * width, LANES)
-        rows_ref[:, pl.ds(at, width)] = chunks[k][...]
+    for chunk, turn in zip(chunks, chunk_turns):
+        at = pl.multiple_of(jnp.bitwise_xor(mine, turn) * width, LANES)
+        rows_ref[:, pl.ds(at, width)] = chunk[...]
     if rows_ref.shape[1] > total:
         rows_ref[:, total:] = jnp.zeros((slice_cols, rows_ref.shape[1] - total), rows_ref.dtype)
     lane = lax.broadcasted_iota(jnp.int32, (slice_cols, LANES), 1)
@@ -101,7 +105,7 @@
             put_separators(rows_ref, interior_total, out_ref, cap * has_interior, owner, anc_ref)
 
 
-def pack(token, chunks, row_counts, ancestors, cap, turns, direct):
+def pack(token, chunks, chunk_turns, row_counts, ancestors, cap, turns, direct):
     slice_cols, width = chunks[0].shape
     dtype = chunks[0].dtype
     sub_count = row_counts.shape[0]
@@ -110,7 +114,7 @@
     kept = (LEVELS + 1) * SEPM
     smem, vmem = pl.BlockSpec(memory_space=pltpu.SMEM), pl.BlockSpec(memory_space=pltpu.VMEM)
     return pl.pallas_call(
-        functools.partial(pack_kernel, interior_total, cap, turns, direct),
+        functools.partial(pack_kernel, interior_total, cap, turns, direct, chunk_turns),
         out_shape=[jax.ShapeDtypeStruct((slice_cols, cap * a + kept * b), dtype) for _, a, b in turns],
         in_specs=[smem, smem, pl.BlockSpec(memory_space=pl.ANY)] + [vmem] * len(chunks),
         out_specs=[vmem] * len(turns),
@@ -120,73 +124,33 @@
     )(row_counts, ancestors, token, *chunks)
 
 
-def stage_modes_kernel(modes_ref, modes_out, token_ref, sem):
-    whole = pltpu.make_async_copy(modes_ref, modes_out, sem)
-    whole.start()
-    token_ref[...] = jnp.zeros_like(token_ref)
-    whole.wait()
-
-
-def stage_modes(modes):
-    vmem = pl.BlockSpec(memory_space=pltpu.VMEM)
-    return pl.pallas_call(
-        stage_modes_kernel,
-        out_shape=(pltpu.VMEM(modes.shape, modes.dtype), pltpu.VMEM((8, LANES), jnp.float32)),
-        in_specs=[pl.BlockSpec(memory_space=pl.ANY)],
-        out_specs=(vmem, vmem),
-        scratch_shapes=[pltpu.SemaphoreType.DMA],
-        compiler_params=pltpu.CompilerParams(vmem_limit_bytes=4 << 20),
-        cost_estimate=pl.CostEstimate(flops=0, transcendentals=0, bytes_accessed=2 * modes.size),
-        name="stage_modes",
-    )(modes)
-
-
-def stage_kernel(
-    anc_ref, pattern_ref, sep_ref, coupling_ref, sep_out, coupling_out, sep_sem, coupling_sem
-):
-    phys = coupling_out.shape[0]
+def mask_kernel(anc_ref, pattern_ref, sep_ref, coupling_ref, sep_out, coupling_out):
     me = lax.axis_index("sub")
-    whole = pltpu.make_async_copy(coupling_ref, coupling_out, coupling_sem)
-    whole.start()
-    parts = []
     for k in range(LEVELS + 1):
         label = me if k == 0 else anc_ref[k - 1, me]
-        part = pltpu.make_async_copy(
-            sep_ref.at[pl.ds(pl.multiple_of(label * BW, BW), BW)],
-            sep_out.at[pl.ds(k * BW, BW)],
-            sep_sem.at[k],
-        )
-        part.start()
-        parts.append(part)
-    whole.wait()
-    for b in range(phys // BW):
+        at = pl.multiple_of(label * BW, BW)
+        sep_out[k * BW : (k + 1) * BW, :] = sep_ref[pl.ds(at, BW), :]
+    for b in range(coupling_ref.shape[0] // BW):
         for l in range(LEVELS):
-
-            @pl.when(pattern_ref[l, 0, b] == 0)
-            def _(b=b, l=l):
-                coupling_out[b * BW : (b + 1) * BW, l * BW : (l + 1) * BW] = jnp.zeros(
-                    (BW, BW), coupling_out.dtype
-                )
-
-    for part in parts:
-        part.wait()
-
-
-def stage_coupling(ancestors, pattern, separator_modes, coupling):
-    hbm = pl.BlockSpec(memory_space=pl.ANY)
+            live = pattern_ref[l, 0, b] != 0
+            at = (slice(b * BW, (b + 1) * BW), slice(l * BW, (l + 1) * BW))
+            part = coupling_ref[at]
+            coupling_out[at] = jnp.where(live, part, jnp.zeros_like(part))
+
+
+def mask(ancestors, pattern, separator_modes, coupling):
     smem, vmem = pl.BlockSpec(memory_space=pltpu.SMEM), pl.BlockSpec(memory_space=pltpu.VMEM)
     return pl.pallas_call(
-        stage_kernel,
+        mask_kernel,
         out_shape=(
             pltpu.VMEM(((LEVELS + 1) * BW, SEPM), coupling.dtype),
             pltpu.VMEM(coupling.shape, coupling.dtype),
         ),
-        in_specs=[smem, smem, hbm, hbm],
+        in_specs=[smem, smem, vmem, vmem],
         out_specs=(vmem, vmem),
-        scratch_shapes=[pltpu.SemaphoreType.DMA((LEVELS + 1,)), pltpu.SemaphoreType.DMA],
         compiler_params=pltpu.CompilerParams(vmem_limit_bytes=4 << 20),
         cost_estimate=pl.CostEstimate(flops=0, transcendentals=0, bytes_accessed=2 * coupling.size),
-        name="stage_coupling",
+        name="mask_coupling",
     )(ancestors, pattern, separator_modes, coupling)
 
 
@@ -284,10 +248,8 @@
     return pltpu.with_memory_space_constraint(array, pltpu.HBM)
 
 
-def turn_order(count):
-    half = count // 2
-    first = [k for k in range(half)]
-    return ORD if count == 8 else first + list(range(half, count))
+def turn_order(count, order):
+    return order if count == len(order) else list(range(count))
 
 
 def body(coefficients, row_counts, ancestors, interior_modes, separator_modes, coupling, pattern):
@@ -299,19 +261,20 @@
     counts = in_hbm(row_counts)
     above = in_hbm(ancestors.T)
     gates = in_hbm(jnp.transpose(pattern, (2, 0, 1)))
-    modes, token = stage_modes(in_hbm(interior_modes))
-    sep, masked = stage_coupling(above, gates, in_hbm(separator_modes), in_hbm(coupling))
+    sep, masked = mask(above, gates, separator_modes, coupling)
     powers = vec_count & (vec_count - 1) == 0 and sub_count & (sub_count - 1) == 0
     if powers and sub_count > 1 and slice_cols % ROWS == 0:
         blocks = split(in_hbm(coefficients), vec_count)
-        chunks = [turn_over(blocks[k], "vec", vec_count, k) if k else blocks[0] for k in range(vec_count)]
+        chunk_turns = turn_order(vec_count, VEC_ORDER)
+        chunks = [turn_over(blocks[k], "vec", vec_count, k) if k else blocks[0] for k in chunk_turns]
         turns = []
-        for k in turn_order(sub_count):
+        for k in turn_order(sub_count, EARLY_ORDER):
             turns += [(k, 0, 1), (k, 1, 0)] if k in CUT else [(k, 1, 1)]
-        packed = pack(token, chunks, counts, above, cap, turns, True)
+        packed = pack(sep, chunks, chunk_turns, counts, above, cap, turns, True)
         slots = [turn_over(p, "sub", sub_count, t[0]) if t[0] else p for p, t in zip(packed, turns)]
         early = [n for n in range(len(turns)) if turns[n][2]]
         late = [n for n in range(len(turns)) if turns[n][1]]
+        late.sort(key=lambda n: turn_order(sub_count, LATE_ORDER).index(turns[n][0]))
         above_places = [(i, cap * turns[n][1], turns[n][0]) for i, n in enumerate(early)]
         places = [(i, 0, turns[n][0]) for i, n in enumerate(late)]
         early, late = [slots[n] for n in early], [slots[n] for n in late]
@@ -319,12 +282,12 @@
         regrouped = coefficients.reshape(vec_count, slice_cols, coefficients.shape[1])
         regrouped = lax.all_to_all(regrouped, "vec", split_axis=0, concat_axis=0, tiled=True)
         turns = [(k, 1, 1) for k in range(sub_count)]
-        slots = pack(token, list(regrouped), counts, above, cap, turns, False)
+        slots = pack(sep, list(regrouped), list(range(vec_count)), counts, above, cap, turns, False)
         slots = lax.all_to_all(jnp.stack(slots), "sub", split_axis=0, concat_axis=0, tiled=True)
         early = late = [slots.reshape(group, cap + kept)]
         above_places, places = [(0, cap, None)], [(0, 0, None)]
     total, own = above_fields(early, above_places, group, sep, masked)
-    return interior(late, places, group, modes, total), own
+    return interior(late, places, group, interior_modes, total), own
 
 
 def solution(mesh):

time: 36.8 us -> 35.6 us (0.967)
  waiting for transfers between devices: 1.27 us -> 9.85 us
  Pallas kernels: 15 us -> 9.43 us
  starting transfers between devices: 19.4 us -> 15.4 us
    ppermute x10 -> x12, waiting for transfers between devices: 1.27 us -> 9.85 us  [turn_over(): return lax.ppermute(block, axis, [(i, i ^ turn) for i in range(count)])]
    pallas_call x2 -> x1, Pallas kernels: 7.4 us -> 1.69 us  [mask(): pl.pallas_call(mask_kernel, out_shape=(pltpu.VMEM(((LEVELS + 1) * BW, SEP...]
    ppermute x10 -> x12, starting transfers between devices: 19.4 us -> 15.4 us  [turn_over(): return lax.ppermute(block, axis, [(i, i ^ turn) for i in range(count)])]
  transfers between devices with their start and end apart: 10 -> 12, of which waited for: 2 -> 6; matrix products, arithmetic and copies ran while one was open for 0% -> 0% of each run, Pallas kernels for 20% -> 10%
where the time goes in v3:
time: 35.6 us; the launch traced here: 35.4 us
  starting transfers between devices  15.4 us (43%)
  waiting for transfers between devices  9.85 us (28%)
  Pallas kernels  9.43 us (26%)
  between operations  0.69 us (2%)
    ppermute x12, starting transfers between devices, turn_over(): return lax.ppermute(block, axis, [(i, i ^ turn) for i in range(count)])  15.4 us
    ppermute x12, waiting for transfers between devices, turn_over(): return lax.ppermute(block, axis, [(i, i ^ turn) for i in range(count)])  9.85 us
    pallas_call x1, Pallas kernels, interior(): pl.pallas_call(functools.partial(interior_kernel, rows, places, len(slots...  3.39 us
    pallas_call x1, Pallas kernels, above_fields(): pl.pallas_call(functools.partial(above_kernel, 2 * BW, places, len(slots)...  2.02 us
    pallas_call x1, Pallas kernels, mask(): pl.pallas_call(mask_kernel, out_shape=(pltpu.VMEM(((LEVELS + 1) * BW, SEP...  1.69 us
    pallas_call x1, Pallas kernels, split(): pl.pallas_call(split_kernel, out_shape=[jax.ShapeDtypeStruct(shape, coeff...  1.2 us
    pallas_call x1, Pallas kernels, pack(): pl.pallas_call(functools.partial(pack_kernel, interior_total, cap, turns,...  1.13 us
  transfers between devices with their start and end apart: 12, of which 6 were waited for; matrix products, arithmetic and copies ran while one was open for 0% of the time, Pallas kernels for 10%

profile of v3, /device:TPU:0, one launch (start us, length us, event | category | flops | bytes accessed | tf_op | source)
XLA Modules:
  0.0 35.4 jit_solution(15187816327792201024)
XLA Ops:
  0.6 0.0 copy-start.1
  0.6 0.0 copy-start.2
  0.6 1.2 %split_slices.1 = (bf16[32,1280]{1,0:T(8,128)(2,1)S(1)}, bf16[32,1280]{1,0:T(8,128)(2,1)S(1)}, bf16[32,1280]{1,0:T(8,128)(2,1)S(1)}, bf16[32,1280]{1,0:T(8,128)(2,1)S(1)}) custom-call(bf16[128,1280]{1,0:T(8,128)(2,1)} %coef_ref.1), custom_call_target="tpu_custom_call" | custom-call | flops 6442450944 | bytes 1048576 | tf_op jit(solution)/shard_map/split_slices/pallas_call | solution.py:44
  1.9 3.0 %collective-permute-start = (bf16[32,1280]{1,0:T(8,128)(2,1)S(1)}, bf16[32,1280]{1,0:T(8,128)(2,1)S(1)}, u32[]{:S(2)}, u32[]{:S(2)}) collective-permute-start(bf16[32,1280]{1,0:T(8,128)(2,1)S(1)} %get-tuple-element.21), channel_id=1, source_target_pairs={{0,2},{1,3},{2,0},{3,1},{4,6},{5,7},{6,4},{7,5},{8,10},{9,11},{10,... | collective-permute-start | bytes 245768 | tf_op jit(solution)/shard_map/ppermute | solution.py:24
  4.9 0.0 collective-permute-start.1
  4.9 0.2 collective-permute-start.2
  5.1 0.0 copy-done.1
  5.1 1.7 %mask_coupling.1 = (bf16[1024,128]{1,0:T(8,128)(2,1)S(1)}, bf16[4096,768]{1,0:T(8,128)(2,1)S(1)}) custom-call(s32[3,8]{1,0:T(4,128)} %bitcast.2, s32[3,1,16]{2,1,0:T(1,128)} %bitcast.4, bf16[2048,128]{1,0:T(8,128)(2,1)S(1)} %copy-done.2, bf16[4096,768]{1,0:T(8,128)(2,1)S(1)} %copy-done.1), custom_call_target="tpu_custom_call" | custom-call | bytes 6291456 | tf_op jit(solution)/shard_map/mask_coupling/pallas_call | solution.py:143
  6.8 0.7 %collective-permute-done.refs_1_ = bf16[32,1280]{1,0:T(8,128)(2,1)S(1)} collective-permute-done((bf16[32,1280]{1,0:T(8,128)(2,1)S(1)}, bf16[32,1280]{1,0:T(8,128)(2,1)S(1)}, u32[]{:S(2)}, u32[]{:S(2)}) %collective-permute-start) | collective-permute-done | bytes 81952 | tf_op jit(solution)/shard_map/ppermute | solution.py:24
  7.5 1.9 %collective-permute-done.1.refs_2_ = bf16[32,1280]{1,0:T(8,128)(2,1)S(1)} collective-permute-done((bf16[32,1280]{1,0:T(8,128)(2,1)S(1)}, bf16[32,1280]{1,0:T(8,128)(2,1)S(1)}, u32[]{:S(2)}, u32[]{:S(2)}) %collective-permute-start.1) | collective-permute-done | bytes 81952 | tf_op jit(solution)/shard_map/ppermute | solution.py:24
  9.4 0.0 collective-permute-done.2.refs_3_
  9.4 1.1 %pack_windows.1 = (bf16[32,1536]{1,0:T(8,128)(2,1)S(1)}, bf16[32,512]{1,0:T(8,128)(2,1)S(1)}, bf16[32,1024]{1,0:T(8,128)(2,1)S(1)}, bf16[32,512]{1,0:T(8,128)(2,...) custom-call(s32[8]{0:T(128)} %counts_ref.1, ...), custom_call_target="tpu_custom_call" | custom-call | tf_op jit(solution)/shard_map/pack_windows/pallas_call | solution.py:116
  10.5 2.9 %collective-permute-start.10 = (bf16[32,512]{1,0:T(8,128)(2,1)S(1)}, bf16[32,512]{1,0:T(8,128)(2,1)S(1)}, u32[]{:S(2)}, u32[]{:S(2)}) collective-permute-start(bf16[32,512]{1,0:T(8,128)(2,1)S(1)} %get-tuple-element.33), channel_id=1, source_target_pairs={{0,16},{4,20},{8,24},{12,28},{16,0},{20,4},{24,8},{28,12},{1,17},{... | collective-permute-start | bytes 98312 | tf_op jit(solution)/shard_map/ppermute | solution.py:24
  13.4 1.3 %collective-permute-start.11 = (bf16[32,512]{1,0:T(8,128)(2,1)S(1)}, bf16[32,512]{1,0:T(8,128)(2,1)S(1)}, u32[]{:S(2)}, u32[]{:S(2)}) collective-permute-start(bf16[32,512]{1,0:T(8,128)(2,1)S(1)} %get-tuple-element.34), channel_id=1, source_target_pairs={{0,24},{4,28},{8,16},{12,20},{16,8},{20,12},{24,0},{28,4},{1,25},{... | collective-permute-start | bytes 98312 | tf_op jit(solution)/shard_map/ppermute | solution.py:24
  14.7 2.6 %collective-permute-start.5 = (bf16[32,1536]{1,0:T(8,128)(2,1)S(1)}, bf16[32,1536]{1,0:T(8,128)(2,1)S(1)}, u32[]{:S(2)}, u32[]{:S(2)}) collective-permute-start(bf16[32,1536]{1,0:T(8,128)(2,1)S(1)} %get-tuple-element.28), channel_id=1, source_target_pairs={{0,20},{4,16},{8,28},{12,24},{16,4},{20,0},{24,12},{28,8},{1,21},{... | collective-permute-start | bytes 294920 | tf_op jit(solution)/shard_map/ppermute | solution.py:24
  17.3 0.5 %collective-permute-start.6 = (bf16[32,1536]{1,0:T(8,128)(2,1)S(1)}, bf16[32,1536]{1,0:T(8,128)(2,1)S(1)}, u32[]{:S(2)}, u32[]{:S(2)}) collective-permute-start(bf16[32,1536]{1,0:T(8,128)(2,1)S(1)} %get-tuple-element.29), channel_id=1, source_target_pairs={{0,4},{4,0},{8,12},{12,8},{16,20},{20,16},{24,28},{28,24},{1,5},{5... | collective-permute-start | bytes 294920 | tf_op jit(solution)/shard_map/ppermute | solution.py:24
  17.9 2.3 %collective-permute-start.7 = (bf16[32,1536]{1,0:T(8,128)(2,1)S(1)}, bf16[32,1536]{1,0:T(8,128)(2,1)S(1)}, u32[]{:S(2)}, u32[]{:S(2)}) collective-permute-start(bf16[32,1536]{1,0:T(8,128)(2,1)S(1)} %get-tuple-element.30), channel_id=1, source_target_pairs={{0,12},{4,8},{8,4},{12,0},{16,28},{20,24},{24,20},{28,16},{1,13},{... | collective-permute-start | bytes 294920 | tf_op jit(solution)/shard_map/ppermute | solution.py:24
  20.1 0.0 collective-permute-done.10.refs_1_
  20.1 0.7 %collective-permute-start.8 = (bf16[32,1536]{1,0:T(8,128)(2,1)S(1)}, bf16[32,1536]{1,0:T(8,128)(2,1)S(1)}, u32[]{:S(2)}, u32[]{:S(2)}) collective-permute-start(bf16[32,1536]{1,0:T(8,128)(2,1)S(1)} %get-tuple-element.31), channel_id=1, source_target_pairs={{0,8},{4,12},{8,0},{12,4},{16,24},{20,28},{24,16},{28,20},{1,9},{5... | collective-permute-start | bytes 294920 | tf_op jit(solution)/shard_map/ppermute | solution.py:24
  20.8 0.0 collective-permute-done.11.refs_2_
  20.8 0.9 %collective-permute-start.9 = (bf16[32,1536]{1,0:T(8,128)(2,1)S(1)}, bf16[32,1536]{1,0:T(8,128)(2,1)S(1)}, u32[]{:S(2)}, u32[]{:S(2)}) collective-permute-start(bf16[32,1536]{1,0:T(8,128)(2,1)S(1)} %get-tuple-element.32), channel_id=1, source_target_pairs={{0,28},{4,24},{8,20},{12,16},{16,12},{20,8},{24,4},{28,0},{1,29},{... | collective-permute-start | bytes 294920 | tf_op jit(solution)/shard_map/ppermute | solution.py:24
  21.7 2.3 %collective-permute-done.5.refs_4_.refs_3_ = bf16[32,1536]{1,0:T(8,128)(2,1)S(1)} collective-permute-done((bf16[32,1536]{1,0:T(8,128)(2,1)S(1)}, bf16[32,1536]{1,0:T(8,128)(2,1)S(1)}, u32[]{:S(2)}, u32[]{:S(2)}) %collective-permute-start.5) | collective-permute-done | bytes 98336 | tf_op jit(solution)/shard_map/ppermute | solution.py:24
  24.0 0.0 collective-permute-start.3
  24.0 1.5 %collective-permute-done.6.refs_3_.refs_4_ = bf16[32,1536]{1,0:T(8,128)(2,1)S(1)} collective-permute-done((bf16[32,1536]{1,0:T(8,128)(2,1)S(1)}, bf16[32,1536]{1,0:T(8,128)(2,1)S(1)}, u32[]{:S(2)}, u32[]{:S(2)}) %collective-permute-start.6) | collective-permute-done | bytes 98336 | tf_op jit(solution)/shard_map/ppermute | solution.py:24
  25.5 1.0 %collective-permute-start.4 = (bf16[32,1024]{1,0:T(8,128)(2,1)S(1)}, bf16[32,1024]{1,0:T(8,128)(2,1)S(1)}, u32[]{:S(2)}, u32[]{:S(2)}) collective-permute-start(bf16[32,1024]{1,0:T(8,128)(2,1)S(1)} %get-tuple-element.27), channel_id=1, source_target_pairs={{0,24},{4,28},{8,16},{12,20},{16,8},{20,12},{24,0},{28,4},{1,25},{... | collective-permute-start | bytes 196616 | tf_op jit(solution)/shard_map/ppermute | solution.py:24
  26.5 0.0 collective-permute-done.7.refs_5_
  26.5 2.6 %collective-permute-done.8.refs_6_ = bf16[32,1536]{1,0:T(8,128)(2,1)S(1)} collective-permute-done((bf16[32,1536]{1,0:T(8,128)(2,1)S(1)}, bf16[32,1536]{1,0:T(8,128)(2,1)S(1)}, u32[]{:S(2)}, u32[]{:S(2)}) %collective-permute-start.8) | collective-permute-done | bytes 98336 | tf_op jit(solution)/shard_map/ppermute | solution.py:24
  29.2 0.0 collective-permute-done.9.refs_7_
  29.2 2.0 %separator_fields_and_coupling.1 = (f32[4096,256]{1,0:T(8,128)S(1)}, bf16[256,256]{1,0:T(8,128)(2,1)}) custom-call(bf16[32,1536]{1,0:T(8,128)(2,1)S(1)} %get-tuple-element.25.refs_0_, bf16[32,512]{1,0:T(8,128)(2,1)S(1)} %collective-permute-done.10.refs_1_, bf16[32,512]{1,0:T(8,128)(2,1)S(1)} %collective-permute-done.11.refs_2_, ...), custom_call_target="tpu_custom_call" | custom-call | flops 1610612736 | bytes 6291456 | tf_op jit(solution)/shard_map/separator_fields_and_coupling/pallas_call | solution.py:188
  31.2 0.8 %collective-permute-done.3.refs_1_ = bf16[32,1024]{1,0:T(8,128)(2,1)S(1)} collective-permute-done((bf16[32,1024]{1,0:T(8,128)(2,1)S(1)}, bf16[32,1024]{1,0:T(8,128)(2,1)S(1)}, u32[]{:S(2)}, u32[]{:S(2)}) %collective-permute-start.3) | collective-permute-done | bytes 65568 | tf_op jit(solution)/shard_map/ppermute | solution.py:24
  32.0 0.0 collective-permute-done.4.refs_2_
  32.0 3.4 %interior_field.1 = bf16[4096,256]{1,0:T(8,128)(2,1)} custom-call(bf16[32,1536]{1,0:T(8,128)(2,1)S(1)} %get-tuple-element.25.refs_0_, bf16[32,1024]{1,0:T(8,128)(2,1)S(1)} %collective-permute-done.3.refs_1_, bf16[32,1024]{1,0:T(8,128)(2,1)S(1)} %collective-permute-done.4.refs_2_, bf16[32,1536]{1,0:T(8,128)(2,1)S(1)} %collective-permute-done.5.refs_4_.refs_3_, ...), custom_call_target="tpu_custom_call" | custom-call | tf_op jit(solution)/shard_map/interior_field/pallas_call | solution.py:231
  (3 shorter events, 0.0 us)
Async XLA Ops:
  0.6 4.5 %copy-start.1 = (bf16[4096,768]{1,0:T(8,128)(2,1)S(1)}, bf16[4096,768]{1,0:T(8,128)(2,1)}, u32[]{:S(2)}) copy-start(bf16[4096,768]{1,0:T(8,128)(2,1)} %coupling_ref.1) | copy-start | bytes 18874372
  0.6 4.4 %copy-start.2 = (bf16[2048,128]{1,0:T(8,128)(2,1)S(1)}, bf16[2048,128]{1,0:T(8,128)(2,1)}, u32[]{:S(2)}) copy-start(bf16[2048,128]{1,0:T(8,128)(2,1)} %sep_ref.1) | copy-start | bytes 1572868
  1.9 5.6 %collective-permute-start = (bf16[32,1280]{1,0:T(8,128)(2,1)S(1)}, bf16[32,1280]{1,0:T(8,128)(2,1)S(1)}, u32[]{:S(2)}, u32[]{:S(2)}) collective-permute-start(bf16[32,1280]{1,0:T(8,128)(2,1)S(1)} %get-tuple-element.21), channel_id=1, source_target_pairs={{0,2},{1,3},{2,0},{3,1},{4,6},{5,7},{6,4},{7,5},{8,10},{9,11},{10,... | collective-permute-start | bytes 245768 | tf_op jit(solution)/shard_map/ppermute | solution.py:24
  4.9 4.5 %collective-permute-start.1 = (bf16[32,1280]{1,0:T(8,128)(2,1)S(1)}, bf16[32,1280]{1,0:T(8,128)(2,1)S(1)}, u32[]{:S(2)}, u32[]{:S(2)}) collective-permute-start(bf16[32,1280]{1,0:T(8,128)(2,1)S(1)} %get-tuple-element.22), channel_id=1, source_target_pairs={{0,3},{1,2},{2,1},{3,0},{4,7},{5,6},{6,5},{7,4},{8,11},{9,10},{10,... | collective-permute-start | bytes 245768 | tf_op jit(solution)/shard_map/ppermute | solution.py:24
  4.9 4.5 %collective-permute-start.2 = (bf16[32,1280]{1,0:T(8,128)(2,1)S(1)}, bf16[32,1280]{1,0:T(8,128)(2,1)S(1)}, u32[]{:S(2)}, u32[]{:S(2)}) collective-permute-start(bf16[32,1280]{1,0:T(8,128)(2,1)S(1)} %get-tuple-element.23), channel_id=1, source_target_pairs={{0,1},{1,0},{2,3},{3,2},{4,5},{5,4},{6,7},{7,6},{8,9},{9,8},{10,11... | collective-permute-start | bytes 245768 | tf_op jit(solution)/shard_map/ppermute | solution.py:24
  5.1 26.9 %copy-start = (bf16[4096,1024]{1,0:T(8,128)(2,1)S(1)}, bf16[4096,1024]{1,0:T(8,128)(2,1)}, u32[]{:S(2)}) copy-start(bf16[4096,1024]{1,0:T(8,128)(2,1)} %refs_8_.1) | copy-start | bytes 25165828
  10.5 9.6 %collective-permute-start.10 = (bf16[32,512]{1,0:T(8,128)(2,1)S(1)}, bf16[32,512]{1,0:T(8,128)(2,1)S(1)}, u32[]{:S(2)}, u32[]{:S(2)}) collective-permute-start(bf16[32,512]{1,0:T(8,128)(2,1)S(1)} %get-tuple-element.33), channel_id=1, source_target_pairs={{0,16},{4,20},{8,24},{12,28},{16,0},{20,4},{24,8},{28,12},{1,17},{... | collective-permute-start | bytes 98312 | tf_op jit(solution)/shard_map/ppermute | solution.py:24
  13.4 7.5 %collective-permute-start.11 = (bf16[32,512]{1,0:T(8,128)(2,1)S(1)}, bf16[32,512]{1,0:T(8,128)(2,1)S(1)}, u32[]{:S(2)}, u32[]{:S(2)}) collective-permute-start(bf16[32,512]{1,0:T(8,128)(2,1)S(1)} %get-tuple-element.34), channel_id=1, source_target_pairs={{0,24},{4,28},{8,16},{12,20},{16,8},{20,12},{24,0},{28,4},{1,25},{... | collective-permute-start | bytes 98312 | tf_op jit(solution)/shard_map/ppermute | solution.py:24
  14.7 9.3 %collective-permute-start.5 = (bf16[32,1536]{1,0:T(8,128)(2,1)S(1)}, bf16[32,1536]{1,0:T(8,128)(2,1)S(1)}, u32[]{:S(2)}, u32[]{:S(2)}) collective-permute-start(bf16[32,1536]{1,0:T(8,128)(2,1)S(1)} %get-tuple-element.28), channel_id=1, source_target_pairs={{0,20},{4,16},{8,28},{12,24},{16,4},{20,0},{24,12},{28,8},{1,21},{... | collective-permute-start | bytes 294920 | tf_op jit(solution)/shard_map/ppermute | solution.py:24
  17.3 8.2 %collective-permute-start.6 = (bf16[32,1536]{1,0:T(8,128)(2,1)S(1)}, bf16[32,1536]{1,0:T(8,128)(2,1)S(1)}, u32[]{:S(2)}, u32[]{:S(2)}) collective-permute-start(bf16[32,1536]{1,0:T(8,128)(2,1)S(1)} %get-tuple-element.29), channel_id=1, source_target_pairs={{0,4},{4,0},{8,12},{12,8},{16,20},{20,16},{24,28},{28,24},{1,5},{5... | collective-permute-start | bytes 294920 | tf_op jit(solution)/shard_map/ppermute | solution.py:24
  17.9 8.7 %collective-permute-start.7 = (bf16[32,1536]{1,0:T(8,128)(2,1)S(1)}, bf16[32,1536]{1,0:T(8,128)(2,1)S(1)}, u32[]{:S(2)}, u32[]{:S(2)}) collective-permute-start(bf16[32,1536]{1,0:T(8,128)(2,1)S(1)} %get-tuple-element.30), channel_id=1, source_target_pairs={{0,12},{4,8},{8,4},{12,0},{16,28},{20,24},{24,20},{28,16},{1,13},{... | collective-permute-start | bytes 294920 | tf_op jit(solution)/shard_map/ppermute | solution.py:24
  20.1 9.0 %collective-permute-start.8 = (bf16[32,1536]{1,0:T(8,128)(2,1)S(1)}, bf16[32,1536]{1,0:T(8,128)(2,1)S(1)}, u32[]{:S(2)}, u32[]{:S(2)}) collective-permute-start(bf16[32,1536]{1,0:T(8,128)(2,1)S(1)} %get-tuple-element.31), channel_id=1, source_target_pairs={{0,8},{4,12},{8,0},{12,4},{16,24},{20,28},{24,16},{28,20},{1,9},{5... | collective-permute-start | bytes 294920 | tf_op jit(solution)/shard_map/ppermute | solution.py:24
  20.8 8.4 %collective-permute-start.9 = (bf16[32,1536]{1,0:T(8,128)(2,1)S(1)}, bf16[32,1536]{1,0:T(8,128)(2,1)S(1)}, u32[]{:S(2)}, u32[]{:S(2)}) collective-permute-start(bf16[32,1536]{1,0:T(8,128)(2,1)S(1)} %get-tuple-element.32), channel_id=1, source_target_pairs={{0,28},{4,24},{8,20},{12,16},{16,12},{20,8},{24,4},{28,0},{1,29},{... | collective-permute-start | bytes 294920 | tf_op jit(solution)/shard_map/ppermute | solution.py:24
  24.0 8.0 %collective-permute-start.3 = (bf16[32,1024]{1,0:T(8,128)(2,1)S(1)}, bf16[32,1024]{1,0:T(8,128)(2,1)S(1)}, u32[]{:S(2)}, u32[]{:S(2)}) collective-permute-start(bf16[32,1024]{1,0:T(8,128)(2,1)S(1)} %get-tuple-element.26), channel_id=1, source_target_pairs={{0,16},{4,20},{8,24},{12,28},{16,0},{20,4},{24,8},{28,12},{1,17},{... | collective-permute-start | bytes 196616 | tf_op jit(solution)/shard_map/ppermute | solution.py:24
  25.5 6.5 %collective-permute-start.4 = (bf16[32,1024]{1,0:T(8,128)(2,1)S(1)}, bf16[32,1024]{1,0:T(8,128)(2,1)S(1)}, u32[]{:S(2)}, u32[]{:S(2)}) collective-permute-start(bf16[32,1024]{1,0:T(8,128)(2,1)S(1)} %get-tuple-element.27), channel_id=1, source_target_pairs={{0,24},{4,28},{8,16},{12,20},{16,8},{20,12},{24,0},{28,4},{1,25},{... | collective-permute-start | bytes 196616 | tf_op jit(solution)/shard_map/ppermute | solution.py:24

commit v4 on v3

--- a/solution.py
+++ b/solution.py
@@ -15,7 +15,8 @@
 EARLY_ORDER = [0, 4, 6, 1, 5, 3, 2, 7]
 CUT = (4, 6)
 LATE_ORDER = [0, 4, 6, 5, 1, 3, 2, 7]
-VEC_ORDER = [2, 3, 1, 0]
+PART = 0
+VEC_ORDER = [2, 1, 3, 0]
 AHEAD = 6 << 30
 CONTRACT = (((1,), (1,)), ((), ()))
 
@@ -53,20 +54,21 @@
     )(coefficients)
 
 
-def put_windows(rows_ref, out_ref, count, offset, cap, lane):
+def put_windows(rows_ref, out_ref, count, offset, first, last, lane):
     start = offset // LANES
     shift = offset - start * LANES
     back = lax.rem(LANES - shift, LANES)
     base = pl.multiple_of(start * LANES, LANES)
     keep = lane < LANES - shift
-    pieces = []
-    for j in range(cap // LANES + 1):
+    pieces = {}
+    for j in range(first // LANES, last // LANES + 1):
         piece = rows_ref[:, pl.ds(base + j * LANES, LANES)].astype(jnp.float32)
-        pieces.append(pltpu.roll(piece, back, 1))
-    for j in range(cap // LANES):
+        pieces[j] = pltpu.roll(piece, back, 1)
+    for j in range(first // LANES, last // LANES):
         merged = jnp.where(keep, pieces[j], pieces[j + 1])
         merged = jnp.where(lane + j * LANES < count, merged, 0.0)
-        out_ref[:, j * LANES : (j + 1) * LANES] = merged.astype(rows_ref.dtype)
+        at = j * LANES - first
+        out_ref[:, at : at + LANES] = merged.astype(rows_ref.dtype)
 
 
 def put_separators(from_ref, first, out_ref, to, owner, anc_ref):
@@ -96,13 +98,13 @@
     if rows_ref.shape[1] > total:
         rows_ref[:, total:] = jnp.zeros((slice_cols, rows_ref.shape[1] - total), rows_ref.dtype)
     lane = lax.broadcasted_iota(jnp.int32, (slice_cols, LANES), 1)
-    for out_ref, (turn, has_interior, has_separators) in zip(outs, turns):
+    for out_ref, (turn, first, last, has_separators) in zip(outs, turns):
         owner = jnp.bitwise_xor(sub, turn)
-        if has_interior:
+        if last > first:
             offset = window_start(counts_ref, sub_count, owner)
-            put_windows(rows_ref, out_ref, counts_ref[owner], offset, cap, lane)
+            put_windows(rows_ref, out_ref, counts_ref[owner], offset, first, last, lane)
         if has_separators:
-            put_separators(rows_ref, interior_total, out_ref, cap * has_interior, owner, anc_ref)
+            put_separators(rows_ref, interior_total, out_ref, last - first, owner, anc_ref)
 
 
 def pack(token, chunks, chunk_turns, row_counts, ancestors, cap, turns, direct):
@@ -115,7 +117,7 @@
     smem, vmem = pl.BlockSpec(memory_space=pltpu.SMEM), pl.BlockSpec(memory_space=pltpu.VMEM)
     return pl.pallas_call(
         functools.partial(pack_kernel, interior_total, cap, turns, direct, chunk_turns),
-        out_shape=[jax.ShapeDtypeStruct((slice_cols, cap * a + kept * b), dtype) for _, a, b in turns],
+        out_shape=[jax.ShapeDtypeStruct((slice_cols, b - a + kept * c), dtype) for _, a, b, c in turns],
         in_specs=[smem, smem, pl.BlockSpec(memory_space=pl.ANY)] + [vmem] * len(chunks),
         out_specs=[vmem] * len(turns),
         scratch_shapes=[pltpu.VMEM((slice_cols, max(total, interior_total + cap)), dtype)],
@@ -124,8 +126,11 @@
     )(row_counts, ancestors, token, *chunks)
 
 
-def mask_kernel(anc_ref, pattern_ref, sep_ref, coupling_ref, sep_out, coupling_out):
+def mask_kernel(
+    counts_ref, anc_ref, pattern_ref, sep_ref, coupling_ref, sep_out, coupling_out, count_out
+):
     me = lax.axis_index("sub")
+    count_out[...] = jnp.full(count_out.shape, counts_ref[me], jnp.int32)
     for k in range(LEVELS + 1):
         label = me if k == 0 else anc_ref[k - 1, me]
         at = pl.multiple_of(label * BW, BW)
@@ -138,29 +143,29 @@
             coupling_out[at] = jnp.where(live, part, jnp.zeros_like(part))
 
 
-def mask(ancestors, pattern, separator_modes, coupling):
+def mask(row_counts, ancestors, pattern, separator_modes, coupling):
     smem, vmem = pl.BlockSpec(memory_space=pltpu.SMEM), pl.BlockSpec(memory_space=pltpu.VMEM)
     return pl.pallas_call(
         mask_kernel,
         out_shape=(
             pltpu.VMEM(((LEVELS + 1) * BW, SEPM), coupling.dtype),
             pltpu.VMEM(coupling.shape, coupling.dtype),
+            pltpu.VMEM((8, LANES), jnp.int32),
         ),
-        in_specs=[smem, smem, vmem, vmem],
-        out_specs=(vmem, vmem),
+        in_specs=[smem, smem, smem, vmem, vmem],
+        out_specs=(vmem, vmem, vmem),
         compiler_params=pltpu.CompilerParams(vmem_limit_bytes=4 << 20),
         cost_estimate=pl.CostEstimate(flops=0, transcendentals=0, bytes_accessed=2 * coupling.size),
         name="mask_coupling",
-    )(ancestors, pattern, separator_modes, coupling)
+    )(row_counts, ancestors, pattern, separator_modes, coupling)
 
 
 def gather_rows(places, slots, got_ref):
-    width = got_ref.shape[1]
-    for n, lanes, turn in places:
+    for n, lanes, first, last, turn in places:
         slice_cols = slots[n].shape[0]
         block = 0 if turn is None else jnp.bitwise_xor(lax.axis_index("sub"), turn)
         at = pl.multiple_of(block * slice_cols, slice_cols)
-        got_ref[pl.ds(at, slice_cols), :] = slots[n][:, lanes : lanes + width]
+        got_ref[pl.ds(at, slice_cols), first:last] = slots[n][:, lanes : lanes + last - first]
 
 
 def above_kernel(rows, places, slot_count, *refs):
@@ -207,31 +212,39 @@
 
 def interior_kernel(rows, places, slot_count, *refs):
     slots, refs = refs[:slot_count], refs[slot_count:]
-    modes_ref, total_ref, field_ref, got_ref, coef_ref, block_ref, sems = refs
+    count_ref, modes_ref, total_ref, field_ref, got_ref, coef_ref, block_ref, sems = refs
+    phys, cap = modes_ref.shape
+    tiles = (jnp.max(count_ref[...]) + BW - 1) // BW
     gather_rows(places, slots, got_ref)
-    coef_ref[...] = got_ref[...].T
-    copies = []
-    for s in range(modes_ref.shape[0] // rows):
-        at = slice(s * rows, (s + 1) * rows)
-        acc = jnp.dot(modes_ref[at, :], coef_ref[...], preferred_element_type=jnp.float32)
-        block_ref[at, :] = (acc + total_ref[at, :]).astype(block_ref.dtype)
-        copy = pltpu.make_async_copy(
-            block_ref.at[pl.ds(s * rows, rows)], field_ref.at[pl.ds(s * rows, rows)], sems.at[s]
-        )
-        copy.start()
-        copies.append(copy)
+    copies = [
+        pltpu.make_async_copy(block_ref.at[pl.ds(at, rows)], field_ref.at[pl.ds(at, rows)], sems.at[n])
+        for n, at in enumerate(range(0, phys, rows))
+    ]
+    for used in range(1, cap // BW + 1):
+
+        @pl.when(tiles == used)
+        def _(depth=used * BW):
+            coef_ref[:depth, :] = got_ref[:, :depth].T
+            for n, first in enumerate(range(0, phys, rows)):
+                at = slice(first, first + rows)
+                acc = jnp.dot(
+                    modes_ref[at, :depth], coef_ref[:depth, :], preferred_element_type=jnp.float32
+                )
+                block_ref[at, :] = (acc + total_ref[at, :]).astype(block_ref.dtype)
+                copies[n].start()
+
     for copy in copies:
         copy.wait()
 
 
-def interior(slots, places, group, modes, total):
+def interior(slots, places, group, count, modes, total):
     phys, cap = modes.shape
     rows = 2 * BW
     vmem = pl.BlockSpec(memory_space=pltpu.VMEM)
     return pl.pallas_call(
         functools.partial(interior_kernel, rows, places, len(slots)),
         out_shape=jax.ShapeDtypeStruct((phys, group), jnp.bfloat16),
-        in_specs=[vmem] * (len(slots) + 2),
+        in_specs=[vmem] * (len(slots) + 3),
         out_specs=pl.BlockSpec(memory_space=pl.ANY),
         scratch_shapes=[
             pltpu.VMEM((group, cap), jnp.bfloat16),
@@ -241,7 +254,7 @@
         ],
         compiler_params=pltpu.CompilerParams(vmem_limit_bytes=8 << 20),
         name="interior_field",
-    )(*slots, modes, total)
+    )(*slots, count, modes, total)
 
 
 def in_hbm(array):
@@ -261,7 +274,7 @@
     counts = in_hbm(row_counts)
     above = in_hbm(ancestors.T)
     gates = in_hbm(jnp.transpose(pattern, (2, 0, 1)))
-    sep, masked = mask(above, gates, separator_modes, coupling)
+    sep, masked, count = mask(counts, above, gates, separator_modes, coupling)
     powers = vec_count & (vec_count - 1) == 0 and sub_count & (sub_count - 1) == 0
     if powers and sub_count > 1 and slice_cols % ROWS == 0:
         blocks = split(in_hbm(coefficients), vec_count)
@@ -269,25 +282,26 @@
         chunks = [turn_over(blocks[k], "vec", vec_count, k) if k else blocks[0] for k in chunk_turns]
         turns = []
         for k in turn_order(sub_count, EARLY_ORDER):
-            turns += [(k, 0, 1), (k, 1, 0)] if k in CUT else [(k, 1, 1)]
+            part = min(PART, cap)
+            turns += [(k, 0, part, 1), (k, part, cap, 0)] if k in CUT else [(k, 0, cap, 1)]
         packed = pack(sep, chunks, chunk_turns, counts, above, cap, turns, True)
         slots = [turn_over(p, "sub", sub_count, t[0]) if t[0] else p for p, t in zip(packed, turns)]
-        early = [n for n in range(len(turns)) if turns[n][2]]
-        late = [n for n in range(len(turns)) if turns[n][1]]
+        early = [n for n in range(len(turns)) if turns[n][3]]
+        late = [n for n in range(len(turns)) if turns[n][2] > turns[n][1]]
         late.sort(key=lambda n: turn_order(sub_count, LATE_ORDER).index(turns[n][0]))
-        above_places = [(i, cap * turns[n][1], turns[n][0]) for i, n in enumerate(early)]
-        places = [(i, 0, turns[n][0]) for i, n in enumerate(late)]
+        above_places = [(i, turns[n][2] - turns[n][1], 0, kept, turns[n][0]) for i, n in enumerate(early)]
+        places = [(i, 0, turns[n][1], turns[n][2], turns[n][0]) for i, n in enumerate(late)]
         early, late = [slots[n] for n in early], [slots[n] for n in late]
     else:
         regrouped = coefficients.reshape(vec_count, slice_cols, coefficients.shape[1])
         regrouped = lax.all_to_all(regrouped, "vec", split_axis=0, concat_axis=0, tiled=True)
-        turns = [(k, 1, 1) for k in range(sub_count)]
+        turns = [(k, 0, cap, 1) for k in range(sub_count)]
         slots = pack(sep, list(regrouped), list(range(vec_count)), counts, above, cap, turns, False)
         slots = lax.all_to_all(jnp.stack(slots), "sub", split_axis=0, concat_axis=0, tiled=True)
         early = late = [slots.reshape(group, cap + kept)]
-        above_places, places = [(0, cap, None)], [(0, 0, None)]
+        above_places, places = [(0, cap, 0, kept, None)], [(0, 0, 0, cap, None)]
     total, own = above_fields(early, above_places, group, sep, masked)
-    return interior(late, places, group, interior_modes, total), own
+    return interior(late, places, group, count, interior_modes, total), own
 
 
 def solution(mesh):

time: 35.6 us -> 35.4 us (level)
  Pallas kernels: 9.43 us -> 9.07 us
    pallas_call x1, Pallas kernels: 3.39 us -> 3.01 us  [interior(): pl.pallas_call(functools.partial(interior_kernel, rows, places, len(slots...]
  transfers between devices with their start and end apart: 12 -> 12, of which waited for: 6 -> 6; matrix products, arithmetic and copies ran while one was open for 0% -> 0% of each run, Pallas kernels for 10% -> 11%
where the time goes in v4:
time: 35.4 us; the launch traced here: 35 us
  starting transfers between devices  15.2 us (43%)
  waiting for transfers between devices  10 us (28%)
  Pallas kernels  9.07 us (26%)
  between operations  0.69 us (2%)
    ppermute x12, starting transfers between devices, turn_over(): return lax.ppermute(block, axis, [(i, i ^ turn) for i in range(count)])  15.2 us
    ppermute x12, waiting for transfers between devices, turn_over(): return lax.ppermute(block, axis, [(i, i ^ turn) for i in range(count)])  10 us
    pallas_call x1, Pallas kernels, interior(): pl.pallas_call(functools.partial(interior_kernel, rows, places, len(slots...  3.01 us
    pallas_call x1, Pallas kernels, above_fields(): pl.pallas_call(functools.partial(above_kernel, 2 * BW, places, len(slots)...  2.03 us
    pallas_call x1, Pallas kernels, mask(): pl.pallas_call(mask_kernel, out_shape=(pltpu.VMEM(((LEVELS + 1) * BW, SEP...  1.7 us
    pallas_call x1, Pallas kernels, split(): pl.pallas_call(split_kernel, out_shape=[jax.ShapeDtypeStruct(shape, coeff...  1.2 us
    pallas_call x1, Pallas kernels, pack(): pl.pallas_call(functools.partial(pack_kernel, interior_total, cap, turns,...  1.13 us
  transfers between devices with their start and end apart: 12, of which 6 were waited for; matrix products, arithmetic and copies ran while one was open for 0% of the time, Pallas kernels for 11%

profile of v4, /device:TPU:0, one launch (start us, length us, event | category | flops | bytes accessed | tf_op | source)
XLA Modules:
  0.0 35.0 jit_solution(14603332344733431601)
XLA Ops:
  0.6 0.0 copy-start.1
  0.6 1.2 %split_slices.1 = (bf16[32,1280]{1,0:T(8,128)(2,1)S(1)}, bf16[32,1280]{1,0:T(8,128)(2,1)S(1)}, bf16[32,1280]{1,0:T(8,128)(2,1)S(1)}, bf16[32,1280]{1,0:T(8,128)(2,1)S(1)}) custom-call(bf16[128,1280]{1,0:T(8,128)(2,1)} %coef_ref.1), custom_call_target="tpu_custom_call" | custom-call | flops 6442450944 | bytes 1048576 | tf_op jit(solution)/shard_map/split_slices/pallas_call | solution.py:45
  1.9 3.0 %collective-permute-start = (bf16[32,1280]{1,0:T(8,128)(2,1)S(1)}, bf16[32,1280]{1,0:T(8,128)(2,1)S(1)}, u32[]{:S(2)}, u32[]{:S(2)}) collective-permute-start(bf16[32,1280]{1,0:T(8,128)(2,1)S(1)} %get-tuple-element.22), channel_id=1, source_target_pairs={{0,2},{1,3},{2,0},{3,1},{4,6},{5,7},{6,4},{7,5},{8,10},{9,11},{10,... | collective-permute-start | bytes 245768 | tf_op jit(solution)/shard_map/ppermute | solution.py:25
  4.9 0.0 collective-permute-start.1
  4.9 0.2 collective-permute-start.2
  5.1 0.0 copy-done.2
  5.1 1.7 %mask_coupling.1 = (bf16[1024,128]{1,0:T(8,128)(2,1)S(1)}, bf16[4096,768]{1,0:T(8,128)(2,1)S(1)}, s32[8,128]{1,0:T(8,128)S(1)}) custom-call(s32[8]{0:T(128)} %counts_ref.3, s32[3,8]{1,0:T(4,128)} %bitcast.2, s32[3,1,16]{2,1,0:T(1,128)} %bitcast.4, bf16[2048,128]{1,0:T(8,128)(2,1)S(1)} %copy-done.2, bf16[4096,768]{1,0:T(8,128)(2,1)S(1)} %copy-done.1), custom_call_target="tpu_custom_call" | custom-call | bytes 6291456 | tf_op jit(solution)/shard_map/mask_coupling/pallas_call | solution.py:148
  6.8 0.7 %collective-permute-done.refs_1_ = bf16[32,1280]{1,0:T(8,128)(2,1)S(1)} collective-permute-done((bf16[32,1280]{1,0:T(8,128)(2,1)S(1)}, bf16[32,1280]{1,0:T(8,128)(2,1)S(1)}, u32[]{:S(2)}, u32[]{:S(2)}) %collective-permute-start) | collective-permute-done | bytes 81952 | tf_op jit(solution)/shard_map/ppermute | solution.py:25
  7.6 0.0 collective-permute-done.1.refs_2_
  7.6 1.4 %collective-permute-done.2.refs_3_ = bf16[32,1280]{1,0:T(8,128)(2,1)S(1)} collective-permute-done((bf16[32,1280]{1,0:T(8,128)(2,1)S(1)}, bf16[32,1280]{1,0:T(8,128)(2,1)S(1)}, u32[]{:S(2)}, u32[]{:S(2)}) %collective-permute-start.2) | collective-permute-done | bytes 81952 | tf_op jit(solution)/shard_map/ppermute | solution.py:25
  9.0 1.1 %pack_windows.1 = (bf16[32,1536]{1,0:T(8,128)(2,1)S(1)}, bf16[32,512]{1,0:T(8,128)(2,1)S(1)}, bf16[32,1024]{1,0:T(8,128)(2,1)S(1)}, bf16[32,512]{1,0:T(8,128)(2,...) custom-call(s32[8]{0:T(128)} %counts_ref.3, ...), custom_call_target="tpu_custom_call" | custom-call | tf_op jit(solution)/shard_map/pack_windows/pallas_call | solution.py:118
  10.1 2.7 %collective-permute-start.10 = (bf16[32,512]{1,0:T(8,128)(2,1)S(1)}, bf16[32,512]{1,0:T(8,128)(2,1)S(1)}, u32[]{:S(2)}, u32[]{:S(2)}) collective-permute-start(bf16[32,512]{1,0:T(8,128)(2,1)S(1)} %get-tuple-element.35), channel_id=1, source_target_pairs={{0,16},{4,20},{8,24},{12,28},{16,0},{20,4},{24,8},{28,12},{1,17},{... | collective-permute-start | bytes 98312 | tf_op jit(solution)/shard_map/ppermute | solution.py:25
  12.8 1.3 %collective-permute-start.11 = (bf16[32,512]{1,0:T(8,128)(2,1)S(1)}, bf16[32,512]{1,0:T(8,128)(2,1)S(1)}, u32[]{:S(2)}, u32[]{:S(2)}) collective-permute-start(bf16[32,512]{1,0:T(8,128)(2,1)S(1)} %get-tuple-element.36), channel_id=1, source_target_pairs={{0,24},{4,28},{8,16},{12,20},{16,8},{20,12},{24,0},{28,4},{1,25},{... | collective-permute-start | bytes 98312 | tf_op jit(solution)/shard_map/ppermute | solution.py:25
  14.1 2.6 %collective-permute-start.5 = (bf16[32,1536]{1,0:T(8,128)(2,1)S(1)}, bf16[32,1536]{1,0:T(8,128)(2,1)S(1)}, u32[]{:S(2)}, u32[]{:S(2)}) collective-permute-start(bf16[32,1536]{1,0:T(8,128)(2,1)S(1)} %get-tuple-element.29), channel_id=1, source_target_pairs={{0,20},{4,16},{8,28},{12,24},{16,4},{20,0},{24,12},{28,8},{1,21},{... | collective-permute-start | bytes 294920 | tf_op jit(solution)/shard_map/ppermute | solution.py:25
  16.7 0.5 %collective-permute-start.6 = (bf16[32,1536]{1,0:T(8,128)(2,1)S(1)}, bf16[32,1536]{1,0:T(8,128)(2,1)S(1)}, u32[]{:S(2)}, u32[]{:S(2)}) collective-permute-start(bf16[32,1536]{1,0:T(8,128)(2,1)S(1)} %get-tuple-element.30), channel_id=1, source_target_pairs={{0,4},{4,0},{8,12},{12,8},{16,20},{20,16},{24,28},{28,24},{1,5},{5... | collective-permute-start | bytes 294920 | tf_op jit(solution)/shard_map/ppermute | solution.py:25
  17.3 2.3 %collective-permute-start.7 = (bf16[32,1536]{1,0:T(8,128)(2,1)S(1)}, bf16[32,1536]{1,0:T(8,128)(2,1)S(1)}, u32[]{:S(2)}, u32[]{:S(2)}) collective-permute-start(bf16[32,1536]{1,0:T(8,128)(2,1)S(1)} %get-tuple-element.31), channel_id=1, source_target_pairs={{0,12},{4,8},{8,4},{12,0},{16,28},{20,24},{24,20},{28,16},{1,13},{... | collective-permute-start | bytes 294920 | tf_op jit(solution)/shard_map/ppermute | solution.py:25
  19.6 0.0 collective-permute-done.10.refs_1_
  19.6 0.7 %collective-permute-start.8 = (bf16[32,1536]{1,0:T(8,128)(2,1)S(1)}, bf16[32,1536]{1,0:T(8,128)(2,1)S(1)}, u32[]{:S(2)}, u32[]{:S(2)}) collective-permute-start(bf16[32,1536]{1,0:T(8,128)(2,1)S(1)} %get-tuple-element.32), channel_id=1, source_target_pairs={{0,8},{4,12},{8,0},{12,4},{16,24},{20,28},{24,16},{28,20},{1,9},{5... | collective-permute-start | bytes 294920 | tf_op jit(solution)/shard_map/ppermute | solution.py:25
  20.2 0.0 collective-permute-done.11.refs_2_
  20.2 0.9 %collective-permute-start.9 = (bf16[32,1536]{1,0:T(8,128)(2,1)S(1)}, bf16[32,1536]{1,0:T(8,128)(2,1)S(1)}, u32[]{:S(2)}, u32[]{:S(2)}) collective-permute-start(bf16[32,1536]{1,0:T(8,128)(2,1)S(1)} %get-tuple-element.33), channel_id=1, source_target_pairs={{0,28},{4,24},{8,20},{12,16},{16,12},{20,8},{24,4},{28,0},{1,29},{... | collective-permute-start | bytes 294920 | tf_op jit(solution)/shard_map/ppermute | solution.py:25
  21.1 2.6 %collective-permute-done.5.refs_4_.refs_3_ = bf16[32,1536]{1,0:T(8,128)(2,1)S(1)} collective-permute-done((bf16[32,1536]{1,0:T(8,128)(2,1)S(1)}, bf16[32,1536]{1,0:T(8,128)(2,1)S(1)}, u32[]{:S(2)}, u32[]{:S(2)}) %collective-permute-start.5) | collective-permute-done | bytes 98336 | tf_op jit(solution)/shard_map/ppermute | solution.py:25
  23.8 0.0 collective-permute-start.3
  23.8 1.9 %collective-permute-done.6.refs_3_.refs_4_ = bf16[32,1536]{1,0:T(8,128)(2,1)S(1)} collective-permute-done((bf16[32,1536]{1,0:T(8,128)(2,1)S(1)}, bf16[32,1536]{1,0:T(8,128)(2,1)S(1)}, u32[]{:S(2)}, u32[]{:S(2)}) %collective-permute-start.6) | collective-permute-done | bytes 98336 | tf_op jit(solution)/shard_map/ppermute | solution.py:25
  25.6 1.0 %collective-permute-start.4 = (bf16[32,1024]{1,0:T(8,128)(2,1)S(1)}, bf16[32,1024]{1,0:T(8,128)(2,1)S(1)}, u32[]{:S(2)}, u32[]{:S(2)}) collective-permute-start(bf16[32,1024]{1,0:T(8,128)(2,1)S(1)} %get-tuple-element.28), channel_id=1, source_target_pairs={{0,24},{4,28},{8,16},{12,20},{16,8},{20,12},{24,0},{28,4},{1,25},{... | collective-permute-start | bytes 196616 | tf_op jit(solution)/shard_map/ppermute | solution.py:25
  26.6 0.0 collective-permute-done.7.refs_5_
  26.6 2.6 %collective-permute-done.8.refs_6_ = bf16[32,1536]{1,0:T(8,128)(2,1)S(1)} collective-permute-done((bf16[32,1536]{1,0:T(8,128)(2,1)S(1)}, bf16[32,1536]{1,0:T(8,128)(2,1)S(1)}, u32[]{:S(2)}, u32[]{:S(2)}) %collective-permute-start.8) | collective-permute-done | bytes 98336 | tf_op jit(solution)/shard_map/ppermute | solution.py:25
  29.2 0.0 collective-permute-done.9.refs_7_
  29.2 2.0 %separator_fields_and_coupling.1 = (f32[4096,256]{1,0:T(8,128)S(1)}, bf16[256,256]{1,0:T(8,128)(2,1)}) custom-call(bf16[32,1536]{1,0:T(8,128)(2,1)S(1)} %get-tuple-element.26.refs_0_, bf16[32,512]{1,0:T(8,128)(2,1)S(1)} %collective-permute-done.10.refs_1_, bf16[32,512]{1,0:T(8,128)(2,1)S(1)} %collective-permute-done.11.refs_2_, ...), custom_call_target="tpu_custom_call" | custom-call | flops 1610612736 | bytes 6291456 | tf_op jit(solution)/shard_map/separator_fields_and_coupling/pallas_call | solution.py:193
  31.3 0.7 %collective-permute-done.3.refs_1_ = bf16[32,1024]{1,0:T(8,128)(2,1)S(1)} collective-permute-done((bf16[32,1024]{1,0:T(8,128)(2,1)S(1)}, bf16[32,1024]{1,0:T(8,128)(2,1)S(1)}, u32[]{:S(2)}, u32[]{:S(2)}) %collective-permute-start.3) | collective-permute-done | bytes 65568 | tf_op jit(solution)/shard_map/ppermute | solution.py:25
  32.0 0.0 collective-permute-done.4.refs_2_
  32.0 0.0 copy-done
  32.0 3.0 %interior_field.1 = bf16[4096,256]{1,0:T(8,128)(2,1)} custom-call(bf16[32,1536]{1,0:T(8,128)(2,1)S(1)} %get-tuple-element.26.refs_0_, bf16[32,1024]{1,0:T(8,128)(2,1)S(1)} %collective-permute-done.3.refs_1_, bf16[32,1024]{1,0:T(8,128)(2,1)S(1)} %collective-permute-done.4.refs_2_, bf16[32,1536]{1,0:T(8,128)(2,1)S(1)} %collective-permute-done.5.refs_4_.refs_3_, ...), custom_call_target="tpu_custom_call" | custom-call | tf_op jit(solution)/shard_map/interior_field/pallas_call | solution.py:244
  (3 shorter events, 0.0 us)
Async XLA Ops:
  0.6 4.5 %copy-start.1 = (bf16[4096,768]{1,0:T(8,128)(2,1)S(1)}, bf16[4096,768]{1,0:T(8,128)(2,1)}, u32[]{:S(2)}) copy-start(bf16[4096,768]{1,0:T(8,128)(2,1)} %coupling_ref.1) | copy-start | bytes 18874372
  0.6 4.5 %copy-start.2 = (bf16[2048,128]{1,0:T(8,128)(2,1)S(1)}, bf16[2048,128]{1,0:T(8,128)(2,1)}, u32[]{:S(2)}) copy-start(bf16[2048,128]{1,0:T(8,128)(2,1)} %sep_ref.1) | copy-start | bytes 1572868
  1.9 5.7 %collective-permute-start = (bf16[32,1280]{1,0:T(8,128)(2,1)S(1)}, bf16[32,1280]{1,0:T(8,128)(2,1)S(1)}, u32[]{:S(2)}, u32[]{:S(2)}) collective-permute-start(bf16[32,1280]{1,0:T(8,128)(2,1)S(1)} %get-tuple-element.22), channel_id=1, source_target_pairs={{0,2},{1,3},{2,0},{3,1},{4,6},{5,7},{6,4},{7,5},{8,10},{9,11},{10,... | collective-permute-start | bytes 245768 | tf_op jit(solution)/shard_map/ppermute | solution.py:25
  4.9 2.7 %collective-permute-start.1 = (bf16[32,1280]{1,0:T(8,128)(2,1)S(1)}, bf16[32,1280]{1,0:T(8,128)(2,1)S(1)}, u32[]{:S(2)}, u32[]{:S(2)}) collective-permute-start(bf16[32,1280]{1,0:T(8,128)(2,1)S(1)} %get-tuple-element.23), channel_id=1, source_target_pairs={{0,1},{1,0},{2,3},{3,2},{4,5},{5,4},{6,7},{7,6},{8,9},{9,8},{10,11... | collective-permute-start | bytes 245768 | tf_op jit(solution)/shard_map/ppermute | solution.py:25
  4.9 4.1 %collective-permute-start.2 = (bf16[32,1280]{1,0:T(8,128)(2,1)S(1)}, bf16[32,1280]{1,0:T(8,128)(2,1)S(1)}, u32[]{:S(2)}, u32[]{:S(2)}) collective-permute-start(bf16[32,1280]{1,0:T(8,128)(2,1)S(1)} %get-tuple-element.24), channel_id=1, source_target_pairs={{0,3},{1,2},{2,1},{3,0},{4,7},{5,6},{6,5},{7,4},{8,11},{9,10},{10,... | collective-permute-start | bytes 245768 | tf_op jit(solution)/shard_map/ppermute | solution.py:25
  5.1 26.9 %copy-start = (bf16[4096,1024]{1,0:T(8,128)(2,1)S(1)}, bf16[4096,1024]{1,0:T(8,128)(2,1)}, u32[]{:S(2)}) copy-start(bf16[4096,1024]{1,0:T(8,128)(2,1)} %refs_9_.1) | copy-start | bytes 25165828
  10.1 9.4 %collective-permute-start.10 = (bf16[32,512]{1,0:T(8,128)(2,1)S(1)}, bf16[32,512]{1,0:T(8,128)(2,1)S(1)}, u32[]{:S(2)}, u32[]{:S(2)}) collective-permute-start(bf16[32,512]{1,0:T(8,128)(2,1)S(1)} %get-tuple-element.35), channel_id=1, source_target_pairs={{0,16},{4,20},{8,24},{12,28},{16,0},{20,4},{24,8},{28,12},{1,17},{... | collective-permute-start | bytes 98312 | tf_op jit(solution)/shard_map/ppermute | solution.py:25
  12.8 7.5 %collective-permute-start.11 = (bf16[32,512]{1,0:T(8,128)(2,1)S(1)}, bf16[32,512]{1,0:T(8,128)(2,1)S(1)}, u32[]{:S(2)}, u32[]{:S(2)}) collective-permute-start(bf16[32,512]{1,0:T(8,128)(2,1)S(1)} %get-tuple-element.36), channel_id=1, source_target_pairs={{0,24},{4,28},{8,16},{12,20},{16,8},{20,12},{24,0},{28,4},{1,25},{... | collective-permute-start | bytes 98312 | tf_op jit(solution)/shard_map/ppermute | solution.py:25
  14.1 9.6 %collective-permute-start.5 = (bf16[32,1536]{1,0:T(8,128)(2,1)S(1)}, bf16[32,1536]{1,0:T(8,128)(2,1)S(1)}, u32[]{:S(2)}, u32[]{:S(2)}) collective-permute-start(bf16[32,1536]{1,0:T(8,128)(2,1)S(1)} %get-tuple-element.29), channel_id=1, source_target_pairs={{0,20},{4,16},{8,28},{12,24},{16,4},{20,0},{24,12},{28,8},{1,21},{... | collective-permute-start | bytes 294920 | tf_op jit(solution)/shard_map/ppermute | solution.py:25
  16.7 8.9 %collective-permute-start.6 = (bf16[32,1536]{1,0:T(8,128)(2,1)S(1)}, bf16[32,1536]{1,0:T(8,128)(2,1)S(1)}, u32[]{:S(2)}, u32[]{:S(2)}) collective-permute-start(bf16[32,1536]{1,0:T(8,128)(2,1)S(1)} %get-tuple-element.30), channel_id=1, source_target_pairs={{0,4},{4,0},{8,12},{12,8},{16,20},{20,16},{24,28},{28,24},{1,5},{5... | collective-permute-start | bytes 294920 | tf_op jit(solution)/shard_map/ppermute | solution.py:25
  17.3 9.3 %collective-permute-start.7 = (bf16[32,1536]{1,0:T(8,128)(2,1)S(1)}, bf16[32,1536]{1,0:T(8,128)(2,1)S(1)}, u32[]{:S(2)}, u32[]{:S(2)}) collective-permute-start(bf16[32,1536]{1,0:T(8,128)(2,1)S(1)} %get-tuple-element.31), channel_id=1, source_target_pairs={{0,12},{4,8},{8,4},{12,0},{16,28},{20,24},{24,20},{28,16},{1,13},{... | collective-permute-start | bytes 294920 | tf_op jit(solution)/shard_map/ppermute | solution.py:25
  19.6 9.7 %collective-permute-start.8 = (bf16[32,1536]{1,0:T(8,128)(2,1)S(1)}, bf16[32,1536]{1,0:T(8,128)(2,1)S(1)}, u32[]{:S(2)}, u32[]{:S(2)}) collective-permute-start(bf16[32,1536]{1,0:T(8,128)(2,1)S(1)} %get-tuple-element.32), channel_id=1, source_target_pairs={{0,8},{4,12},{8,0},{12,4},{16,24},{20,28},{24,16},{28,20},{1,9},{5... | collective-permute-start | bytes 294920 | tf_op jit(solution)/shard_map/ppermute | solution.py:25
  20.2 9.0 %collective-permute-start.9 = (bf16[32,1536]{1,0:T(8,128)(2,1)S(1)}, bf16[32,1536]{1,0:T(8,128)(2,1)S(1)}, u32[]{:S(2)}, u32[]{:S(2)}) collective-permute-start(bf16[32,1536]{1,0:T(8,128)(2,1)S(1)} %get-tuple-element.33), channel_id=1, source_target_pairs={{0,28},{4,24},{8,20},{12,16},{16,12},{20,8},{24,4},{28,0},{1,29},{... | collective-permute-start | bytes 294920 | tf_op jit(solution)/shard_map/ppermute | solution.py:25
  23.8 8.2 %collective-permute-start.3 = (bf16[32,1024]{1,0:T(8,128)(2,1)S(1)}, bf16[32,1024]{1,0:T(8,128)(2,1)S(1)}, u32[]{:S(2)}, u32[]{:S(2)}) collective-permute-start(bf16[32,1024]{1,0:T(8,128)(2,1)S(1)} %get-tuple-element.27), channel_id=1, source_target_pairs={{0,16},{4,20},{8,24},{12,28},{16,0},{20,4},{24,8},{28,12},{1,17},{... | collective-permute-start | bytes 196616 | tf_op jit(solution)/shard_map/ppermute | solution.py:25
  25.6 6.3 %collective-permute-start.4 = (bf16[32,1024]{1,0:T(8,128)(2,1)S(1)}, bf16[32,1024]{1,0:T(8,128)(2,1)S(1)}, u32[]{:S(2)}, u32[]{:S(2)}) collective-permute-start(bf16[32,1024]{1,0:T(8,128)(2,1)S(1)} %get-tuple-element.28), channel_id=1, source_target_pairs={{0,24},{4,28},{8,16},{12,20},{16,8},{20,12},{24,0},{28,4},{1,25},{... | collective-permute-start | bytes 196616 | tf_op jit(solution)/shard_map/ppermute | solution.py:25

commit v5 on v4

--- a/solution.py
+++ b/solution.py
@@ -12,10 +12,10 @@
 LEVELS = 3
 LANES = 128
 ROWS = 16
-EARLY_ORDER = [0, 4, 6, 1, 5, 3, 2, 7]
+EARLY_ORDER = [0, 4, 3, 1, 2, 6, 5, 7]
 CUT = (4, 6)
-LATE_ORDER = [0, 4, 6, 5, 1, 3, 2, 7]
-PART = 0
+LATE_ORDER = [0, 4, 5, 6, 1, 3, 2, 7]
+PART = 128
 VEC_ORDER = [2, 1, 3, 0]
 AHEAD = 6 << 30
 CONTRACT = (((1,), (1,)), ((), ()))
@@ -214,7 +214,7 @@
     slots, refs = refs[:slot_count], refs[slot_count:]
     count_ref, modes_ref, total_ref, field_ref, got_ref, coef_ref, block_ref, sems = refs
     phys, cap = modes_ref.shape
-    tiles = (jnp.max(count_ref[...]) + BW - 1) // BW
+    tiles = jnp.clip((jnp.max(count_ref[...]) + BW - 1) // BW, 1, cap // BW)
     gather_rows(places, slots, got_ref)
     copies = [
         pltpu.make_async_copy(block_ref.at[pl.ds(at, rows)], field_ref.at[pl.ds(at, rows)], sems.at[n])

time: 35.4 us -> 35 us (0.989); the launches traced: 35 us -> 35.4 us
  waiting for transfers between devices: 10 us -> 6.45 us
  starting transfers between devices: 15.2 us -> 18.6 us
  Pallas kernels: 9.07 us -> 9.62 us
    ppermute x12, waiting for transfers between devices: 10 us -> 6.45 us  [turn_over(): return lax.ppermute(block, axis, [(i, i ^ turn) for i in range(count)])]
    ppermute x12, starting transfers between devices: 15.2 us -> 18.6 us  [turn_over(): return lax.ppermute(block, axis, [(i, i ^ turn) for i in range(count)])]
    pallas_call x1, Pallas kernels: 3.01 us -> 3.56 us  [interior(): pl.pallas_call(functools.partial(interior_kernel, rows, places, len(slots...]
where the time goes in v5:
time: 35 us; the launch traced here: 35.4 us
  starting transfers between devices  18.6 us (53%)
  Pallas kernels  9.62 us (27%)
  waiting for transfers between devices  6.45 us (18%)
  between operations  0.69 us (2%)
    ppermute x12, starting transfers between devices, turn_over(): return lax.ppermute(block, axis, [(i, i ^ turn) for i in range(count)])  18.6 us
    ppermute x12, waiting for transfers between devices, turn_over(): return lax.ppermute(block, axis, [(i, i ^ turn) for i in range(count)])  6.45 us
    pallas_call x1, Pallas kernels, interior(): pl.pallas_call(functools.partial(interior_kernel, rows, places, len(slots...  3.56 us
    pallas_call x1, Pallas kernels, above_fields(): pl.pallas_call(functools.partial(above_kernel, 2 * BW, places, len(slots)...  2.02 us
    pallas_call x1, Pallas kernels, mask(): pl.pallas_call(mask_kernel, out_shape=(pltpu.VMEM(((LEVELS + 1) * BW, SEP...  1.7 us
    pallas_call x1, Pallas kernels, split(): pl.pallas_call(split_kernel, out_shape=[jax.ShapeDtypeStruct(shape, coeff...  1.2 us
    pallas_call x1, Pallas kernels, pack(): pl.pallas_call(functools.partial(pack_kernel, interior_total, cap, turns,...  1.13 us
  transfers between devices with their start and end apart: 12, of which 6 were waited for; matrix products, arithmetic and copies ran while one was open for 0% of the time, Pallas kernels for 11%

profile of v5, /device:TPU:0, one launch (start us, length us, event | category | flops | bytes accessed | tf_op | source)
XLA Modules:
  0.0 35.4 jit_solution(18090687766404296745)
XLA Ops:
  0.6 0.0 copy-start.1
  0.6 0.0 copy-start.2
  0.6 1.2 %split_slices.1 = (bf16[32,1280]{1,0:T(8,128)(2,1)S(1)}, bf16[32,1280]{1,0:T(8,128)(2,1)S(1)}, bf16[32,1280]{1,0:T(8,128)(2,1)S(1)}, bf16[32,1280]{1,0:T(8,128)(2,1)S(1)}) custom-call(bf16[128,1280]{1,0:T(8,128)(2,1)} %coef_ref.1), custom_call_target="tpu_custom_call" | custom-call | flops 6442450944 | bytes 1048576 | tf_op jit(solution)/shard_map/split_slices/pallas_call | solution.py:45
  1.9 3.0 %collective-permute-start = (bf16[32,1280]{1,0:T(8,128)(2,1)S(1)}, bf16[32,1280]{1,0:T(8,128)(2,1)S(1)}, u32[]{:S(2)}, u32[]{:S(2)}) collective-permute-start(bf16[32,1280]{1,0:T(8,128)(2,1)S(1)} %get-tuple-element.22), channel_id=1, source_target_pairs={{0,2},{1,3},{2,0},{3,1},{4,6},{5,7},{6,4},{7,5},{8,10},{9,11},{10,... | collective-permute-start | bytes 245768 | tf_op jit(solution)/shard_map/ppermute | solution.py:25
  4.9 0.0 collective-permute-start.1
  4.9 0.2 collective-permute-start.2
  5.1 0.0 copy-done.1
  5.1 1.7 %mask_coupling.1 = (bf16[1024,128]{1,0:T(8,128)(2,1)S(1)}, bf16[4096,768]{1,0:T(8,128)(2,1)S(1)}, s32[8,128]{1,0:T(8,128)S(1)}) custom-call(s32[8]{0:T(128)} %counts_ref.3, s32[3,8]{1,0:T(4,128)} %bitcast.2, s32[3,1,16]{2,1,0:T(1,128)} %bitcast.4, bf16[2048,128]{1,0:T(8,128)(2,1)S(1)} %copy-done.2, bf16[4096,768]{1,0:T(8,128)(2,1)S(1)} %copy-done.1), custom_call_target="tpu_custom_call" | custom-call | bytes 6291456 | tf_op jit(solution)/shard_map/mask_coupling/pallas_call | solution.py:148
  6.8 0.7 %collective-permute-done.refs_1_ = bf16[32,1280]{1,0:T(8,128)(2,1)S(1)} collective-permute-done((bf16[32,1280]{1,0:T(8,128)(2,1)S(1)}, bf16[32,1280]{1,0:T(8,128)(2,1)S(1)}, u32[]{:S(2)}, u32[]{:S(2)}) %collective-permute-start) | collective-permute-done | bytes 81952 | tf_op jit(solution)/shard_map/ppermute | solution.py:25
  7.6 0.0 collective-permute-done.1.refs_2_
  7.6 1.4 %collective-permute-done.2.refs_3_ = bf16[32,1280]{1,0:T(8,128)(2,1)S(1)} collective-permute-done((bf16[32,1280]{1,0:T(8,128)(2,1)S(1)}, bf16[32,1280]{1,0:T(8,128)(2,1)S(1)}, u32[]{:S(2)}, u32[]{:S(2)}) %collective-permute-start.2) | collective-permute-done | bytes 81952 | tf_op jit(solution)/shard_map/ppermute | solution.py:25
  9.0 1.1 %pack_windows.1 = (bf16[32,1536]{1,0:T(8,128)(2,1)S(1)}, bf16[32,640]{1,0:T(8,128)(2,1)S(1)}, bf16[32,896]{1,0:T(8,128)(2,1)S(1)}, bf16[32,1536]{1,0:T(8,128)(2,...) custom-call(s32[8]{0:T(128)} %counts_ref.3, ...), custom_call_target="tpu_custom_call" | custom-call | tf_op jit(solution)/shard_map/pack_windows/pallas_call | solution.py:118
  10.1 2.7 %collective-permute-start.3 = (bf16[32,640]{1,0:T(8,128)(2,1)S(1)}, bf16[32,640]{1,0:T(8,128)(2,1)S(1)}, u32[]{:S(2)}, u32[]{:S(2)}) collective-permute-start(bf16[32,640]{1,0:T(8,128)(2,1)S(1)} %get-tuple-element.27), channel_id=1, source_target_pairs={{0,16},{4,20},{8,24},{12,28},{16,0},{20,4},{24,8},{28,12},{1,17},{... | collective-permute-start | bytes 122888 | tf_op jit(solution)/shard_map/ppermute | solution.py:25
  12.8 1.3 %collective-permute-start.6 = (bf16[32,640]{1,0:T(8,128)(2,1)S(1)}, bf16[32,640]{1,0:T(8,128)(2,1)S(1)}, u32[]{:S(2)}, u32[]{:S(2)}) collective-permute-start(bf16[32,640]{1,0:T(8,128)(2,1)S(1)} %get-tuple-element.30), channel_id=1, source_target_pairs={{0,24},{4,28},{8,16},{12,20},{16,8},{20,12},{24,0},{28,4},{1,25},{... | collective-permute-start | bytes 122888 | tf_op jit(solution)/shard_map/ppermute | solution.py:25
  14.1 2.6 %collective-permute-start.5 = (bf16[32,1536]{1,0:T(8,128)(2,1)S(1)}, bf16[32,1536]{1,0:T(8,128)(2,1)S(1)}, u32[]{:S(2)}, u32[]{:S(2)}) collective-permute-start(bf16[32,1536]{1,0:T(8,128)(2,1)S(1)} %get-tuple-element.29), channel_id=1, source_target_pairs={{0,20},{4,16},{8,28},{12,24},{16,4},{20,0},{24,12},{28,8},{1,21},{... | collective-permute-start | bytes 294920 | tf_op jit(solution)/shard_map/ppermute | solution.py:25
  16.8 0.5 %collective-permute-start.8 = (bf16[32,1536]{1,0:T(8,128)(2,1)S(1)}, bf16[32,1536]{1,0:T(8,128)(2,1)S(1)}, u32[]{:S(2)}, u32[]{:S(2)}) collective-permute-start(bf16[32,1536]{1,0:T(8,128)(2,1)S(1)} %get-tuple-element.32), channel_id=1, source_target_pairs={{0,4},{4,0},{8,12},{12,8},{16,20},{20,16},{24,28},{28,24},{1,5},{5... | collective-permute-start | bytes 294920 | tf_op jit(solution)/shard_map/ppermute | solution.py:25
  17.3 2.3 %collective-permute-start.9 = (bf16[32,1536]{1,0:T(8,128)(2,1)S(1)}, bf16[32,1536]{1,0:T(8,128)(2,1)S(1)}, u32[]{:S(2)}, u32[]{:S(2)}) collective-permute-start(bf16[32,1536]{1,0:T(8,128)(2,1)S(1)} %get-tuple-element.33), channel_id=1, source_target_pairs={{0,12},{4,8},{8,4},{12,0},{16,28},{20,24},{24,20},{28,16},{1,13},{... | collective-permute-start | bytes 294920 | tf_op jit(solution)/shard_map/ppermute | solution.py:25
  19.6 0.0 collective-permute-done.3.refs_1_
  19.6 0.7 %collective-permute-start.10 = (bf16[32,1536]{1,0:T(8,128)(2,1)S(1)}, bf16[32,1536]{1,0:T(8,128)(2,1)S(1)}, u32[]{:S(2)}, u32[]{:S(2)}) collective-permute-start(bf16[32,1536]{1,0:T(8,128)(2,1)S(1)} %get-tuple-element.34), channel_id=1, source_target_pairs={{0,8},{4,12},{8,0},{12,4},{16,24},{20,28},{24,16},{28,20},{1,9},{5... | collective-permute-start | bytes 294920 | tf_op jit(solution)/shard_map/ppermute | solution.py:25
  20.2 0.0 collective-permute-done.6.refs_5_.refs_4_
  20.2 3.2 %collective-permute-start.11 = (bf16[32,1536]{1,0:T(8,128)(2,1)S(1)}, bf16[32,1536]{1,0:T(8,128)(2,1)S(1)}, u32[]{:S(2)}, u32[]{:S(2)}) collective-permute-start(bf16[32,1536]{1,0:T(8,128)(2,1)S(1)} %get-tuple-element.35), channel_id=1, source_target_pairs={{0,28},{4,24},{8,20},{12,16},{16,12},{20,8},{24,4},{28,0},{1,29},{... | collective-permute-start | bytes 294920 | tf_op jit(solution)/shard_map/ppermute | solution.py:25
  23.4 0.6 %collective-permute-done.5.refs_6_.refs_3_ = bf16[32,1536]{1,0:T(8,128)(2,1)S(1)} collective-permute-done((bf16[32,1536]{1,0:T(8,128)(2,1)S(1)}, bf16[32,1536]{1,0:T(8,128)(2,1)S(1)}, u32[]{:S(2)}, u32[]{:S(2)}) %collective-permute-start.5) | collective-permute-done | bytes 98336 | tf_op jit(solution)/shard_map/ppermute | solution.py:25
  24.0 0.1 collective-permute-start.4
  24.1 0.9 %collective-permute-done.8.refs_3_.refs_6_ = bf16[32,1536]{1,0:T(8,128)(2,1)S(1)} collective-permute-done((bf16[32,1536]{1,0:T(8,128)(2,1)S(1)}, bf16[32,1536]{1,0:T(8,128)(2,1)S(1)}, u32[]{:S(2)}, u32[]{:S(2)}) %collective-permute-start.8) | collective-permute-done | bytes 98336 | tf_op jit(solution)/shard_map/ppermute | solution.py:25
  25.0 2.0 %collective-permute-start.7 = (bf16[32,896]{1,0:T(8,128)(2,1)S(1)}, bf16[32,896]{1,0:T(8,128)(2,1)S(1)}, u32[]{:S(2)}, u32[]{:S(2)}) collective-permute-start(bf16[32,896]{1,0:T(8,128)(2,1)S(1)} %get-tuple-element.31), channel_id=1, source_target_pairs={{0,24},{4,28},{8,16},{12,20},{16,8},{20,12},{24,0},{28,4},{1,25},{... | collective-permute-start | bytes 172040 | tf_op jit(solution)/shard_map/ppermute | solution.py:25
  26.9 0.0 collective-permute-done.9.refs_2_.refs_7_
  26.9 2.3 %collective-permute-done.10.refs_4_.refs_8_ = bf16[32,1536]{1,0:T(8,128)(2,1)S(1)} collective-permute-done((bf16[32,1536]{1,0:T(8,128)(2,1)S(1)}, bf16[32,1536]{1,0:T(8,128)(2,1)S(1)}, u32[]{:S(2)}, u32[]{:S(2)}) %collective-permute-start.10) | collective-permute-done | bytes 98336 | tf_op jit(solution)/shard_map/ppermute | solution.py:25
  29.2 0.0 collective-permute-done.11.refs_7_.refs_9_
  29.2 2.0 %separator_fields_and_coupling.1 = (f32[4096,256]{1,0:T(8,128)S(1)}, bf16[256,256]{1,0:T(8,128)(2,1)}) custom-call(bf16[32,1536]{1,0:T(8,128)(2,1)S(1)} %get-tuple-element.26.refs_0_, bf16[32,640]{1,0:T(8,128)(2,1)S(1)} %collective-permute-done.3.refs_1_, bf16[32,1536]{1,0:T(8,128)(2,1)S(1)} %collective-permute-done.9.refs_2_.refs_7_, ...), custom_call_target="tpu_custom_call" | custom-call | flops 1610612736 | bytes 6291456 | tf_op jit(solution)/shard_map/separator_fields_and_coupling/pallas_call | solution.py:193
  31.3 0.5 %collective-permute-done.4.refs_2_ = bf16[32,896]{1,0:T(8,128)(2,1)S(1)} collective-permute-done((bf16[32,896]{1,0:T(8,128)(2,1)S(1)}, bf16[32,896]{1,0:T(8,128)(2,1)S(1)}, u32[]{:S(2)}, u32[]{:S(2)}) %collective-permute-start.4) | collective-permute-done | bytes 57376 | tf_op jit(solution)/shard_map/ppermute | solution.py:25
  31.8 0.0 collective-permute-done.7.refs_5_
  31.8 3.6 %interior_field.1 = bf16[4096,256]{1,0:T(8,128)(2,1)} custom-call(bf16[32,1536]{1,0:T(8,128)(2,1)S(1)} %get-tuple-element.26.refs_0_, bf16[32,640]{1,0:T(8,128)(2,1)S(1)} %collective-permute-done.3.refs_1_, bf16[32,896]{1,0:T(8,128)(2,1)S(1)} %collective-permute-done.4.refs_2_, bf16[32,1536]{1,0:T(8,128)(2,1)S(1)} %collective-permute-done.5.refs_6_.refs_3_, ...), custom_call_target="tpu_custom_call" | custom-call | tf_op jit(solution)/shard_map/interior_field/pallas_call | solution.py:244
  (3 shorter events, 0.0 us)
Async XLA Ops:
  0.6 4.5 %copy-start.1 = (bf16[4096,768]{1,0:T(8,128)(2,1)S(1)}, bf16[4096,768]{1,0:T(8,128)(2,1)}, u32[]{:S(2)}) copy-start(bf16[4096,768]{1,0:T(8,128)(2,1)} %coupling_ref.1) | copy-start | bytes 18874372
  0.6 4.5 %copy-start.2 = (bf16[2048,128]{1,0:T(8,128)(2,1)S(1)}, bf16[2048,128]{1,0:T(8,128)(2,1)}, u32[]{:S(2)}) copy-start(bf16[2048,128]{1,0:T(8,128)(2,1)} %sep_ref.1) | copy-start | bytes 1572868
  1.9 5.7 %collective-permute-start = (bf16[32,1280]{1,0:T(8,128)(2,1)S(1)}, bf16[32,1280]{1,0:T(8,128)(2,1)S(1)}, u32[]{:S(2)}, u32[]{:S(2)}) collective-permute-start(bf16[32,1280]{1,0:T(8,128)(2,1)S(1)} %get-tuple-element.22), channel_id=1, source_target_pairs={{0,2},{1,3},{2,0},{3,1},{4,6},{5,7},{6,4},{7,5},{8,10},{9,11},{10,... | collective-permute-start | bytes 245768 | tf_op jit(solution)/shard_map/ppermute | solution.py:25
  4.9 2.7 %collective-permute-start.1 = (bf16[32,1280]{1,0:T(8,128)(2,1)S(1)}, bf16[32,1280]{1,0:T(8,128)(2,1)S(1)}, u32[]{:S(2)}, u32[]{:S(2)}) collective-permute-start(bf16[32,1280]{1,0:T(8,128)(2,1)S(1)} %get-tuple-element.23), channel_id=1, source_target_pairs={{0,1},{1,0},{2,3},{3,2},{4,5},{5,4},{6,7},{7,6},{8,9},{9,8},{10,11... | collective-permute-start | bytes 245768 | tf_op jit(solution)/shard_map/ppermute | solution.py:25
  4.9 4.1 %collective-permute-start.2 = (bf16[32,1280]{1,0:T(8,128)(2,1)S(1)}, bf16[32,1280]{1,0:T(8,128)(2,1)S(1)}, u32[]{:S(2)}, u32[]{:S(2)}) collective-permute-start(bf16[32,1280]{1,0:T(8,128)(2,1)S(1)} %get-tuple-element.24), channel_id=1, source_target_pairs={{0,3},{1,2},{2,1},{3,0},{4,7},{5,6},{6,5},{7,4},{8,11},{9,10},{10,... | collective-permute-start | bytes 245768 | tf_op jit(solution)/shard_map/ppermute | solution.py:25
  5.1 26.7 %copy-start = (bf16[4096,1024]{1,0:T(8,128)(2,1)S(1)}, bf16[4096,1024]{1,0:T(8,128)(2,1)}, u32[]{:S(2)}) copy-start(bf16[4096,1024]{1,0:T(8,128)(2,1)} %refs_11_.1) | copy-start | bytes 25165828
  10.1 9.4 %collective-permute-start.3 = (bf16[32,640]{1,0:T(8,128)(2,1)S(1)}, bf16[32,640]{1,0:T(8,128)(2,1)S(1)}, u32[]{:S(2)}, u32[]{:S(2)}) collective-permute-start(bf16[32,640]{1,0:T(8,128)(2,1)S(1)} %get-tuple-element.27), channel_id=1, source_target_pairs={{0,16},{4,20},{8,24},{12,28},{16,0},{20,4},{24,8},{28,12},{1,17},{... | collective-permute-start | bytes 122888 | tf_op jit(solution)/shard_map/ppermute | solution.py:25
  12.8 7.5 %collective-permute-start.6 = (bf16[32,640]{1,0:T(8,128)(2,1)S(1)}, bf16[32,640]{1,0:T(8,128)(2,1)S(1)}, u32[]{:S(2)}, u32[]{:S(2)}) collective-permute-start(bf16[32,640]{1,0:T(8,128)(2,1)S(1)} %get-tuple-element.30), channel_id=1, source_target_pairs={{0,24},{4,28},{8,16},{12,20},{16,8},{20,12},{24,0},{28,4},{1,25},{... | collective-permute-start | bytes 122888 | tf_op jit(solution)/shard_map/ppermute | solution.py:25
  14.1 9.8 %collective-permute-start.5 = (bf16[32,1536]{1,0:T(8,128)(2,1)S(1)}, bf16[32,1536]{1,0:T(8,128)(2,1)S(1)}, u32[]{:S(2)}, u32[]{:S(2)}) collective-permute-start(bf16[32,1536]{1,0:T(8,128)(2,1)S(1)} %get-tuple-element.29), channel_id=1, source_target_pairs={{0,20},{4,16},{8,28},{12,24},{16,4},{20,0},{24,12},{28,8},{1,21},{... | collective-permute-start | bytes 294920 | tf_op jit(solution)/shard_map/ppermute | solution.py:25
  16.8 8.2 %collective-permute-start.8 = (bf16[32,1536]{1,0:T(8,128)(2,1)S(1)}, bf16[32,1536]{1,0:T(8,128)(2,1)S(1)}, u32[]{:S(2)}, u32[]{:S(2)}) collective-permute-start(bf16[32,1536]{1,0:T(8,128)(2,1)S(1)} %get-tuple-element.32), channel_id=1, source_target_pairs={{0,4},{4,0},{8,12},{12,8},{16,20},{20,16},{24,28},{28,24},{1,5},{5... | collective-permute-start | bytes 294920 | tf_op jit(solution)/shard_map/ppermute | solution.py:25
  17.3 9.6 %collective-permute-start.9 = (bf16[32,1536]{1,0:T(8,128)(2,1)S(1)}, bf16[32,1536]{1,0:T(8,128)(2,1)S(1)}, u32[]{:S(2)}, u32[]{:S(2)}) collective-permute-start(bf16[32,1536]{1,0:T(8,128)(2,1)S(1)} %get-tuple-element.33), channel_id=1, source_target_pairs={{0,12},{4,8},{8,4},{12,0},{16,28},{20,24},{24,20},{28,16},{1,13},{... | collective-permute-start | bytes 294920 | tf_op jit(solution)/shard_map/ppermute | solution.py:25
  19.6 9.7 %collective-permute-start.10 = (bf16[32,1536]{1,0:T(8,128)(2,1)S(1)}, bf16[32,1536]{1,0:T(8,128)(2,1)S(1)}, u32[]{:S(2)}, u32[]{:S(2)}) collective-permute-start(bf16[32,1536]{1,0:T(8,128)(2,1)S(1)} %get-tuple-element.34), channel_id=1, source_target_pairs={{0,8},{4,12},{8,0},{12,4},{16,24},{20,28},{24,16},{28,20},{1,9},{5... | collective-permute-start | bytes 294920 | tf_op jit(solution)/shard_map/ppermute | solution.py:25
  20.2 9.0 %collective-permute-start.11 = (bf16[32,1536]{1,0:T(8,128)(2,1)S(1)}, bf16[32,1536]{1,0:T(8,128)(2,1)S(1)}, u32[]{:S(2)}, u32[]{:S(2)}) collective-permute-start(bf16[32,1536]{1,0:T(8,128)(2,1)S(1)} %get-tuple-element.35), channel_id=1, source_target_pairs={{0,28},{4,24},{8,20},{12,16},{16,12},{20,8},{24,4},{28,0},{1,29},{... | collective-permute-start | bytes 294920 | tf_op jit(solution)/shard_map/ppermute | solution.py:25
  24.0 7.8 %collective-permute-start.4 = (bf16[32,896]{1,0:T(8,128)(2,1)S(1)}, bf16[32,896]{1,0:T(8,128)(2,1)S(1)}, u32[]{:S(2)}, u32[]{:S(2)}) collective-permute-start(bf16[32,896]{1,0:T(8,128)(2,1)S(1)} %get-tuple-element.28), channel_id=1, source_target_pairs={{0,16},{4,20},{8,24},{12,28},{16,0},{20,4},{24,8},{28,12},{1,17},{... | collective-permute-start | bytes 172040 | tf_op jit(solution)/shard_map/ppermute | solution.py:25
  25.0 6.8 %collective-permute-start.7 = (bf16[32,896]{1,0:T(8,128)(2,1)S(1)}, bf16[32,896]{1,0:T(8,128)(2,1)S(1)}, u32[]{:S(2)}, u32[]{:S(2)}) collective-permute-start(bf16[32,896]{1,0:T(8,128)(2,1)S(1)} %get-tuple-element.31), channel_id=1, source_target_pairs={{0,24},{4,28},{8,16},{12,20},{16,8},{20,12},{24,0},{28,4},{1,25},{... | collective-permute-start | bytes 172040 | tf_op jit(solution)/shard_map/ppermute | solution.py:25

commit v6 on v5

--- a/solution.py
+++ b/solution.py
@@ -62,13 +62,13 @@
     keep = lane < LANES - shift
     pieces = {}
     for j in range(first // LANES, last // LANES + 1):
-        piece = rows_ref[:, pl.ds(base + j * LANES, LANES)].astype(jnp.float32)
+        piece = rows_ref[:, pl.ds(base + j * LANES, LANES)]
         pieces[j] = pltpu.roll(piece, back, 1)
     for j in range(first // LANES, last // LANES):
         merged = jnp.where(keep, pieces[j], pieces[j + 1])
-        merged = jnp.where(lane + j * LANES < count, merged, 0.0)
+        merged = jnp.where(lane + j * LANES < count, merged, jnp.zeros_like(merged))
         at = j * LANES - first
-        out_ref[:, at : at + LANES] = merged.astype(rows_ref.dtype)
+        out_ref[:, at : at + LANES] = merged
 
 
 def put_separators(from_ref, first, out_ref, to, owner, anc_ref):
@@ -160,8 +160,11 @@
     )(row_counts, ancestors, pattern, separator_modes, coupling)
 
 
-def gather_rows(places, slots, got_ref):
+def gather_rows(places, slots, got_ref, limit):
     for n, lanes, first, last, turn in places:
+        last = min(last, limit)
+        if last <= first:
+            continue
         slice_cols = slots[n].shape[0]
         block = 0 if turn is None else jnp.bitwise_xor(lax.axis_index("sub"), turn)
         at = pl.multiple_of(block * slice_cols, slice_cols)
@@ -170,7 +173,7 @@
 
 def above_kernel(rows, places, slot_count, *refs):
     slots, (sep_ref, coupling_ref, total_ref, own_ref, got_ref, above_ref) = refs[:slot_count], refs[slot_count:]
-    gather_rows(places, slots, got_ref)
+    gather_rows(places, slots, got_ref, got_ref.shape[1])
     for k in range(LEVELS + 1):
         part = got_ref[:, k * SEPM : (k + 1) * SEPM]
         block = lax.dot_general(
@@ -215,7 +218,6 @@
     count_ref, modes_ref, total_ref, field_ref, got_ref, coef_ref, block_ref, sems = refs
     phys, cap = modes_ref.shape
     tiles = jnp.clip((jnp.max(count_ref[...]) + BW - 1) // BW, 1, cap // BW)
-    gather_rows(places, slots, got_ref)
     copies = [
         pltpu.make_async_copy(block_ref.at[pl.ds(at, rows)], field_ref.at[pl.ds(at, rows)], sems.at[n])
         for n, at in enumerate(range(0, phys, rows))
@@ -224,6 +226,7 @@
 
         @pl.when(tiles == used)
         def _(depth=used * BW):
+            gather_rows(places, slots, got_ref, depth)
             coef_ref[:depth, :] = got_ref[:, :depth].T
             for n, first in enumerate(range(0, phys, rows)):
                 at = slice(first, first + rows)

time: 35 us -> 35 us (level); the launches traced: 35.4 us -> 34.8 us
  Pallas kernels: 9.62 us -> 9.1 us
    pallas_call x1, Pallas kernels: 3.56 us -> 3.05 us  [interior(): pl.pallas_call(functools.partial(interior_kernel, rows, places, len(slots...]
where the time goes in v6:
time: 35 us; the launch traced here: 34.8 us
  starting transfers between devices  18.6 us (53%)
  Pallas kernels  9.1 us (26%)
  waiting for transfers between devices  6.44 us (18%)
  between operations  0.68 us (2%)
    ppermute x12, starting transfers between devices, turn_over(): return lax.ppermute(block, axis, [(i, i ^ turn) for i in range(count)])  18.6 us
    ppermute x12, waiting for transfers between devices, turn_over(): return lax.ppermute(block, axis, [(i, i ^ turn) for i in range(count)])  6.44 us
    pallas_call x1, Pallas kernels, interior(): pl.pallas_call(functools.partial(interior_kernel, rows, places, len(slots...  3.05 us
    pallas_call x1, Pallas kernels, above_fields(): pl.pallas_call(functools.partial(above_kernel, 2 * BW, places, len(slots)...  2.03 us
    pallas_call x1, Pallas kernels, mask(): pl.pallas_call(mask_kernel, out_shape=(pltpu.VMEM(((LEVELS + 1) * BW, SEP...  1.7 us
    pallas_call x1, Pallas kernels, split(): pl.pallas_call(split_kernel, out_shape=[jax.ShapeDtypeStruct(shape, coeff...  1.2 us
    pallas_call x1, Pallas kernels, pack(): pl.pallas_call(functools.partial(pack_kernel, interior_total, cap, turns,...  1.12 us
  transfers between devices with their start and end apart: 12, of which 6 were waited for; matrix products, arithmetic and copies ran while one was open for 0% of the time, Pallas kernels for 11%

profile of v6, /device:TPU:0, one launch (start us, length us, event | category | flops | bytes accessed | tf_op | source)
XLA Modules:
  0.0 34.8 jit_solution(17220223729502953441)
XLA Ops:
  0.6 0.0 copy-start.1
  0.6 0.0 copy-start.2
  0.6 1.2 %split_slices.1 = (bf16[32,1280]{1,0:T(8,128)(2,1)S(1)}, bf16[32,1280]{1,0:T(8,128)(2,1)S(1)}, bf16[32,1280]{1,0:T(8,128)(2,1)S(1)}, bf16[32,1280]{1,0:T(8,128)(2,1)S(1)}) custom-call(bf16[128,1280]{1,0:T(8,128)(2,1)} %coef_ref.1), custom_call_target="tpu_custom_call" | custom-call | flops 6442450944 | bytes 1048576 | tf_op jit(solution)/shard_map/split_slices/pallas_call | solution.py:45
  1.9 3.0 %collective-permute-start = (bf16[32,1280]{1,0:T(8,128)(2,1)S(1)}, bf16[32,1280]{1,0:T(8,128)(2,1)S(1)}, u32[]{:S(2)}, u32[]{:S(2)}) collective-permute-start(bf16[32,1280]{1,0:T(8,128)(2,1)S(1)} %get-tuple-element.22), channel_id=1, source_target_pairs={{0,2},{1,3},{2,0},{3,1},{4,6},{5,7},{6,4},{7,5},{8,10},{9,11},{10,... | collective-permute-start | bytes 245768 | tf_op jit(solution)/shard_map/ppermute | solution.py:25
  4.9 0.0 collective-permute-start.1
  4.9 0.2 collective-permute-start.2
  5.1 1.7 %mask_coupling.1 = (bf16[1024,128]{1,0:T(8,128)(2,1)S(1)}, bf16[4096,768]{1,0:T(8,128)(2,1)S(1)}, s32[8,128]{1,0:T(8,128)S(1)}) custom-call(s32[8]{0:T(128)} %counts_ref.3, s32[3,8]{1,0:T(4,128)} %bitcast.2, s32[3,1,16]{2,1,0:T(1,128)} %bitcast.4, bf16[2048,128]{1,0:T(8,128)(2,1)S(1)} %copy-done.2, bf16[4096,768]{1,0:T(8,128)(2,1)S(1)} %copy-done.1), custom_call_target="tpu_custom_call" | custom-call | bytes 6291456 | tf_op jit(solution)/shard_map/mask_coupling/pallas_call | solution.py:148
  6.8 0.7 %collective-permute-done.refs_1_ = bf16[32,1280]{1,0:T(8,128)(2,1)S(1)} collective-permute-done((bf16[32,1280]{1,0:T(8,128)(2,1)S(1)}, bf16[32,1280]{1,0:T(8,128)(2,1)S(1)}, u32[]{:S(2)}, u32[]{:S(2)}) %collective-permute-start) | collective-permute-done | bytes 81952 | tf_op jit(solution)/shard_map/ppermute | solution.py:25
  7.6 0.0 collective-permute-done.1.refs_2_
  7.6 1.4 %collective-permute-done.2.refs_3_ = bf16[32,1280]{1,0:T(8,128)(2,1)S(1)} collective-permute-done((bf16[32,1280]{1,0:T(8,128)(2,1)S(1)}, bf16[32,1280]{1,0:T(8,128)(2,1)S(1)}, u32[]{:S(2)}, u32[]{:S(2)}) %collective-permute-start.2) | collective-permute-done | bytes 81952 | tf_op jit(solution)/shard_map/ppermute | solution.py:25
  9.0 1.1 %pack_windows.1 = (bf16[32,1536]{1,0:T(8,128)(2,1)S(1)}, bf16[32,640]{1,0:T(8,128)(2,1)S(1)}, bf16[32,896]{1,0:T(8,128)(2,1)S(1)}, bf16[32,1536]{1,0:T(8,128)(2,...) custom-call(s32[8]{0:T(128)} %counts_ref.3, ...), custom_call_target="tpu_custom_call" | custom-call | tf_op jit(solution)/shard_map/pack_windows/pallas_call | solution.py:118
  10.1 2.7 %collective-permute-start.3 = (bf16[32,640]{1,0:T(8,128)(2,1)S(1)}, bf16[32,640]{1,0:T(8,128)(2,1)S(1)}, u32[]{:S(2)}, u32[]{:S(2)}) collective-permute-start(bf16[32,640]{1,0:T(8,128)(2,1)S(1)} %get-tuple-element.27), channel_id=1, source_target_pairs={{0,16},{4,20},{8,24},{12,28},{16,0},{20,4},{24,8},{28,12},{1,17},{... | collective-permute-start | bytes 122888 | tf_op jit(solution)/shard_map/ppermute | solution.py:25
  12.8 1.3 %collective-permute-start.6 = (bf16[32,640]{1,0:T(8,128)(2,1)S(1)}, bf16[32,640]{1,0:T(8,128)(2,1)S(1)}, u32[]{:S(2)}, u32[]{:S(2)}) collective-permute-start(bf16[32,640]{1,0:T(8,128)(2,1)S(1)} %get-tuple-element.30), channel_id=1, source_target_pairs={{0,24},{4,28},{8,16},{12,20},{16,8},{20,12},{24,0},{28,4},{1,25},{... | collective-permute-start | bytes 122888 | tf_op jit(solution)/shard_map/ppermute | solution.py:25
  14.1 2.6 %collective-permute-start.5 = (bf16[32,1536]{1,0:T(8,128)(2,1)S(1)}, bf16[32,1536]{1,0:T(8,128)(2,1)S(1)}, u32[]{:S(2)}, u32[]{:S(2)}) collective-permute-start(bf16[32,1536]{1,0:T(8,128)(2,1)S(1)} %get-tuple-element.29), channel_id=1, source_target_pairs={{0,20},{4,16},{8,28},{12,24},{16,4},{20,0},{24,12},{28,8},{1,21},{... | collective-permute-start | bytes 294920 | tf_op jit(solution)/shard_map/ppermute | solution.py:25
  16.7 0.5 %collective-permute-start.8 = (bf16[32,1536]{1,0:T(8,128)(2,1)S(1)}, bf16[32,1536]{1,0:T(8,128)(2,1)S(1)}, u32[]{:S(2)}, u32[]{:S(2)}) collective-permute-start(bf16[32,1536]{1,0:T(8,128)(2,1)S(1)} %get-tuple-element.32), channel_id=1, source_target_pairs={{0,4},{4,0},{8,12},{12,8},{16,20},{20,16},{24,28},{28,24},{1,5},{5... | collective-permute-start | bytes 294920 | tf_op jit(solution)/shard_map/ppermute | solution.py:25
  17.3 2.3 %collective-permute-start.9 = (bf16[32,1536]{1,0:T(8,128)(2,1)S(1)}, bf16[32,1536]{1,0:T(8,128)(2,1)S(1)}, u32[]{:S(2)}, u32[]{:S(2)}) collective-permute-start(bf16[32,1536]{1,0:T(8,128)(2,1)S(1)} %get-tuple-element.33), channel_id=1, source_target_pairs={{0,12},{4,8},{8,4},{12,0},{16,28},{20,24},{24,20},{28,16},{1,13},{... | collective-permute-start | bytes 294920 | tf_op jit(solution)/shard_map/ppermute | solution.py:25
  19.5 0.0 collective-permute-done.3.refs_1_
  19.5 0.7 %collective-permute-start.10 = (bf16[32,1536]{1,0:T(8,128)(2,1)S(1)}, bf16[32,1536]{1,0:T(8,128)(2,1)S(1)}, u32[]{:S(2)}, u32[]{:S(2)}) collective-permute-start(bf16[32,1536]{1,0:T(8,128)(2,1)S(1)} %get-tuple-element.34), channel_id=1, source_target_pairs={{0,8},{4,12},{8,0},{12,4},{16,24},{20,28},{24,16},{28,20},{1,9},{5... | collective-permute-start | bytes 294920 | tf_op jit(solution)/shard_map/ppermute | solution.py:25
  20.2 0.0 collective-permute-done.6.refs_5_.refs_4_
  20.2 3.2 %collective-permute-start.11 = (bf16[32,1536]{1,0:T(8,128)(2,1)S(1)}, bf16[32,1536]{1,0:T(8,128)(2,1)S(1)}, u32[]{:S(2)}, u32[]{:S(2)}) collective-permute-start(bf16[32,1536]{1,0:T(8,128)(2,1)S(1)} %get-tuple-element.35), channel_id=1, source_target_pairs={{0,28},{4,24},{8,20},{12,16},{16,12},{20,8},{24,4},{28,0},{1,29},{... | collective-permute-start | bytes 294920 | tf_op jit(solution)/shard_map/ppermute | solution.py:25
  23.4 0.6 %collective-permute-done.5.refs_6_.refs_3_ = bf16[32,1536]{1,0:T(8,128)(2,1)S(1)} collective-permute-done((bf16[32,1536]{1,0:T(8,128)(2,1)S(1)}, bf16[32,1536]{1,0:T(8,128)(2,1)S(1)}, u32[]{:S(2)}, u32[]{:S(2)}) %collective-permute-start.5) | collective-permute-done | bytes 98336 | tf_op jit(solution)/shard_map/ppermute | solution.py:25
  24.0 0.1 collective-permute-start.4
  24.1 0.9 %collective-permute-done.8.refs_3_.refs_6_ = bf16[32,1536]{1,0:T(8,128)(2,1)S(1)} collective-permute-done((bf16[32,1536]{1,0:T(8,128)(2,1)S(1)}, bf16[32,1536]{1,0:T(8,128)(2,1)S(1)}, u32[]{:S(2)}, u32[]{:S(2)}) %collective-permute-start.8) | collective-permute-done | bytes 98336 | tf_op jit(solution)/shard_map/ppermute | solution.py:25
  24.9 2.0 %collective-permute-start.7 = (bf16[32,896]{1,0:T(8,128)(2,1)S(1)}, bf16[32,896]{1,0:T(8,128)(2,1)S(1)}, u32[]{:S(2)}, u32[]{:S(2)}) collective-permute-start(bf16[32,896]{1,0:T(8,128)(2,1)S(1)} %get-tuple-element.31), channel_id=1, source_target_pairs={{0,24},{4,28},{8,16},{12,20},{16,8},{20,12},{24,0},{28,4},{1,25},{... | collective-permute-start | bytes 172040 | tf_op jit(solution)/shard_map/ppermute | solution.py:25
  26.9 0.0 collective-permute-done.9.refs_2_.refs_7_
  26.9 2.3 %collective-permute-done.10.refs_4_.refs_8_ = bf16[32,1536]{1,0:T(8,128)(2,1)S(1)} collective-permute-done((bf16[32,1536]{1,0:T(8,128)(2,1)S(1)}, bf16[32,1536]{1,0:T(8,128)(2,1)S(1)}, u32[]{:S(2)}, u32[]{:S(2)}) %collective-permute-start.10) | collective-permute-done | bytes 98336 | tf_op jit(solution)/shard_map/ppermute | solution.py:25
  29.2 0.0 collective-permute-done.11.refs_7_.refs_9_
  29.2 2.0 %separator_fields_and_coupling.1 = (f32[4096,256]{1,0:T(8,128)S(1)}, bf16[256,256]{1,0:T(8,128)(2,1)}) custom-call(bf16[32,1536]{1,0:T(8,128)(2,1)S(1)} %get-tuple-element.26.refs_0_, bf16[32,640]{1,0:T(8,128)(2,1)S(1)} %collective-permute-done.3.refs_1_, bf16[32,1536]{1,0:T(8,128)(2,1)S(1)} %collective-permute-done.9.refs_2_.refs_7_, ...), custom_call_target="tpu_custom_call" | custom-call | flops 1610612736 | bytes 6291456 | tf_op jit(solution)/shard_map/separator_fields_and_coupling/pallas_call | solution.py:196
  31.3 0.5 %collective-permute-done.4.refs_2_ = bf16[32,896]{1,0:T(8,128)(2,1)S(1)} collective-permute-done((bf16[32,896]{1,0:T(8,128)(2,1)S(1)}, bf16[32,896]{1,0:T(8,128)(2,1)S(1)}, u32[]{:S(2)}, u32[]{:S(2)}) %collective-permute-start.4) | collective-permute-done | bytes 57376 | tf_op jit(solution)/shard_map/ppermute | solution.py:25
  31.8 0.0 collective-permute-done.7.refs_5_
  31.8 0.0 copy-done
  31.8 3.1 %interior_field.1 = bf16[4096,256]{1,0:T(8,128)(2,1)} custom-call(bf16[32,1536]{1,0:T(8,128)(2,1)S(1)} %get-tuple-element.26.refs_0_, bf16[32,640]{1,0:T(8,128)(2,1)S(1)} %collective-permute-done.3.refs_1_, bf16[32,896]{1,0:T(8,128)(2,1)S(1)} %collective-permute-done.4.refs_2_, bf16[32,1536]{1,0:T(8,128)(2,1)S(1)} %collective-permute-done.5.refs_6_.refs_3_, ...), custom_call_target="tpu_custom_call" | custom-call | tf_op jit(solution)/shard_map/interior_field/pallas_call | solution.py:247
  (3 shorter events, 0.0 us)
Async XLA Ops:
  0.6 4.5 %copy-start.1 = (bf16[4096,768]{1,0:T(8,128)(2,1)S(1)}, bf16[4096,768]{1,0:T(8,128)(2,1)}, u32[]{:S(2)}) copy-start(bf16[4096,768]{1,0:T(8,128)(2,1)} %coupling_ref.1) | copy-start | bytes 18874372
  0.6 4.5 %copy-start.2 = (bf16[2048,128]{1,0:T(8,128)(2,1)S(1)}, bf16[2048,128]{1,0:T(8,128)(2,1)}, u32[]{:S(2)}) copy-start(bf16[2048,128]{1,0:T(8,128)(2,1)} %sep_ref.1) | copy-start | bytes 1572868
  1.9 5.7 %collective-permute-start = (bf16[32,1280]{1,0:T(8,128)(2,1)S(1)}, bf16[32,1280]{1,0:T(8,128)(2,1)S(1)}, u32[]{:S(2)}, u32[]{:S(2)}) collective-permute-start(bf16[32,1280]{1,0:T(8,128)(2,1)S(1)} %get-tuple-element.22), channel_id=1, source_target_pairs={{0,2},{1,3},{2,0},{3,1},{4,6},{5,7},{6,4},{7,5},{8,10},{9,11},{10,... | collective-permute-start | bytes 245768 | tf_op jit(solution)/shard_map/ppermute | solution.py:25
  4.9 2.7 %collective-permute-start.1 = (bf16[32,1280]{1,0:T(8,128)(2,1)S(1)}, bf16[32,1280]{1,0:T(8,128)(2,1)S(1)}, u32[]{:S(2)}, u32[]{:S(2)}) collective-permute-start(bf16[32,1280]{1,0:T(8,128)(2,1)S(1)} %get-tuple-element.23), channel_id=1, source_target_pairs={{0,1},{1,0},{2,3},{3,2},{4,5},{5,4},{6,7},{7,6},{8,9},{9,8},{10,11... | collective-permute-start | bytes 245768 | tf_op jit(solution)/shard_map/ppermute | solution.py:25
  4.9 4.1 %collective-permute-start.2 = (bf16[32,1280]{1,0:T(8,128)(2,1)S(1)}, bf16[32,1280]{1,0:T(8,128)(2,1)S(1)}, u32[]{:S(2)}, u32[]{:S(2)}) collective-permute-start(bf16[32,1280]{1,0:T(8,128)(2,1)S(1)} %get-tuple-element.24), channel_id=1, source_target_pairs={{0,3},{1,2},{2,1},{3,0},{4,7},{5,6},{6,5},{7,4},{8,11},{9,10},{10,... | collective-permute-start | bytes 245768 | tf_op jit(solution)/shard_map/ppermute | solution.py:25
  5.1 26.7 %copy-start = (bf16[4096,1024]{1,0:T(8,128)(2,1)S(1)}, bf16[4096,1024]{1,0:T(8,128)(2,1)}, u32[]{:S(2)}) copy-start(bf16[4096,1024]{1,0:T(8,128)(2,1)} %refs_11_.1) | copy-start | bytes 25165828
  10.1 9.4 %collective-permute-start.3 = (bf16[32,640]{1,0:T(8,128)(2,1)S(1)}, bf16[32,640]{1,0:T(8,128)(2,1)S(1)}, u32[]{:S(2)}, u32[]{:S(2)}) collective-permute-start(bf16[32,640]{1,0:T(8,128)(2,1)S(1)} %get-tuple-element.27), channel_id=1, source_target_pairs={{0,16},{4,20},{8,24},{12,28},{16,0},{20,4},{24,8},{28,12},{1,17},{... | collective-permute-start | bytes 122888 | tf_op jit(solution)/shard_map/ppermute | solution.py:25
  12.8 7.5 %collective-permute-start.6 = (bf16[32,640]{1,0:T(8,128)(2,1)S(1)}, bf16[32,640]{1,0:T(8,128)(2,1)S(1)}, u32[]{:S(2)}, u32[]{:S(2)}) collective-permute-start(bf16[32,640]{1,0:T(8,128)(2,1)S(1)} %get-tuple-element.30), channel_id=1, source_target_pairs={{0,24},{4,28},{8,16},{12,20},{16,8},{20,12},{24,0},{28,4},{1,25},{... | collective-permute-start | bytes 122888 | tf_op jit(solution)/shard_map/ppermute | solution.py:25
  14.1 9.8 %collective-permute-start.5 = (bf16[32,1536]{1,0:T(8,128)(2,1)S(1)}, bf16[32,1536]{1,0:T(8,128)(2,1)S(1)}, u32[]{:S(2)}, u32[]{:S(2)}) collective-permute-start(bf16[32,1536]{1,0:T(8,128)(2,1)S(1)} %get-tuple-element.29), channel_id=1, source_target_pairs={{0,20},{4,16},{8,28},{12,24},{16,4},{20,0},{24,12},{28,8},{1,21},{... | collective-permute-start | bytes 294920 | tf_op jit(solution)/shard_map/ppermute | solution.py:25
  16.7 8.2 %collective-permute-start.8 = (bf16[32,1536]{1,0:T(8,128)(2,1)S(1)}, bf16[32,1536]{1,0:T(8,128)(2,1)S(1)}, u32[]{:S(2)}, u32[]{:S(2)}) collective-permute-start(bf16[32,1536]{1,0:T(8,128)(2,1)S(1)} %get-tuple-element.32), channel_id=1, source_target_pairs={{0,4},{4,0},{8,12},{12,8},{16,20},{20,16},{24,28},{28,24},{1,5},{5... | collective-permute-start | bytes 294920 | tf_op jit(solution)/shard_map/ppermute | solution.py:25
  17.3 9.6 %collective-permute-start.9 = (bf16[32,1536]{1,0:T(8,128)(2,1)S(1)}, bf16[32,1536]{1,0:T(8,128)(2,1)S(1)}, u32[]{:S(2)}, u32[]{:S(2)}) collective-permute-start(bf16[32,1536]{1,0:T(8,128)(2,1)S(1)} %get-tuple-element.33), channel_id=1, source_target_pairs={{0,12},{4,8},{8,4},{12,0},{16,28},{20,24},{24,20},{28,16},{1,13},{... | collective-permute-start | bytes 294920 | tf_op jit(solution)/shard_map/ppermute | solution.py:25
  19.5 9.7 %collective-permute-start.10 = (bf16[32,1536]{1,0:T(8,128)(2,1)S(1)}, bf16[32,1536]{1,0:T(8,128)(2,1)S(1)}, u32[]{:S(2)}, u32[]{:S(2)}) collective-permute-start(bf16[32,1536]{1,0:T(8,128)(2,1)S(1)} %get-tuple-element.34), channel_id=1, source_target_pairs={{0,8},{4,12},{8,0},{12,4},{16,24},{20,28},{24,16},{28,20},{1,9},{5... | collective-permute-start | bytes 294920 | tf_op jit(solution)/shard_map/ppermute | solution.py:25
  20.2 9.0 %collective-permute-start.11 = (bf16[32,1536]{1,0:T(8,128)(2,1)S(1)}, bf16[32,1536]{1,0:T(8,128)(2,1)S(1)}, u32[]{:S(2)}, u32[]{:S(2)}) collective-permute-start(bf16[32,1536]{1,0:T(8,128)(2,1)S(1)} %get-tuple-element.35), channel_id=1, source_target_pairs={{0,28},{4,24},{8,20},{12,16},{16,12},{20,8},{24,4},{28,0},{1,29},{... | collective-permute-start | bytes 294920 | tf_op jit(solution)/shard_map/ppermute | solution.py:25
  24.0 7.8 %collective-permute-start.4 = (bf16[32,896]{1,0:T(8,128)(2,1)S(1)}, bf16[32,896]{1,0:T(8,128)(2,1)S(1)}, u32[]{:S(2)}, u32[]{:S(2)}) collective-permute-start(bf16[32,896]{1,0:T(8,128)(2,1)S(1)} %get-tuple-element.28), channel_id=1, source_target_pairs={{0,16},{4,20},{8,24},{12,28},{16,0},{20,4},{24,8},{28,12},{1,17},{... | collective-permute-start | bytes 172040 | tf_op jit(solution)/shard_map/ppermute | solution.py:25
  24.9 6.8 %collective-permute-start.7 = (bf16[32,896]{1,0:T(8,128)(2,1)S(1)}, bf16[32,896]{1,0:T(8,128)(2,1)S(1)}, u32[]{:S(2)}, u32[]{:S(2)}) collective-permute-start(bf16[32,896]{1,0:T(8,128)(2,1)S(1)} %get-tuple-element.31), channel_id=1, source_target_pairs={{0,24},{4,28},{8,16},{12,20},{16,8},{20,12},{24,0},{28,4},{1,25},{... | collective-permute-start | bytes 172040 | tf_op jit(solution)/shard_map/ppermute | solution.py:25
